TPU v7x, 32 devices: a whole 2x2x4 slice. The times are simulated.
32 devices in a mesh: band: 4 (over x, core), gx: 4 (over z), gy: 2 (over y).
Axes of the slice: x: 2, y: 2, z: 4, core: 2. Of those that a mesh axis runs over, the one named last changes fastest.
Arguments:
- start_bands: float32 [64, 24, 16, 128], P('band', 'gx', 'gy'), may hold values from -40 to 40
- potential: float32 [24, 16, 128], P('gx', 'gy'), may hold values from 0 to 2
Outputs:
- new_bands: float32 [64, 24, 16, 128], P('band', 'gx', 'gy')
All inputs are finite; a program needn't handle non-finite values.
Results may differ from a plain program's by a relative error of at most 0.00025.
Values sent between devices are 32-bit elements; how exact they have to be, the bound alone decides.
No kernel may reach another device: no remote copies, remote signals or barrier semaphores. Data moves between devices by JAX's collectives and lax.ppermute only.
A program may use at most 64 MiB of HBM per device.

v0:
```python
import jax
import jax.numpy as jnp
from jax import lax
from jax.sharding import PartitionSpec as P

DEGREE = 4


COEFFS = (
    -5369.0 / 1800.0,
    12.0 / 7.0,
    -15.0 / 56.0,
    10.0 / 189.0,
    -1.0 / 112.0,
    2.0 / 1925.0,
    -1.0 / 16632.0,
)
LOWER_END = -0.5
CUT_LOW = 3.0
CUT_HIGH = 12.7


def padded_2(block, sides, width):
    for axis, dim in sides:
        count = lax.axis_size(axis)
        forward = [(i, i + 1) for i in range(count - 1)]
        forward.append((count - 1, 0))
        backward = [(target, source) for source, target in forward]
        low = lax.ppermute(
            lax.slice_in_dim(block, block.shape[dim] - width, None, axis=dim), axis, forward
        )
        high = lax.ppermute(lax.slice_in_dim(block, 0, width, axis=dim), axis, backward)
        block = jnp.concatenate([low, block, high], axis=dim)
    return block


def filter_weights(degree):
    half_width = (CUT_HIGH - CUT_LOW) / 2.0
    middle = (CUT_HIGH + CUT_LOW) / 2.0
    sigma = half_width / (LOWER_END - middle)
    tau = 2.0 / sigma
    first = sigma / half_width
    others = []
    for index in range(degree - 1):
        sigma_new = 1.0 / (tau - sigma)
        others.append((2.0 * sigma_new / half_width, sigma * sigma_new))
        sigma = sigma_new
    return (middle, first, others)


def hamiltonian(field, potential):
    reach = len(COEFFS) - 1
    width_x = field.shape[1]
    width_y = field.shape[2]
    padded = padded_2(field, (("gx", 1), ("gy", 2)), reach)
    laplace = 3.0 * COEFFS[0] * field
    for offset in range(1, reach + 1):
        ahead_x = padded[:, reach + offset : reach + offset + width_x, reach : reach + width_y]
        behind_x = padded[:, reach - offset : reach - offset + width_x, reach : reach + width_y]
        ahead_y = padded[:, reach : reach + width_x, reach + offset : reach + offset + width_y]
        behind_y = padded[:, reach : reach + width_x, reach - offset : reach - offset + width_y]
        neighbours = ahead_x + behind_x
        neighbours = neighbours + ahead_y + behind_y
        neighbours = neighbours + jnp.roll(field, -offset, 3) + jnp.roll(field, offset, 3)
        laplace = laplace + COEFFS[offset] * neighbours
    return -0.5 * laplace + potential * field


def chebyshev(field, potential):
    middle, first, others = filter_weights(DEGREE)
    current = (hamiltonian(field, potential) - middle * field) * first
    previous = field
    for scale_now, scale_back in others:
        following = (
            hamiltonian(current, potential) - middle * current
        ) * scale_now - scale_back * previous
        previous = current
        current = following
    return current


def invert_factor(margin, identity):
    lower_factor = jnp.linalg.cholesky(margin)
    return jax.scipy.linalg.solve_triangular(lower_factor, identity, lower=True)


def on_device(start_bands, potential):
    filtered = chebyshev(start_bands, potential)
    own_bands = filtered.shape[0]
    flattened = filtered.reshape(own_bands, -1)
    total_cells = flattened.shape[1] * lax.axis_size("gx") * lax.axis_size("gy")
    all_bands = own_bands * lax.axis_size("band")
    identity = jnp.eye(all_bands, dtype=jnp.float32)
    products = jnp.dot(
        flattened,
        lax.all_gather(flattened, "band", axis=0, tiled=True).T,
        precision=lax.Precision.HIGHEST,
        preferred_element_type=jnp.float32,
    )
    first_row = lax.axis_index("band") * own_bands
    summed = lax.psum(products, ("gx", "gy"))
    margin = lax.all_gather(summed, "band", axis=0, tiled=True) * (1.0 / total_cells)
    inverse = invert_factor(margin, identity)
    own_rows = lax.dynamic_slice_in_dim(inverse, first_row, own_bands, 0)
    rotated = jnp.dot(
        own_rows,
        lax.all_gather(flattened, "band", axis=0, tiled=True),
        precision=lax.Precision.HIGHEST,
        preferred_element_type=jnp.float32,
    )
    return rotated.reshape(filtered.shape)


def solution(mesh):
    in_specs = (P("band", "gx", "gy", None), P("gx", "gy", None))
    out_specs = P("band", "gx", "gy", None)
    return jax.shard_map(
        on_device, mesh=mesh, in_specs=in_specs, out_specs=out_specs, check_vma=False
    )
```

profile of v0, /device:TPU:0, one launch (start us, length us, event | category | flops | bytes accessed | tf_op | source)
XLA Modules:
  0.0 329.6 jit_solution(11481466139396830053)
XLA Ops:
  6.5 1.1 copy.40
  7.7 3.1 collective-permute-start.1
  10.7 2.1 collective-permute-start
  14.5 8.2 %collective-permute-done.1 = f32[16,6,8,128]{3,0,2,1:T(8,128)S(1)} collective-permute-done((f32[16,6,8,128]{3,0,2,1:T(8,128)S(1)}, f32[16,6,8,128]{3,0,2,1:T(8,128)S(1)}, u32[]{:S(2)}, u32[]{:S(2)}) %collective-permute-start.1) | collective-permute-done | bytes 393248 | tf_op jit(solution)/shard_map/ppermute | solution.py:29
  23.0 6.7 %collective-permute-done = f32[16,6,8,128]{3,0,2,1:T(8,128)S(1)} collective-permute-done((f32[16,6,8,128]{3,0,2,1:T(8,128)S(1)}, f32[16,6,8,128]{3,0,2,1:T(8,128)S(1)}, u32[]{:S(2)}, u32[]{:S(2)}) %collective-permute-start) | collective-permute-done | bytes 393248 | tf_op jit(solution)/shard_map/ppermute | solution.py:32
  29.8 0.2 fusion.210
  30.0 1.6 collective-permute-start.2
  31.6 0.5 collective-permute-start.3
  32.7 20.0 %collective-permute-done.2 = f32[16,18,6,128]{3,0,2,1:T(8,128)S(1)} collective-permute-done((f32[16,18,6,128]{3,0,2,1:T(8,128)S(1)}, f32[16,18,6,128]{3,0,2,1:T(8,128)S(1)}, u32[]{:S(2)}, u32[]{:S(2)}) %collective-permute-start.2) | collective-permute-done | bytes 884768 | tf_op jit(solution)/shard_map/ppermute | solution.py:32
  52.7 17.3 %collective-permute-done.3 = f32[16,18,6,128]{3,0,2,1:T(8,128)S(1)} collective-permute-done((f32[16,18,6,128]{3,0,2,1:T(8,128)S(1)}, f32[16,18,6,128]{3,0,2,1:T(8,128)S(1)}, u32[]{:S(2)}, u32[]{:S(2)}) %collective-permute-start.3) | collective-permute-done | bytes 884768 | tf_op jit(solution)/shard_map/ppermute | solution.py:29
  70.0 2.8 broadcast_multiply_fusion
  72.8 1.7 collective-permute-start.4
  74.6 0.3 collective-permute-start.5
  75.1 0.2 fusion.236
  75.3 0.2 fusion.237
  75.5 0.2 fusion.238
  75.7 0.2 fusion.239
  75.9 0.2 fusion.240
  76.0 0.2 fusion.241
  76.2 0.2 fusion.242
  76.4 15.1 %collective-permute-done.4 = f32[16,6,8,128]{3,0,2,1:T(8,128)S(1)} collective-permute-done((f32[16,6,8,128]{3,0,2,1:T(8,128)S(1)}, f32[16,6,8,128]{3,0,2,1:T(8,128)S(1)}, u32[]{:S(2)}, u32[]{:S(2)}) %collective-permute-start.4) | collective-permute-done | bytes 393248 | tf_op jit(solution)/shard_map/ppermute | solution.py:32
  91.6 0.2 fusion.209
  91.9 1.6 collective-permute-start.6
  93.5 0.5 collective-permute-start.7
  94.1 0.2 fusion.244
  94.7 19.8 %collective-permute-done.6 = f32[16,18,6,128]{3,0,2,1:T(8,128)S(1)} collective-permute-done((f32[16,18,6,128]{3,0,2,1:T(8,128)S(1)}, f32[16,18,6,128]{3,0,2,1:T(8,128)S(1)}, u32[]{:S(2)}, u32[]{:S(2)}) %collective-permute-start.6) | collective-permute-done | bytes 884768 | tf_op jit(solution)/shard_map/ppermute | solution.py:32
  114.5 14.3 %collective-permute-done.7 = f32[16,18,6,128]{3,0,2,1:T(8,128)S(1)} collective-permute-done((f32[16,18,6,128]{3,0,2,1:T(8,128)S(1)}, f32[16,18,6,128]{3,0,2,1:T(8,128)S(1)}, u32[]{:S(2)}, u32[]{:S(2)}) %collective-permute-start.7) | collective-permute-done | bytes 884768 | tf_op jit(solution)/shard_map/ppermute | solution.py:29
  128.8 0.5 pad_maximum_fusion
  129.3 2.8 fusion.100
  132.2 5.6 %collective-permute-start.8 = (f32[16,6,8,128]{3,0,2,1:T(8,128)S(1)}, f32[16,6,8,128]{3,0,2,1:T(8,128)S(1)}, u32[]{:S(2)}, u32[]{:S(2)}) collective-permute-start(f32[16,6,8,128]{3,0,2,1:T(8,128)S(1)} %fusion.100), channel_id=1, source_target_pairs={{2,0},{4,2},{6,4},{0,6},{3,1},{5,3},{7,5},{1,7},{10,8},{12,10},{14... | collective-permute-start | bytes 1179656 | tf_op jit(solution)/shard_map/ppermute | solution.py:32
  138.5 0.2 fusion.227
  139.3 8.1 %collective-permute-done.8 = f32[16,6,8,128]{3,0,2,1:T(8,128)S(1)} collective-permute-done((f32[16,6,8,128]{3,0,2,1:T(8,128)S(1)}, f32[16,6,8,128]{3,0,2,1:T(8,128)S(1)}, u32[]{:S(2)}, u32[]{:S(2)}) %collective-permute-start.8) | collective-permute-done | bytes 393248 | tf_op jit(solution)/shard_map/ppermute | solution.py:32
  147.4 7.6 %collective-permute-done.9 = f32[16,6,8,128]{3,0,2,1:T(8,128)S(1)} collective-permute-done((f32[16,6,8,128]{3,0,2,1:T(8,128)S(1)}, f32[16,6,8,128]{3,0,2,1:T(8,128)S(1)}, u32[]{:S(2)}, u32[]{:S(2)}) %collective-permute-start.9) | collective-permute-done | bytes 393248 | tf_op jit(solution)/shard_map/ppermute | solution.py:29
  155.1 0.2 fusion.208
  155.3 1.6 collective-permute-start.10
  156.9 0.5 collective-permute-start.11
  157.9 0.2 fusion.234
  158.1 19.8 %collective-permute-done.10 = f32[16,18,6,128]{3,0,2,1:T(8,128)S(1)} collective-permute-done((f32[16,18,6,128]{3,0,2,1:T(8,128)S(1)}, f32[16,18,6,128]{3,0,2,1:T(8,128)S(1)}, u32[]{:S(2)}, u32[]{:S(2)}) %collective-permute-start.10) | collective-permute-done | bytes 884768 | tf_op jit(solution)/shard_map/ppermute | solution.py:32
  177.9 16.2 %collective-permute-done.11 = f32[16,18,6,128]{3,0,2,1:T(8,128)S(1)} collective-permute-done((f32[16,18,6,128]{3,0,2,1:T(8,128)S(1)}, f32[16,18,6,128]{3,0,2,1:T(8,128)S(1)}, u32[]{:S(2)}, u32[]{:S(2)}) %collective-permute-start.11) | collective-permute-done | bytes 884768 | tf_op jit(solution)/shard_map/ppermute | solution.py:29
  194.1 0.5 pad_maximum_fusion.1
  194.6 2.5 fusion.57
  197.2 2.0 collective-permute-start.12
  200.4 0.2 fusion.217
  200.8 8.0 %collective-permute-done.12 = f32[16,6,8,128]{3,0,2,1:T(8,128)S(1)} collective-permute-done((f32[16,6,8,128]{3,0,2,1:T(8,128)S(1)}, f32[16,6,8,128]{3,0,2,1:T(8,128)S(1)}, u32[]{:S(2)}, u32[]{:S(2)}) %collective-permute-start.12) | collective-permute-done | bytes 393248 | tf_op jit(solution)/shard_map/ppermute | solution.py:32
  208.7 5.7 %collective-permute-done.13 = f32[16,6,8,128]{3,0,2,1:T(8,128)S(1)} collective-permute-done((f32[16,6,8,128]{3,0,2,1:T(8,128)S(1)}, f32[16,6,8,128]{3,0,2,1:T(8,128)S(1)}, u32[]{:S(2)}, u32[]{:S(2)}) %collective-permute-start.13) | collective-permute-done | bytes 393248 | tf_op jit(solution)/shard_map/ppermute | solution.py:29
  214.6 0.2 fusion.207
  214.8 1.6 collective-permute-start.14
  216.4 0.5 collective-permute-start.15
  217.6 19.8 %collective-permute-done.14 = f32[16,18,6,128]{3,0,2,1:T(8,128)S(1)} collective-permute-done((f32[16,18,6,128]{3,0,2,1:T(8,128)S(1)}, f32[16,18,6,128]{3,0,2,1:T(8,128)S(1)}, u32[]{:S(2)}, u32[]{:S(2)}) %collective-permute-start.14) | collective-permute-done | bytes 884768 | tf_op jit(solution)/shard_map/ppermute | solution.py:32
  237.4 14.5 %collective-permute-done.15 = f32[16,18,6,128]{3,0,2,1:T(8,128)S(1)} collective-permute-done((f32[16,18,6,128]{3,0,2,1:T(8,128)S(1)}, f32[16,18,6,128]{3,0,2,1:T(8,128)S(1)}, u32[]{:S(2)}, u32[]{:S(2)}) %collective-permute-start.15) | collective-permute-done | bytes 884768 | tf_op jit(solution)/shard_map/ppermute | solution.py:29
  252.0 0.5 pad_maximum_fusion.2
  252.5 2.5 fusion.14
  255.2 0.9 copy.86
  256.1 22.8 %all-gather.2.cloned.1.call-done = f32[64,6144]{1,0:T(8,128)} async-done(((f32[16,6144]{1,0:T(8,128)}), f32[64,6144]{1,0:T(8,128)}) %all-gather.2.cloned.1.call-update) | async-done | bytes 1572880 | tf_op jit(solution)/shard_map/all_gather | solution.py:96
  278.9 2.8 fusion.205
  281.8 21.6 %psum.7 = f32[16,64]{1,0:T(8,128)S(1)} all-reduce(f32[16,64]{1,0:T(8,128)S(1)} %fusion.205), channel_id=1, replica_groups=mesh['band'=4,'gx'=4,'gy'=2] {'gx','gy'}, use_global_device_ids=true, to_apply=%region_0.1 | all-reduce | flops 1024 | bytes 8192 | tf_op jit(solution)/shard_map/psum | solution.py:101
  303.4 5.2 %all_gather.8 = f32[64,64]{1,0:T(8,128)S(1)} all-gather(f32[16,64]{1,0:T(8,128)S(1)} %psum.7), channel_id=1, replica_groups=mesh['band'=4,'gx'=4,'gy'=2] {'band'}, dimensions={0}, use_global_device_ids=true | all-gather | bytes 20480 | tf_op jit(solution)/shard_map/all_gather | solution.py:102
  308.8 5.8 %cholesky.17 = f32[64,64]{1,0:T(8,128)S(1)} custom-call(f32[64,64]{1,0:T(8,128)S(1)} %fusion.202), custom_call_target="Cholesky" | custom-call | tf_op jit(solution)/shard_map/jit(cholesky)/cholesky | solution.py:83
  314.6 0.6 compare_reduce_fusion
  315.3 0.7 fusion.199
  315.9 4.9 %custom-call.7 = f32[1,64,64]{1,2,0:T(8,128)S(1)} custom-call(f32[1,64,64]{2,1,0:T(8,128)S(1)} %fusion.199), custom_call_target="InvertDiagBlocksLowerTriangular" | custom-call | tf_op jit(solution)/shard_map/jit(_solve_triangular)/triangular_solve | solution.py:84
  320.8 0.2 fusion.200
  321.1 0.9 convolution_bitcast_fusion
  322.0 0.8 copy.77
  (61 shorter events, 7.9 us)
Async XLA Ops:
  6.5 272.4 %all-gather.2.cloned.1.call-start = ((), (), s32[]{:S(2)}) async-start(), calls=%async_computation | async-start | bytes 1966080 | tf_op jit(solution)/shard_map/all_gather | solution.py:96
  7.7 15.1 %collective-permute-start.1 = (f32[16,6,8,128]{3,0,2,1:T(8,128)S(1)}, f32[16,6,8,128]{3,0,2,1:T(8,128)S(1)}, u32[]{:S(2)}, u32[]{:S(2)}) collective-permute-start(f32[16,6,8,128]{3,0,2,1:T(8,128)S(1)} %copy.40), channel_id=1, source_target_pairs={{0,2},{2,4},{4,6},{6,0},{1,3},{3,5},{5,7},{7,1},{8,10},{10,12},{12... | collective-permute-start | bytes 1179656 | tf_op jit(solution)/shard_map/ppermute | solution.py:29
  10.7 19.0 %collective-permute-start = (f32[16,6,8,128]{3,0,2,1:T(8,128)S(1)}, f32[16,6,8,128]{3,0,2,1:T(8,128)S(1)}, u32[]{:S(2)}, u32[]{:S(2)}) collective-permute-start(f32[16,6,8,128]{3,0,2,1:T(8,128)S(1)} %copy.40), channel_id=1, source_target_pairs={{2,0},{4,2},{6,4},{0,6},{3,1},{5,3},{7,5},{1,7},{10,8},{12,10},{14... | collective-permute-start | bytes 1179656 | tf_op jit(solution)/shard_map/ppermute | solution.py:32
  14.1 8.7 %copy-start.1 = (f32[16,6,8,128]{3,2,1,0:T(8,128)S(1)}, f32[16,6,8,128]{3,2,1,0:T(8,128)}, u32[]{:S(2)}) copy-start(f32[16,6,8,128]{3,2,1,0:T(8,128)} %param.2) | copy-start | bytes 1179652
  29.8 2.3 copy-start.2
  30.0 22.6 %collective-permute-start.2 = (f32[16,18,6,128]{3,0,2,1:T(8,128)S(1)}, f32[16,18,6,128]{3,0,2,1:T(8,128)S(1)}, u32[]{:S(2)}, u32[]{:S(2)}) collective-permute-start(f32[16,18,6,128]{3,0,2,1:T(8,128)S(1)} %get-tuple-element.19), channel_id=1, source_target_pairs={{1,0},{0,1},{3,2},{2,3},{5,4},{4,5},{7,6},{6,7},{9,8},{8,9},{11,10... | collective-permute-start | bytes 2654216 | tf_op jit(solution)/shard_map/ppermute | solution.py:32
  31.6 38.4 %collective-permute-start.3 = (f32[16,18,6,128]{3,0,2,1:T(8,128)S(1)}, f32[16,18,6,128]{3,0,2,1:T(8,128)S(1)}, u32[]{:S(2)}, u32[]{:S(2)}) collective-permute-start(f32[16,18,6,128]{3,0,2,1:T(8,128)S(1)} %get-tuple-element.20), channel_id=1, source_target_pairs={{0,1},{1,0},{2,3},{3,2},{4,5},{5,4},{6,7},{7,6},{8,9},{9,8},{10,11... | collective-permute-start | bytes 2654216 | tf_op jit(solution)/shard_map/ppermute | solution.py:29
  72.8 18.7 %collective-permute-start.4 = (f32[16,6,8,128]{3,0,2,1:T(8,128)S(1)}, f32[16,6,8,128]{3,0,2,1:T(8,128)S(1)}, u32[]{:S(2)}, u32[]{:S(2)}) collective-permute-start(f32[16,6,8,128]{3,0,2,1:T(8,128)S(1)} %get-tuple-element.5), channel_id=1, source_target_pairs={{2,0},{4,2},{6,4},{0,6},{3,1},{5,3},{7,5},{1,7},{10,8},{12,10},{14... | collective-permute-start | bytes 1179656 | tf_op jit(solution)/shard_map/ppermute | solution.py:32
  74.6 16.9 %collective-permute-start.5 = (f32[16,6,8,128]{3,0,2,1:T(8,128)S(1)}, f32[16,6,8,128]{3,0,2,1:T(8,128)S(1)}, u32[]{:S(2)}, u32[]{:S(2)}) collective-permute-start(f32[16,6,8,128]{3,0,2,1:T(8,128)S(1)} %get-tuple-element.5), channel_id=1, source_target_pairs={{0,2},{2,4},{4,6},{6,0},{1,3},{3,5},{5,7},{7,1},{8,10},{10,12},{12... | collective-permute-start | bytes 1179656 | tf_op jit(solution)/shard_map/ppermute | solution.py:29
  91.9 22.7 %collective-permute-start.6 = (f32[16,18,6,128]{3,0,2,1:T(8,128)S(1)}, f32[16,18,6,128]{3,0,2,1:T(8,128)S(1)}, u32[]{:S(2)}, u32[]{:S(2)}) collective-permute-start(f32[16,18,6,128]{3,0,2,1:T(8,128)S(1)} %get-tuple-element.17), channel_id=1, source_target_pairs={{1,0},{0,1},{3,2},{2,3},{5,4},{4,5},{7,6},{6,7},{9,8},{8,9},{11,10... | collective-permute-start | bytes 2654216 | tf_op jit(solution)/shard_map/ppermute | solution.py:32
  93.5 35.4 %collective-permute-start.7 = (f32[16,18,6,128]{3,0,2,1:T(8,128)S(1)}, f32[16,18,6,128]{3,0,2,1:T(8,128)S(1)}, u32[]{:S(2)}, u32[]{:S(2)}) collective-permute-start(f32[16,18,6,128]{3,0,2,1:T(8,128)S(1)} %get-tuple-element.18), channel_id=1, source_target_pairs={{0,1},{1,0},{2,3},{3,2},{4,5},{5,4},{6,7},{7,6},{8,9},{9,8},{10,11... | collective-permute-start | bytes 2654216 | tf_op jit(solution)/shard_map/ppermute | solution.py:29
  132.2 15.2 %collective-permute-start.8 = (f32[16,6,8,128]{3,0,2,1:T(8,128)S(1)}, f32[16,6,8,128]{3,0,2,1:T(8,128)S(1)}, u32[]{:S(2)}, u32[]{:S(2)}) collective-permute-start(f32[16,6,8,128]{3,0,2,1:T(8,128)S(1)} %fusion.100), channel_id=1, source_target_pairs={{2,0},{4,2},{6,4},{0,6},{3,1},{5,3},{7,5},{1,7},{10,8},{12,10},{14... | collective-permute-start | bytes 1179656 | tf_op jit(solution)/shard_map/ppermute | solution.py:32
  137.8 17.2 %collective-permute-start.9 = (f32[16,6,8,128]{3,0,2,1:T(8,128)S(1)}, f32[16,6,8,128]{3,0,2,1:T(8,128)S(1)}, u32[]{:S(2)}, u32[]{:S(2)}) collective-permute-start(f32[16,6,8,128]{3,0,2,1:T(8,128)S(1)} %fusion.100), channel_id=1, source_target_pairs={{0,2},{2,4},{4,6},{6,0},{1,3},{3,5},{5,7},{7,1},{8,10},{10,12},{12... | collective-permute-start | bytes 1179656 | tf_op jit(solution)/shard_map/ppermute | solution.py:29
  155.3 22.6 %collective-permute-start.10 = (f32[16,18,6,128]{3,0,2,1:T(8,128)S(1)}, f32[16,18,6,128]{3,0,2,1:T(8,128)S(1)}, u32[]{:S(2)}, u32[]{:S(2)}) collective-permute-start(f32[16,18,6,128]{3,0,2,1:T(8,128)S(1)} %get-tuple-element.13), channel_id=1, source_target_pairs={{1,0},{0,1},{3,2},{2,3},{5,4},{4,5},{7,6},{6,7},{9,8},{8,9},{11,10... | collective-permute-start | bytes 2654216 | tf_op jit(solution)/shard_map/ppermute | solution.py:32
  156.9 37.2 %collective-permute-start.11 = (f32[16,18,6,128]{3,0,2,1:T(8,128)S(1)}, f32[16,18,6,128]{3,0,2,1:T(8,128)S(1)}, u32[]{:S(2)}, u32[]{:S(2)}) collective-permute-start(f32[16,18,6,128]{3,0,2,1:T(8,128)S(1)} %get-tuple-element.14), channel_id=1, source_target_pairs={{0,1},{1,0},{2,3},{3,2},{4,5},{5,4},{6,7},{7,6},{8,9},{9,8},{10,11... | collective-permute-start | bytes 2654216 | tf_op jit(solution)/shard_map/ppermute | solution.py:29
  197.2 11.5 %collective-permute-start.12 = (f32[16,6,8,128]{3,0,2,1:T(8,128)S(1)}, f32[16,6,8,128]{3,0,2,1:T(8,128)S(1)}, u32[]{:S(2)}, u32[]{:S(2)}) collective-permute-start(f32[16,6,8,128]{3,0,2,1:T(8,128)S(1)} %fusion.57), channel_id=1, source_target_pairs={{2,0},{4,2},{6,4},{0,6},{3,1},{5,3},{7,5},{1,7},{10,8},{12,10},{14... | collective-permute-start | bytes 1179656 | tf_op jit(solution)/shard_map/ppermute | solution.py:32
  199.2 15.3 %collective-permute-start.13 = (f32[16,6,8,128]{3,0,2,1:T(8,128)S(1)}, f32[16,6,8,128]{3,0,2,1:T(8,128)S(1)}, u32[]{:S(2)}, u32[]{:S(2)}) collective-permute-start(f32[16,6,8,128]{3,0,2,1:T(8,128)S(1)} %fusion.57), channel_id=1, source_target_pairs={{0,2},{2,4},{4,6},{6,0},{1,3},{3,5},{5,7},{7,1},{8,10},{10,12},{12... | collective-permute-start | bytes 1179656 | tf_op jit(solution)/shard_map/ppermute | solution.py:29
  214.8 22.6 %collective-permute-start.14 = (f32[16,18,6,128]{3,0,2,1:T(8,128)S(1)}, f32[16,18,6,128]{3,0,2,1:T(8,128)S(1)}, u32[]{:S(2)}, u32[]{:S(2)}) collective-permute-start(f32[16,18,6,128]{3,0,2,1:T(8,128)S(1)} %get-tuple-element.9), channel_id=1, source_target_pairs={{1,0},{0,1},{3,2},{2,3},{5,4},{4,5},{7,6},{6,7},{9,8},{8,9},{11,10... | collective-permute-start | bytes 2654216 | tf_op jit(solution)/shard_map/ppermute | solution.py:32
  216.4 35.6 %collective-permute-start.15 = (f32[16,18,6,128]{3,0,2,1:T(8,128)S(1)}, f32[16,18,6,128]{3,0,2,1:T(8,128)S(1)}, u32[]{:S(2)}, u32[]{:S(2)}) collective-permute-start(f32[16,18,6,128]{3,0,2,1:T(8,128)S(1)} %get-tuple-element.10), channel_id=1, source_target_pairs={{0,1},{1,0},{2,3},{3,2},{4,5},{5,4},{6,7},{7,6},{8,9},{9,8},{10,11... | collective-permute-start | bytes 2654216 | tf_op jit(solution)/shard_map/ppermute | solution.py:29
  278.9 42.2 %copy-start = (f32[64,6144]{1,0:T(8,128)S(1)}, f32[64,6144]{1,0:T(8,128)}, u32[]{:S(2)}) copy-start(f32[64,6144]{1,0:T(8,128)} %all-gather.2.cloned.1.call-done) | copy-start | bytes 4718596
Sparse Core Ops, SparseCore 0:
  256.2 22.6 all-gather.1
where the time goes:
time: 330 us
  waiting for transfers between devices  224 us (68%)
  blocking collectives  26.8 us (8%)
  other arithmetic  24.7 us (7%)
  starting transfers between devices  23.3 us (7%)
  between operations  13.7 us (4%)
  local copies, waits for them, and re-layouts  13.1 us (4%)
  matrix products  3.93 us (1%)
    ppermute x8, waiting for transfers between devices, padded_2(): lax.ppermute(lax.slice_in_dim(block, 0, width, axis=dim), axis, backward)  117 us
    ppermute x8, waiting for transfers between devices, padded_2(): lax.ppermute(lax.slice_in_dim(block, block.shape[dim] - width, None, axis...  83.9 us
    all_gather x1, waiting for transfers between devices, on_device(): lax.all_gather(flattened, 'band', axis=0, tiled=True)  22.8 us
    psum x1, blocking collectives, on_device(): summed = lax.psum(products, ('gx', 'gy'))  21.6 us
    ppermute x8, starting transfers between devices, padded_2(): lax.ppermute(lax.slice_in_dim(block, 0, width, axis=dim), axis, backward)  17.7 us
    sub x3, other arithmetic, chebyshev(): (hamiltonian(current, potential) - middle * current) * scale_now  7.92 us
    slice x36, local copies, waits for them, and re-layouts, hamiltonian(): jnp.roll(field, offset, 3)  6.69 us
  transfers between devices with their start and end apart: 17, of which 16 were waited for; matrix products, arithmetic and copies ran while one was open for 3% of the time, Pallas kernels for 0%

commit v1 on v0

--- a/solution.py
+++ b/solution.py
@@ -1,6 +1,12 @@
+import functools
+
 import jax
 import jax.numpy as jnp
+import ml_dtypes
+import numpy as np
 from jax import lax
+from jax.experimental import pallas as pl
+from jax.experimental.pallas import tpu as pltpu
 from jax.sharding import PartitionSpec as P
 
 DEGREE = 4
@@ -15,9 +21,25 @@
     2.0 / 1925.0,
     -1.0 / 16632.0,
 )
+REACH = len(COEFFS) - 1
 LOWER_END = -0.5
 CUT_LOW = 3.0
 CUT_HIGH = 12.7
+TILE = 8
+
+
+def filter_weights(degree):
+    half_width = (CUT_HIGH - CUT_LOW) / 2.0
+    middle = (CUT_HIGH + CUT_LOW) / 2.0
+    sigma = half_width / (LOWER_END - middle)
+    tau = 2.0 / sigma
+    first = sigma / half_width
+    others = []
+    for index in range(degree - 1):
+        sigma_new = 1.0 / (tau - sigma)
+        others.append((2.0 * sigma_new / half_width, sigma * sigma_new))
+        sigma = sigma_new
+    return (middle, first, others)
 
 
 def padded_2(block, sides, width):
@@ -34,31 +56,16 @@
     return block
 
 
-def filter_weights(degree):
-    half_width = (CUT_HIGH - CUT_LOW) / 2.0
-    middle = (CUT_HIGH + CUT_LOW) / 2.0
-    sigma = half_width / (LOWER_END - middle)
-    tau = 2.0 / sigma
-    first = sigma / half_width
-    others = []
-    for index in range(degree - 1):
-        sigma_new = 1.0 / (tau - sigma)
-        others.append((2.0 * sigma_new / half_width, sigma * sigma_new))
-        sigma = sigma_new
-    return (middle, first, others)
-
-
 def hamiltonian(field, potential):
-    reach = len(COEFFS) - 1
     width_x = field.shape[1]
     width_y = field.shape[2]
-    padded = padded_2(field, (("gx", 1), ("gy", 2)), reach)
+    padded = padded_2(field, (("gx", 1), ("gy", 2)), REACH)
     laplace = 3.0 * COEFFS[0] * field
-    for offset in range(1, reach + 1):
-        ahead_x = padded[:, reach + offset : reach + offset + width_x, reach : reach + width_y]
-        behind_x = padded[:, reach - offset : reach - offset + width_x, reach : reach + width_y]
-        ahead_y = padded[:, reach : reach + width_x, reach + offset : reach + offset + width_y]
-        behind_y = padded[:, reach : reach + width_x, reach - offset : reach - offset + width_y]
+    for offset in range(1, REACH + 1):
+        ahead_x = padded[:, REACH + offset : REACH + offset + width_x, REACH : REACH + width_y]
+        behind_x = padded[:, REACH - offset : REACH - offset + width_x, REACH : REACH + width_y]
+        ahead_y = padded[:, REACH : REACH + width_x, REACH + offset : REACH + offset + width_y]
+        behind_y = padded[:, REACH : REACH + width_x, REACH - offset : REACH - offset + width_y]
         neighbours = ahead_x + behind_x
         neighbours = neighbours + ahead_y + behind_y
         neighbours = neighbours + jnp.roll(field, -offset, 3) + jnp.roll(field, offset, 3)
@@ -84,7 +91,7 @@
     return jax.scipy.linalg.solve_triangular(lower_factor, identity, lower=True)
 
 
-def on_device(start_bands, potential):
+def on_device_halo(start_bands, potential):
     filtered = chebyshev(start_bands, potential)
     own_bands = filtered.shape[0]
     flattened = filtered.reshape(own_bands, -1)
@@ -111,6 +118,277 @@
     return rotated.reshape(filtered.shape)
 
 
+def split3(value):
+    high = value.astype(jnp.bfloat16)
+    rest = value - high.astype(jnp.float32)
+    mid = rest.astype(jnp.bfloat16)
+    low = (rest - mid.astype(jnp.float32)).astype(jnp.bfloat16)
+    return high, mid, low
+
+
+def z_weights(nz):
+    circulant = np.zeros((nz, nz), np.float32)
+    at = np.arange(nz)
+    for offset in range(1, REACH + 1):
+        circulant[at, (at + offset) % nz] += np.float32(-0.5 * COEFFS[offset])
+        circulant[at, (at - offset) % nz] += np.float32(-0.5 * COEFFS[offset])
+    high = circulant.astype(ml_dtypes.bfloat16)
+    rest = circulant - high.astype(np.float32)
+    mid = rest.astype(ml_dtypes.bfloat16)
+    low = (rest - mid.astype(np.float32)).astype(ml_dtypes.bfloat16)
+    first = np.block([[high, mid], [high, mid]])
+    second = np.concatenate([high, low], 0)
+    return first, second
+
+
+def filter_kernel(dims, core_ref, own_ref, other_ref, w1_ref, w2_ref, out_ref, pot, buf_a, buf_b, zbuf):
+    gx, gy, own, nx, ny, nz, pieces = dims
+    width = gx * nx
+    height = gy * ny
+    cells = nx * ny
+    half = cells // 2
+    rows = cells // pieces
+    middle, first, others = filter_weights(DEGREE)
+    shift = -middle - 1.5 * COEFFS[0]
+    pad = TILE
+
+    def place(buf, k, x, tile, value):
+        buf[k, x, pl.ds(pad + tile * TILE, TILE), :] = value
+        if tile == 0:
+            buf[k, x, pl.ds(pad + height, TILE), :] = value
+        if tile == height // TILE - 1:
+            buf[k, x, pl.ds(0, TILE), :] = value
+
+    core = core_ref[0]
+    for g in range(gx * gy):
+        at_x, at_y = (g // gy) * nx, (g % gy) * ny
+        for k in range(own):
+            for i in range(nx):
+                for t in range(ny // TILE):
+                    value = own_ref[g, pl.ds(k * cells + i * ny + t * TILE, TILE), :]
+                    place(buf_a, k, at_x + i, at_y // TILE + t, value)
+        mine = pl.ds(pl.multiple_of(core * half, TILE), half)
+        theirs = pl.ds(pl.multiple_of((1 - core) * half, TILE), half)
+        pot[g, mine, :] = own_ref[g, own * cells :, :] + shift
+        pot[g, theirs, :] = other_ref[g] + shift
+
+    buffers = (buf_a, buf_b)
+    steps = [(first, None)] + others
+    for step, (scale, back) in enumerate(steps):
+        src, dst = buffers[step % 2], buffers[(step + 1) % 2]
+        last = step == len(steps) - 1
+        field = src[:, :, pl.ds(pad, height), :].reshape(own * width * height, nz)
+        high, mid, low = split3(field)
+        part = jnp.dot(jnp.concatenate([high, mid], 1), w1_ref[...], preferred_element_type=jnp.float32)
+        rest = jnp.dot(jnp.concatenate([low, high], 1), w2_ref[...], preferred_element_type=jnp.float32)
+        zbuf[...] = (part[:, :nz] + part[:, nz:] + rest).reshape(own, width, height, nz)
+        for k in range(own):
+            for x in range(width):
+                for tile in range(height // TILE):
+                    g = (x // nx) * gy + tile * TILE // ny
+                    in_pencil = (x % nx) * ny + (tile * TILE) % ny
+                    at = pad + tile * TILE
+                    centre = src[k, x, pl.ds(at, TILE), :]
+                    total = zbuf[k, x, pl.ds(tile * TILE, TILE), :] + pot[g, pl.ds(in_pencil, TILE), :] * centre
+                    for j in range(1, REACH + 1):
+                        near = src[k, (x + j) % width, pl.ds(at, TILE), :] + src[k, (x - j) % width, pl.ds(at, TILE), :]
+                        near = near + src[k, x, pl.ds(at + j, TILE), :] + src[k, x, pl.ds(at - j, TILE), :]
+                        total = total + (-0.5 * COEFFS[j]) * near
+                    value = scale * total
+                    if back is not None:
+                        value = value - back * dst[k, x, pl.ds(at, TILE), :]
+                    if not last:
+                        place(dst, k, x, tile, value)
+                        continue
+                    for r in range(0, TILE, TILE // 2):
+                        piece, row = divmod(in_pencil + r, rows)
+                        to = piece_owner(piece, pieces) * gx * gy + g
+                        out_ref[to, pl.ds(k * rows + row, TILE // 2), :] = value[r : r + TILE // 2]
+
+
+def piece_owner(piece, pieces):
+    chips = pieces // 2
+    return (piece % chips) * 2 + piece // chips
+
+
+def apply_filter(core, own, other, dims):
+    gx, gy, bands, nx, ny, nz, pieces = dims
+    width, height = gx * nx, gy * ny
+    w1, w2 = z_weights(nz)
+    padded = (bands, width, height + 2 * TILE, nz)
+    vmem = pl.BlockSpec(memory_space=pltpu.VMEM)
+    return pl.pallas_call(
+        functools.partial(filter_kernel, dims),
+        out_shape=jax.ShapeDtypeStruct((pieces * gx * gy, bands * nx * ny // pieces, nz), jnp.float32),
+        in_specs=[pl.BlockSpec(memory_space=pltpu.SMEM)] + [vmem] * 4,
+        out_specs=vmem,
+        scratch_shapes=[
+            pltpu.VMEM((gx * gy, nx * ny, nz), jnp.float32),
+            pltpu.VMEM(padded, jnp.float32),
+            pltpu.VMEM(padded, jnp.float32),
+            pltpu.VMEM((bands, width, height, nz), jnp.float32),
+        ],
+        compiler_params=pltpu.CompilerParams(vmem_limit_bytes=40 * 1024 * 1024),
+        name="filter",
+    )(core, own, other, w1, w2)
+
+
+def margin_kernel(rows, bands, scale, x_ref, out_ref):
+    total = jnp.zeros((bands, bands), jnp.float32)
+    for r in range(rows):
+        block = x_ref[pl.ds(r, bands, stride=rows), :]
+        total = total + lax.dot_general(
+            block, block, (((1,), (1,)), ((), ())), precision=lax.Precision.HIGHEST, preferred_element_type=jnp.float32
+        )
+    total = total * scale
+    out_ref[:, pl.ds(0, bands)] = total[: bands // 2]
+    out_ref[:, pl.ds(bands, bands)] = total[bands // 2 :]
+
+
+def partial_margin(blocks, bands, scale):
+    rows = blocks.shape[0] // bands
+    return pl.pallas_call(
+        functools.partial(margin_kernel, rows, bands, scale),
+        out_shape=jax.ShapeDtypeStruct((bands // 2, 2 * bands), jnp.float32),
+        in_specs=[pl.BlockSpec(memory_space=pltpu.VMEM)],
+        out_specs=pl.BlockSpec(memory_space=pltpu.VMEM),
+        name="margin",
+    )(blocks)
+
+
+def sum_over(value, axes, masks, count):
+    total = value
+    for mask in masks:
+        total = total + lax.ppermute(value, axes, [(i, i ^ mask) for i in range(count)])
+    return total
+
+
+def inverse_kernel(bands, m_ref, out_ref):
+    folded = m_ref[...]
+    margin = jnp.concatenate([folded[:, :bands], folded[:, bands:]], 0)
+    row_at = lax.broadcasted_iota(jnp.int32, (bands, bands), 0)
+    col_at = lax.broadcasted_iota(jnp.int32, (bands, bands), 1)
+    both = jnp.concatenate([margin, jnp.where(row_at == col_at, 1.0, 0.0)], 1)
+    lines = lax.broadcasted_iota(jnp.int32, (bands, 1), 0)
+    pivots = jnp.ones((bands, 1), jnp.float32)
+    for j in range(bands):
+        row = both[j : j + 1, :]
+        column = both[:, j : j + 1]
+        pivot = row[:, j : j + 1]
+        pivots = jnp.where(lines == j, pivot, pivots)
+        factor = jnp.where(lines > j, column, 0.0)
+        both = both - factor * (row * (1.0 / pivot))
+    out_ref[...] = both[:, bands:] * lax.rsqrt(pivots)
+
+
+def inverse_factor(folded, bands):
+    return pl.pallas_call(
+        functools.partial(inverse_kernel, bands),
+        out_shape=jax.ShapeDtypeStruct((bands, bands), jnp.float32),
+        in_specs=[pl.BlockSpec(memory_space=pltpu.VMEM)],
+        out_specs=pl.BlockSpec(memory_space=pltpu.VMEM),
+        name="inverse",
+    )(folded)
+
+
+def rotate_kernel(dims, place_ref, inv_ref, *refs):
+    rows, bands, own, pieces = dims
+    parts, out_ref = refs[:-1], refs[-1]
+    first = pl.multiple_of(place_ref[0], TILE)
+    inverse = inv_ref[pl.ds(first, own), :]
+    for index, part in enumerate(parts):
+        at = place_ref[1 + index]
+        for r in range(rows):
+            block = part[pl.ds(r, bands, stride=rows), :]
+            value = jnp.dot(inverse, block, precision=lax.Precision.HIGHEST, preferred_element_type=jnp.float32)
+            out_ref[pl.ds(at + r, own, stride=rows * pieces), :] = value
+
+
+def rotate(place, inverse, parts, own):
+    bands = inverse.shape[0]
+    pieces = len(parts)
+    rows = parts[0].shape[0] // bands
+    nz = parts[0].shape[1]
+    vmem = pl.BlockSpec(memory_space=pltpu.VMEM)
+    return pl.pallas_call(
+        functools.partial(rotate_kernel, (rows, bands, own, pieces)),
+        out_shape=jax.ShapeDtypeStruct((own * rows * pieces, nz), jnp.float32),
+        in_specs=[pl.BlockSpec(memory_space=pltpu.SMEM)] + [vmem] * (1 + pieces),
+        out_specs=vmem,
+        compiler_params=pltpu.CompilerParams(vmem_limit_bytes=32 * 1024 * 1024),
+        name="rotate",
+    )(place, inverse, *parts)
+
+
+def on_device_fields(start_bands, potential):
+    own_bands, nx, ny, nz = start_bands.shape
+    gx, gy, pieces = lax.axis_size("gx"), lax.axis_size("gy"), lax.axis_size("band")
+    grid = gx * gy
+    own = own_bands // grid
+    cells = nx * ny
+    bands = own_bands * pieces
+    rows = cells // pieces
+    band = lax.axis_index("band")
+    core = band % 2
+    swap = [(i, i ^ 1) for i in range(pieces)]
+
+    fields = start_bands.reshape(grid, own * cells, nz)
+    flat_potential = potential.reshape(cells, nz)
+    half = cells // 2
+    own_half = lax.dynamic_slice_in_dim(flat_potential, core * half, half, 0)
+    packed = jnp.concatenate([fields, jnp.broadcast_to(own_half[None], (grid, half, nz))], 1)
+    packed = lax.all_to_all(packed, ("gx", "gy"), 0, 0)
+    other = lax.ppermute(packed[:, own * cells :, :], "band", swap)
+    dims = (gx, gy, own, nx, ny, nz, pieces)
+    filtered = apply_filter(core.reshape(1), packed, other, dims)
+    blocks = lax.all_to_all(filtered, ("band", "gx", "gy"), 0, 0).reshape(bands * rows, nz)
+
+    parts, offsets = [blocks], [band]
+    for mask in range(2, pieces, 2):
+        parts.append(lax.ppermute(blocks, "band", [(i, i ^ mask) for i in range(pieces)]))
+        offsets.append(band ^ mask)
+    for index in range(len(parts)):
+        parts.append(lax.ppermute(parts[index], "band", swap))
+        offsets.append(offsets[index] ^ 1)
+    chips = pieces // 2
+    offsets = [((at % 2) * chips + at // 2) * rows for at in offsets]
+
+    margin = partial_margin(blocks, bands, 1.0 / (cells * nz * grid))
+    margin = sum_over(margin, "band", [1], pieces)
+    masks = [chip * 2 * gy + y for chip in range(chips) for y in range(gy)][1:]
+    margin = sum_over(margin, ("band", "gy"), masks, pieces * gy)
+    margin = sum_over(margin, "gx", range(1, gx), gx)
+    inverse = inverse_factor(margin, bands)
+    place = jnp.stack([band * own_bands] + offsets).astype(jnp.int32)
+    rotated = rotate(place, inverse, parts, own_bands)
+    return rotated.reshape(start_bands.shape)
+
+
+def power_of_two(count):
+    return count & (count - 1) == 0
+
+
+def on_device(start_bands, potential):
+    own_bands, nx, ny, nz = start_bands.shape
+    gx, gy, pieces = lax.axis_size("gx"), lax.axis_size("gy"), lax.axis_size("band")
+    cells = nx * ny
+    whole_fields = (
+        own_bands % (gx * gy) == 0
+        and own_bands % TILE == 0
+        and all(power_of_two(count) for count in (gx, gy, pieces))
+        and pieces > 1
+        and ny % TILE == 0
+        and nz % 128 == 0
+        and cells % (2 * TILE) == 0
+        and cells % (pieces * TILE // 2) == 0
+        and (own_bands // (gx * gy)) * (cells // pieces) % TILE == 0
+        and gx * nx > 2 * REACH
+    )
+    if whole_fields:
+        return on_device_fields(start_bands, potential)
+    return on_device_halo(start_bands, potential)
+
+
 def solution(mesh):
     in_specs = (P("band", "gx", "gy", None), P("gx", "gy", None))
     out_specs = P("band", "gx", "gy", None)

time: 330 us -> 74.8 us (0.23)
  waiting for transfers between devices: 224 us -> 7.87 us
  other arithmetic: 24.7 us -> 2.36 us
  Pallas kernels: 0 us -> 15.8 us
  starting transfers between devices: 23.3 us -> 8.6 us
  between operations: 13.7 us -> 0.05 us
  local copies, waits for them, and re-layouts: 13.1 us -> 1.61 us
  blocking collectives: 26.8 us -> 38 us
  matrix products: 3.93 us -> 0 us
    ppermute x16 -> x11, waiting for transfers between devices: 201 us -> 7.87 us  [the longest x7 3.92 us: sum_over(): lax.ppermute(value, axes, [(i, i ^ mask) for i in range(count)])]
    all_to_all x0 -> x2, blocking collectives: none -> 38 us  [the longest x1 20.9 us: on_device_fields(): packed = lax.all_to_all(packed, ('gx', 'gy'), 0, 0)]
    all_gather x1 -> x0, waiting for transfers between devices: 22.8 us -> none  [on_device(): lax.all_gather(flattened, 'band', axis=0, tiled=True)]
    psum x1 -> x0, blocking collectives: 21.6 us -> none  [on_device(): summed = lax.psum(products, ('gx', 'gy'))]
    pallas_call x0 -> x4, Pallas kernels: none -> 15.8 us  [the longest x1 7 us: inverse_factor(): pl.pallas_call(functools.partial(inverse_kernel, bands), out_shape=jax.Sh...]
    ppermute x16 -> x11, starting transfers between devices: 23.3 us -> 8.6 us  [the longest x7 7.98 us: sum_over(): lax.ppermute(value, axes, [(i, i ^ mask) for i in range(count)])]
    another operation x5 -> x0, other arithmetic: 12.1 us -> none  [the longest x3 6.52 us: invert_factor(): lower_factor = jnp.linalg.cholesky(margin)]
    slice x52 -> x1, local copies, waits for them, and re-layouts: 9.73 us -> 0.01 us  [on_device_fields(): other = lax.ppermute(packed[:, own * cells:, :], 'band', swap)]
  transfers between devices with their start and end apart: 17 -> 11, of which waited for: 16 -> 6; matrix products, arithmetic and copies ran while one was open for 3% -> 2% of each run, Pallas kernels for 0% -> 13%
where the time goes in v1:
time: 74.8 us; the launch traced here: 74.3 us
  blocking collectives  38 us (51%)
  Pallas kernels  15.8 us (21%)
  starting transfers between devices  8.6 us (11%)
  waiting for transfers between devices  7.87 us (11%)
  other arithmetic  2.36 us (3%)
  local copies, waits for them, and re-layouts  1.61 us (2%)
    all_to_all x1, blocking collectives, on_device_fields(): packed = lax.all_to_all(packed, ('gx', 'gy'), 0, 0)  20.9 us
    all_to_all x1, blocking collectives, on_device_fields(): lax.all_to_all(filtered, ('band', 'gx', 'gy'), 0, 0)  17.1 us
    ppermute x7, starting transfers between devices, sum_over(): lax.ppermute(value, axes, [(i, i ^ mask) for i in range(count)])  7.98 us
    pallas_call x1, Pallas kernels, inverse_factor(): pl.pallas_call(functools.partial(inverse_kernel, bands), out_shape=jax.Sh...  7 us
    ppermute x7, waiting for transfers between devices, sum_over(): lax.ppermute(value, axes, [(i, i ^ mask) for i in range(count)])  3.92 us
    pallas_call x1, Pallas kernels, apply_filter(): pl.pallas_call(functools.partial(filter_kernel, dims), out_shape=jax.Shap...  3.29 us
    pallas_call x1, Pallas kernels, rotate(): pl.pallas_call(functools.partial(rotate_kernel, (rows, bands, own, pieces...  3.08 us
    ppermute x1, waiting for transfers between devices, on_device_fields(): lax.ppermute(blocks, 'band', [(i, i ^ mask) for i in range(pieces)])  2.66 us
  transfers between devices with their start and end apart: 11, of which 6 were waited for; matrix products, arithmetic and copies ran while one was open for 2% of the time, Pallas kernels for 13%

profile of v1, /device:TPU:0, one launch (start us, length us, event | category | flops | bytes accessed | tf_op | source)
XLA Modules:
  0.0 74.3 jit_solution(16953164119900601806)
XLA Ops:
  0.0 0.0 copy-start
  0.0 0.7 copy-done
  0.8 1.0 %pad_maximum_fusion = f32[8,120,128]{2,1,0:T(8,128)S(1)} fusion(f32[8,24,128]{2,1,0:T(8,128)S(1)} %broadcast_in_dim.2, f32[8,96,128]{2,1,0:T(8,128)} %bitcast.11), kind=kLoop, calls=%fused_computation | loop fusion | flops 122880 | bytes 983040 | tf_op jit(solution)/shard_map/concatenate | solution.py:339
  1.8 20.9 %all_to_all.10.own_ref = f32[8,120,128]{2,1,0:T(8,128)S(1)} all-to-all(f32[8,120,128]{2,1,0:T(8,128)S(1)} %pad_maximum_fusion), channel_id=1, replica_groups=mesh['band'=4,'gx'=4,'gy'=2] {'gx','gy'}, dimensions={0} | all-to-all | bytes 983040 | tf_op jit(solution)/shard_map/all_to_all | solution.py:340
  22.7 0.0 copy-start.2
  22.7 0.0 copy-start.3
  22.7 0.1 collective-permute-start
  22.8 1.3 %collective-permute-done.other_ref = f32[8,24,128]{2,1,0:T(8,128)S(1)} collective-permute-done((f32[8,24,128]{2,1,0:T(8,128)S(1)}, f32[8,24,128]{2,1,0:T(8,128)S(1)}, u32[]{:S(2)}, u32[]{:S(2)}) %collective-permute-start) | collective-permute-done | bytes 98336 | tf_op jit(solution)/shard_map/ppermute | solution.py:341
  24.1 0.0 copy-done.2
  24.1 0.0 copy-done.3
  24.1 3.3 %filter.1 = f32[32,24,128]{2,1,0:T(8,128)S(1)} custom-call(s32[1]{0:T(128)} %bitcast.5.core_ref, f32[8,120,128]{2,1,0:T(8,128)S(1)} %all_to_all.10.own_ref, f32[8,24,128]{2,1,0:T(8,128)S(1)} %collective-permute-done.other_ref, bf16[256,256]{1,0:T(8,128)(2,1)S(1)} %copy-done.2, bf16[256,128]{1,0:T(8,128)(2,1)S(1)} %copy-done.3), custom_call_target="tpu_custom_call" | custom-call | tf_op jit(solution)/shard_map/filter/pallas_call | solution.py:220
  27.4 17.1 %all_to_all.11 = f32[32,24,128]{2,1,0:T(8,128)} all-to-all(f32[32,24,128]{2,1,0:T(8,128)S(1)} %filter.1), channel_id=1, replica_groups=mesh['band'=4,'gx'=4,'gy'=2] {'band','gx','gy'}, dimensions={0} | all-to-all | bytes 786432 | tf_op jit(solution)/shard_map/all_to_all | solution.py:344
  44.4 0.5 collective-permute-start.8
  45.0 2.4 %margin.1 = f32[32,128]{1,0:T(8,128)} custom-call(f32[768,128]{1,0:T(8,128)} %bitcast.8.x_ref.refs_0_), custom_call_target="tpu_custom_call" | custom-call | tf_op jit(solution)/shard_map/margin/pallas_call | solution.py:250
  47.4 0.0 collective-permute-start.1
  47.5 1.4 %collective-permute-done.1 = f32[32,128]{1,0:T(8,128)S(1)} collective-permute-done((f32[32,128]{1,0:T(8,128)}, f32[32,128]{1,0:T(8,128)S(1)}, u32[]{:S(2)}, u32[]{:S(2)}) %collective-permute-start.1) | collective-permute-done | bytes 16416 | tf_op jit(solution)/shard_map/ppermute | solution.py:262
  48.8 0.7 add.63
  49.6 1.8 %collective-permute-start.4 = (f32[32,128]{1,0:T(8,128)S(1)}, f32[32,128]{1,0:T(8,128)S(1)}, u32[]{:S(2)}, u32[]{:S(2)}) collective-permute-start(f32[32,128]{1,0:T(8,128)S(1)} %add.63), channel_id=1, source_target_pairs={{0,17},{1,16},{8,25},{9,24},{16,1},{17,0},{24,9},{25,8},{2,19},{3,... | collective-permute-start | bytes 49160 | tf_op jit(solution)/shard_map/ppermute | solution.py:262
  51.3 0.6 collective-permute-start.3
  51.9 1.1 %collective-permute-start.2 = (f32[32,128]{1,0:T(8,128)S(1)}, f32[32,128]{1,0:T(8,128)S(1)}, u32[]{:S(2)}, u32[]{:S(2)}) collective-permute-start(f32[32,128]{1,0:T(8,128)S(1)} %add.63), channel_id=1, source_target_pairs={{0,1},{1,0},{8,9},{9,8},{16,17},{17,16},{24,25},{25,24},{2,3},{3,2... | collective-permute-start | bytes 49160 | tf_op jit(solution)/shard_map/ppermute | solution.py:262
  53.0 0.0 collective-permute-start.9
  53.0 2.7 %collective-permute-done.8.refs_1_ = f32[768,128]{1,0:T(8,128)S(1)} collective-permute-done((f32[768,128]{1,0:T(8,128)}, f32[768,128]{1,0:T(8,128)S(1)}, u32[]{:S(2)}, u32[]{:S(2)}) %collective-permute-start.8) | collective-permute-done | bytes 393248 | tf_op jit(solution)/shard_map/ppermute | solution.py:348
  55.7 0.0 collective-permute-start.10
  55.7 0.9 %collective-permute-done.4 = f32[32,128]{1,0:T(8,128)S(1)} collective-permute-done((f32[32,128]{1,0:T(8,128)S(1)}, f32[32,128]{1,0:T(8,128)S(1)}, u32[]{:S(2)}, u32[]{:S(2)}) %collective-permute-start.4) | collective-permute-done | bytes 16416 | tf_op jit(solution)/shard_map/ppermute | solution.py:262
  56.6 0.0 collective-permute-done.3
  56.6 0.0 collective-permute-done.2
  56.7 0.9 %collective-permute-start.7 = (f32[32,128]{1,0:T(8,128)S(1)}, f32[32,128]{1,0:T(8,128)S(1)}, u32[]{:S(2)}, u32[]{:S(2)}) collective-permute-start(f32[32,128]{1,0:T(8,128)S(1)} %add_add_fusion.1), channel_id=1, source_target_pairs={{0,6},{2,4},{4,2},{6,0},{1,7},{3,5},{5,3},{7,1},{8,14},{10,12},{12... | collective-permute-start | bytes 49160 | tf_op jit(solution)/shard_map/ppermute | solution.py:262
  57.5 1.3 %collective-permute-start.6 = (f32[32,128]{1,0:T(8,128)S(1)}, f32[32,128]{1,0:T(8,128)S(1)}, u32[]{:S(2)}, u32[]{:S(2)}) collective-permute-start(f32[32,128]{1,0:T(8,128)S(1)} %add_add_fusion.1), channel_id=1, source_target_pairs={{0,4},{2,6},{4,0},{6,2},{1,5},{3,7},{5,1},{7,3},{8,12},{10,14},{12... | collective-permute-start | bytes 49160 | tf_op jit(solution)/shard_map/ppermute | solution.py:262
  58.8 2.3 %collective-permute-start.5 = (f32[32,128]{1,0:T(8,128)S(1)}, f32[32,128]{1,0:T(8,128)S(1)}, u32[]{:S(2)}, u32[]{:S(2)}) collective-permute-start(f32[32,128]{1,0:T(8,128)S(1)} %add_add_fusion.1), channel_id=1, source_target_pairs={{0,2},{2,0},{4,6},{6,4},{1,3},{3,1},{5,7},{7,5},{8,10},{10,8},{12,... | collective-permute-start | bytes 49160 | tf_op jit(solution)/shard_map/ppermute | solution.py:262
  61.1 0.1 stack.23.place_ref
  61.2 1.2 %collective-permute-done.7 = f32[32,128]{1,0:T(8,128)S(1)} collective-permute-done((f32[32,128]{1,0:T(8,128)S(1)}, f32[32,128]{1,0:T(8,128)S(1)}, u32[]{:S(2)}, u32[]{:S(2)}) %collective-permute-start.7) | collective-permute-done | bytes 16416 | tf_op jit(solution)/shard_map/ppermute | solution.py:262
  62.4 0.0 collective-permute-done.6
  62.4 0.4 collective-permute-done.5
  62.8 0.6 add_add_fusion.m_ref
  63.4 7.0 %inverse.1.inv_ref = f32[64,64]{1,0:T(8,128)} custom-call(f32[32,128]{1,0:T(8,128)} %add_add_fusion.m_ref), custom_call_target="tpu_custom_call" | custom-call | tf_op jit(solution)/shard_map/inverse/pallas_call | solution.py:285
  70.4 0.0 collective-permute-done.9.refs_2_
  70.4 0.0 collective-permute-done.10.refs_3_
  70.4 0.0 copy-start.1
  70.4 0.8 %copy-done.1 = f32[64,64]{1,0:T(8,128)S(1)} copy-done((f32[64,64]{1,0:T(8,128)S(1)}, f32[64,64]{1,0:T(8,128)}, u32[]{:S(2)}) %copy-start.1) | copy-done | bytes 16408
  71.2 3.1 %rotate.1 = f32[768,128]{1,0:T(8,128)} custom-call(s32[5]{0:T(128)S(1)} %stack.23.place_ref, f32[64,64]{1,0:T(8,128)S(1)} %copy-done.1, f32[768,128]{1,0:T(8,128)} %bitcast.8.x_ref.refs_0_, f32[768,128]{1,0:T(8,128)S(1)} %collective-permute-done.8.refs_1_, f32[768,128]{1,0:T(8,128)S(1)} %collective-permute-done.9.refs_2_, ...), custom_call_target="tpu_custom_call" | custom-call | tf_op jit(solution)/shard_map/rotate/pallas_call | solution.py:313
  (4 shorter events, 0.0 us)
Async XLA Ops:
  0.0 0.7 copy-start
  22.7 1.4 %copy-start.2 = (bf16[256,256]{1,0:T(8,128)(2,1)S(1)}, bf16[256,256]{1,0:T(8,128)(2,1)}, u32[]{:S(2)}) copy-start(bf16[256,256]{1,0:T(8,128)(2,1)} %constant.78.clone.w1_ref) | copy-start | bytes 393220
  22.7 1.4 %copy-start.3 = (bf16[256,128]{1,0:T(8,128)(2,1)S(1)}, bf16[256,128]{1,0:T(8,128)(2,1)}, u32[]{:S(2)}) copy-start(bf16[256,128]{1,0:T(8,128)(2,1)} %constant.79.clone.w2_ref) | copy-start | bytes 196612
  22.7 1.4 %collective-permute-start = (f32[8,24,128]{2,1,0:T(8,128)S(1)}, f32[8,24,128]{2,1,0:T(8,128)S(1)}, u32[]{:S(2)}, u32[]{:S(2)}) collective-permute-start(f32[8,24,128]{2,1,0:T(8,128)S(1)} %slice.4), channel_id=1, source_target_pairs={{0,8},{8,0},{16,24},{24,16},{1,9},{9,1},{17,25},{25,17},{2,10},{10... | collective-permute-start | bytes 294920 | tf_op jit(solution)/shard_map/ppermute | solution.py:341
  44.4 11.3 %collective-permute-start.8 = (f32[768,128]{1,0:T(8,128)}, f32[768,128]{1,0:T(8,128)S(1)}, u32[]{:S(2)}, u32[]{:S(2)}) collective-permute-start(f32[768,128]{1,0:T(8,128)} %bitcast.8.x_ref.refs_0_), channel_id=1, source_target_pairs={{0,16},{8,24},{16,0},{24,8},{1,17},{9,25},{17,1},{25,9},{2,18},{10... | collective-permute-start | bytes 1179656 | tf_op jit(solution)/shard_map/ppermute | solution.py:348
  47.4 1.4 %collective-permute-start.1 = (f32[32,128]{1,0:T(8,128)}, f32[32,128]{1,0:T(8,128)S(1)}, u32[]{:S(2)}, u32[]{:S(2)}) collective-permute-start(f32[32,128]{1,0:T(8,128)} %margin.1), channel_id=1, source_target_pairs={{0,8},{8,0},{16,24},{24,16},{1,9},{9,1},{17,25},{25,17},{2,10},{10... | collective-permute-start | bytes 49160 | tf_op jit(solution)/shard_map/ppermute | solution.py:262
  49.6 7.1 %collective-permute-start.4 = (f32[32,128]{1,0:T(8,128)S(1)}, f32[32,128]{1,0:T(8,128)S(1)}, u32[]{:S(2)}, u32[]{:S(2)}) collective-permute-start(f32[32,128]{1,0:T(8,128)S(1)} %add.63), channel_id=1, source_target_pairs={{0,17},{1,16},{8,25},{9,24},{16,1},{17,0},{24,9},{25,8},{2,19},{3,... | collective-permute-start | bytes 49160 | tf_op jit(solution)/shard_map/ppermute | solution.py:262
  51.3 5.3 %collective-permute-start.3 = (f32[32,128]{1,0:T(8,128)S(1)}, f32[32,128]{1,0:T(8,128)S(1)}, u32[]{:S(2)}, u32[]{:S(2)}) collective-permute-start(f32[32,128]{1,0:T(8,128)S(1)} %add.63), channel_id=1, source_target_pairs={{0,16},{1,17},{8,24},{9,25},{16,0},{17,1},{24,8},{25,9},{2,18},{3,... | collective-permute-start | bytes 49160 | tf_op jit(solution)/shard_map/ppermute | solution.py:262
  51.9 4.7 %collective-permute-start.2 = (f32[32,128]{1,0:T(8,128)S(1)}, f32[32,128]{1,0:T(8,128)S(1)}, u32[]{:S(2)}, u32[]{:S(2)}) collective-permute-start(f32[32,128]{1,0:T(8,128)S(1)} %add.63), channel_id=1, source_target_pairs={{0,1},{1,0},{8,9},{9,8},{16,17},{17,16},{24,25},{25,24},{2,3},{3,2... | collective-permute-start | bytes 49160 | tf_op jit(solution)/shard_map/ppermute | solution.py:262
  53.0 17.4 %collective-permute-start.9 = (f32[768,128]{1,0:T(8,128)}, f32[768,128]{1,0:T(8,128)S(1)}, u32[]{:S(2)}, u32[]{:S(2)}) collective-permute-start(f32[768,128]{1,0:T(8,128)} %bitcast.8.x_ref.refs_0_), channel_id=1, source_target_pairs={{0,8},{8,0},{16,24},{24,16},{1,9},{9,1},{17,25},{25,17},{2,10},{10... | collective-permute-start | bytes 1179656 | tf_op jit(solution)/shard_map/ppermute | solution.py:351
  55.7 14.7 %collective-permute-start.10 = (f32[768,128]{1,0:T(8,128)S(1)}, f32[768,128]{1,0:T(8,128)S(1)}, u32[]{:S(2)}, u32[]{:S(2)}) collective-permute-start(f32[768,128]{1,0:T(8,128)S(1)} %collective-permute-done.8.refs_1_), channel_id=1, source_target_pairs={{0,8},{8,0},{16,24},{24,16},{1,9},{9,1},{17,25},{25,17},{2,10},{10... | collective-permute-start | bytes 1179656 | tf_op jit(solution)/shard_map/ppermute | solution.py:351
  56.7 5.8 %collective-permute-start.7 = (f32[32,128]{1,0:T(8,128)S(1)}, f32[32,128]{1,0:T(8,128)S(1)}, u32[]{:S(2)}, u32[]{:S(2)}) collective-permute-start(f32[32,128]{1,0:T(8,128)S(1)} %add_add_fusion.1), channel_id=1, source_target_pairs={{0,6},{2,4},{4,2},{6,0},{1,7},{3,5},{5,3},{7,1},{8,14},{10,12},{12... | collective-permute-start | bytes 49160 | tf_op jit(solution)/shard_map/ppermute | solution.py:262
  57.5 4.9 %collective-permute-start.6 = (f32[32,128]{1,0:T(8,128)S(1)}, f32[32,128]{1,0:T(8,128)S(1)}, u32[]{:S(2)}, u32[]{:S(2)}) collective-permute-start(f32[32,128]{1,0:T(8,128)S(1)} %add_add_fusion.1), channel_id=1, source_target_pairs={{0,4},{2,6},{4,0},{6,2},{1,5},{3,7},{5,1},{7,3},{8,12},{10,14},{12... | collective-permute-start | bytes 49160 | tf_op jit(solution)/shard_map/ppermute | solution.py:262
  58.8 4.0 %collective-permute-start.5 = (f32[32,128]{1,0:T(8,128)S(1)}, f32[32,128]{1,0:T(8,128)S(1)}, u32[]{:S(2)}, u32[]{:S(2)}) collective-permute-start(f32[32,128]{1,0:T(8,128)S(1)} %add_add_fusion.1), channel_id=1, source_target_pairs={{0,2},{2,0},{4,6},{6,4},{1,3},{3,1},{5,7},{7,5},{8,10},{10,8},{12,... | collective-permute-start | bytes 49160 | tf_op jit(solution)/shard_map/ppermute | solution.py:262
  70.4 0.8 %copy-start.1 = (f32[64,64]{1,0:T(8,128)S(1)}, f32[64,64]{1,0:T(8,128)}, u32[]{:S(2)}) copy-start(f32[64,64]{1,0:T(8,128)} %inverse.1.inv_ref) | copy-start | bytes 49156

commit v2 on v1

--- a/solution.py
+++ b/solution.py
@@ -7,7 +7,7 @@
 from jax import lax
 from jax.experimental import pallas as pl
 from jax.experimental.pallas import tpu as pltpu
-from jax.sharding import PartitionSpec as P
+from jax.sharding import Mesh, PartitionSpec as P
 
 DEGREE = 4
 
@@ -228,109 +228,161 @@
             pltpu.VMEM(padded, jnp.float32),
             pltpu.VMEM((bands, width, height, nz), jnp.float32),
         ],
-        compiler_params=pltpu.CompilerParams(vmem_limit_bytes=40 * 1024 * 1024),
+        compiler_params=pltpu.CompilerParams(vmem_limit_bytes=16 * 1024 * 1024),
         name="filter",
     )(core, own, other, w1, w2)
 
 
 def margin_kernel(rows, bands, scale, x_ref, out_ref):
-    total = jnp.zeros((bands, bands), jnp.float32)
+    highs, mids, lows = [], [], []
     for r in range(rows):
-        block = x_ref[pl.ds(r, bands, stride=rows), :]
-        total = total + lax.dot_general(
-            block, block, (((1,), (1,)), ((), ())), precision=lax.Precision.HIGHEST, preferred_element_type=jnp.float32
-        )
-    total = total * scale
-    out_ref[:, pl.ds(0, bands)] = total[: bands // 2]
-    out_ref[:, pl.ds(bands, bands)] = total[bands // 2 :]
+        high, mid, low = split3(x_ref[pl.ds(r, bands, stride=rows), :])
+        highs.append(high)
+        mids.append(mid)
+        lows.append(low)
+    terms = [jnp.concatenate(term, 1) for term in (highs, mids, lows)]
+    stacked = jnp.concatenate(terms, 0)
+    products = lax.dot_general(stacked, stacked, (((1,), (1,)), ((), ())), preferred_element_type=jnp.float32)
+
+    def block(i, j):
+        return products[i * bands : (i + 1) * bands, j * bands : (j + 1) * bands]
+
+    small = block(0, 2) + block(2, 0) + block(1, 1)
+    total = (small + (block(0, 1) + block(1, 0)) + block(0, 0)) * scale
+    half = bands // 2
+    for at, (i, j) in enumerate(((0, 0), (1, 0), (1, 1))):
+        part = total[i * half : (i + 1) * half, j * half : (j + 1) * half]
+        folds = [part[t * TILE : (t + 1) * TILE] for t in range(half // TILE)]
+        out_ref[pl.ds(at * TILE, TILE), :] = jnp.concatenate(folds, 1)
 
 
 def partial_margin(blocks, bands, scale):
     rows = blocks.shape[0] // bands
     return pl.pallas_call(
         functools.partial(margin_kernel, rows, bands, scale),
-        out_shape=jax.ShapeDtypeStruct((bands // 2, 2 * bands), jnp.float32),
+        out_shape=jax.ShapeDtypeStruct((3 * TILE, bands // 2 * (bands // 2) // TILE), jnp.float32),
         in_specs=[pl.BlockSpec(memory_space=pltpu.VMEM)],
         out_specs=pl.BlockSpec(memory_space=pltpu.VMEM),
+        compiler_params=pltpu.CompilerParams(vmem_limit_bytes=8 * 1024 * 1024),
         name="margin",
     )(blocks)
 
 
-def sum_over(value, axes, masks, count):
-    total = value
-    for mask in masks:
-        total = total + lax.ppermute(value, axes, [(i, i ^ mask) for i in range(count)])
-    return total
-
-
-def inverse_kernel(bands, m_ref, out_ref):
-    folded = m_ref[...]
-    margin = jnp.concatenate([folded[:, :bands], folded[:, bands:]], 0)
+def eliminate(margin, between):
+    bands = margin.shape[0]
+    tiles = bands // TILE
     row_at = lax.broadcasted_iota(jnp.int32, (bands, bands), 0)
     col_at = lax.broadcasted_iota(jnp.int32, (bands, bands), 1)
     both = jnp.concatenate([margin, jnp.where(row_at == col_at, 1.0, 0.0)], 1)
-    lines = lax.broadcasted_iota(jnp.int32, (bands, 1), 0)
-    pivots = jnp.ones((bands, 1), jnp.float32)
-    for j in range(bands):
-        row = both[j : j + 1, :]
-        column = both[:, j : j + 1]
-        pivot = row[:, j : j + 1]
-        pivots = jnp.where(lines == j, pivot, pivots)
-        factor = jnp.where(lines > j, column, 0.0)
-        both = both - factor * (row * (1.0 / pivot))
-    out_ref[...] = both[:, bands:] * lax.rsqrt(pivots)
-
-
-def inverse_factor(folded, bands):
-    return pl.pallas_call(
-        functools.partial(inverse_kernel, bands),
-        out_shape=jax.ShapeDtypeStruct((bands, bands), jnp.float32),
-        in_specs=[pl.BlockSpec(memory_space=pltpu.VMEM)],
-        out_specs=pl.BlockSpec(memory_space=pltpu.VMEM),
-        name="inverse",
-    )(folded)
-
-
-def rotate_kernel(dims, place_ref, inv_ref, *refs):
-    rows, bands, own, pieces = dims
-    parts, out_ref = refs[:-1], refs[-1]
+    width = 2 * bands
+    lines = lax.broadcasted_iota(jnp.int32, (TILE, width), 0)
+    both = [both[t * TILE : (t + 1) * TILE] for t in range(tiles)]
+    for p in range(tiles):
+        between(p)
+        spread = [
+            [
+                jnp.broadcast_to(both[t][:, p * TILE + c : p * TILE + c + 1], (TILE, width)) if t >= p else None
+                for t in range(tiles)
+            ]
+            for c in range(TILE)
+        ]
+        pivots = None
+        for j in range(TILE):
+            pivot = jnp.broadcast_to(spread[j][p][j : j + 1, :], (TILE, width))
+            pivots = pivot if j == 0 else jnp.where(lines == j, pivot, pivots)
+            ratio = 1.0 / pivot
+            factor = [spread[j][t] * ratio if t >= p else None for t in range(tiles)]
+            factor[p] = jnp.where(lines > j, factor[p], 0.0)
+            for c in range(j + 1, TILE):
+                entry = jnp.broadcast_to(spread[j][p][c : c + 1, :], (TILE, width))
+                for t in range(p, tiles):
+                    spread[c][t] = spread[c][t] - factor[t] * entry
+            line = jnp.broadcast_to(both[p][j : j + 1, :], (TILE, width))
+            for t in range(p, tiles):
+                both[t] = both[t] - factor[t] * line
+        both[p] = both[p] * lax.rsqrt(pivots)
+    return jnp.concatenate(both, 0)[:, bands:]
+
+
+def rotate_kernel(dims, place_ref, margins_ref, *refs):
+    rows, bands, own, pieces, tiles = dims
+    parts = refs[:pieces]
+    out_ref, inv_ref, split_ref = refs[pieces:]
+    folded = margins_ref[0]
+    for term in range(1, margins_ref.shape[0]):
+        folded = folded + margins_ref[term]
+    half = bands // 2
+    quarters = []
+    for at in range(3):
+        part = folded[at * TILE : (at + 1) * TILE]
+        quarters.append(jnp.concatenate([part[:, t * half : (t + 1) * half] for t in range(half // TILE)], 0))
+    low, cross, high = quarters
+    margin = jnp.concatenate(
+        [jnp.concatenate([low, cross.T], 1), jnp.concatenate([cross, high], 1)], 0
+    )
+    jobs = [(part, r) for part in range(pieces) for r in range(rows)]
+    nz = parts[0].shape[1]
+
+    def split_some(step):
+        share = -(-len(jobs) // tiles)
+        for at in range(step * share, min(len(jobs), (step + 1) * share)):
+            part, r = jobs[at]
+            terms_of = split3(parts[part][pl.ds(r, bands, stride=rows), :])
+            for i, term in enumerate(terms_of):
+                split_ref[at // 2, pl.ds(i * bands, bands), pl.ds((at % 2) * nz, nz)] = term
+
+    inv_ref[...] = eliminate(margin, split_some)
     first = pl.multiple_of(place_ref[0], TILE)
-    inverse = inv_ref[pl.ds(first, own), :]
-    for index, part in enumerate(parts):
-        at = place_ref[1 + index]
-        for r in range(rows):
-            block = part[pl.ds(r, bands, stride=rows), :]
-            value = jnp.dot(inverse, block, precision=lax.Precision.HIGHEST, preferred_element_type=jnp.float32)
-            out_ref[pl.ds(at + r, own, stride=rows * pieces), :] = value
-
-
-def rotate(place, inverse, parts, own):
-    bands = inverse.shape[0]
+    high, mid, low = split3(inv_ref[pl.ds(first, own), :])
+    zero = jnp.zeros_like(high)
+    left = jnp.concatenate(
+        [
+            jnp.concatenate([high, high, high], 1),
+            jnp.concatenate([mid, mid, zero], 1),
+            jnp.concatenate([low, zero, zero], 1),
+        ],
+        0,
+    )
+    for pair in range(len(jobs) // 2):
+        product = jnp.dot(left, split_ref[pair], preferred_element_type=jnp.float32)
+        value = product[:own] + (product[own : 2 * own] + product[2 * own :])
+        for i in range(2):
+            part, r = jobs[2 * pair + i]
+            start = place_ref[1 + part] + r
+            out_ref[pl.ds(start, own, stride=rows * pieces), :] = value[:, i * nz : (i + 1) * nz]
+
+
+def rotate(place, margins, parts, own, bands):
     pieces = len(parts)
     rows = parts[0].shape[0] // bands
     nz = parts[0].shape[1]
     vmem = pl.BlockSpec(memory_space=pltpu.VMEM)
+    dims = (rows, bands, own, pieces, bands // TILE)
     return pl.pallas_call(
-        functools.partial(rotate_kernel, (rows, bands, own, pieces)),
+        functools.partial(rotate_kernel, dims),
         out_shape=jax.ShapeDtypeStruct((own * rows * pieces, nz), jnp.float32),
         in_specs=[pl.BlockSpec(memory_space=pltpu.SMEM)] + [vmem] * (1 + pieces),
         out_specs=vmem,
-        compiler_params=pltpu.CompilerParams(vmem_limit_bytes=32 * 1024 * 1024),
+        scratch_shapes=[
+            pltpu.VMEM((bands, bands), jnp.float32),
+            pltpu.VMEM((rows * pieces // 2, 3 * bands, 2 * nz), jnp.bfloat16),
+        ],
+        compiler_params=pltpu.CompilerParams(vmem_limit_bytes=12 * 1024 * 1024),
         name="rotate",
-    )(place, inverse, *parts)
+    )(place, margins, *parts)
 
 
 def on_device_fields(start_bands, potential):
     own_bands, nx, ny, nz = start_bands.shape
-    gx, gy, pieces = lax.axis_size("gx"), lax.axis_size("gy"), lax.axis_size("band")
+    gx, gy, chips = lax.axis_size("gx"), lax.axis_size("gy"), lax.axis_size("chip")
+    pieces = 2 * chips
     grid = gx * gy
     own = own_bands // grid
     cells = nx * ny
     bands = own_bands * pieces
     rows = cells // pieces
-    band = lax.axis_index("band")
-    core = band % 2
-    swap = [(i, i ^ 1) for i in range(pieces)]
+    chip, core = lax.axis_index("chip"), lax.axis_index("core")
+    swap = [(0, 1), (1, 0)]
 
     fields = start_bands.reshape(grid, own * cells, nz)
     flat_potential = potential.reshape(cells, nz)
@@ -338,29 +390,28 @@
     own_half = lax.dynamic_slice_in_dim(flat_potential, core * half, half, 0)
     packed = jnp.concatenate([fields, jnp.broadcast_to(own_half[None], (grid, half, nz))], 1)
     packed = lax.all_to_all(packed, ("gx", "gy"), 0, 0)
-    other = lax.ppermute(packed[:, own * cells :, :], "band", swap)
+    other = lax.ppermute(packed[:, own * cells :, :], "core", swap)
     dims = (gx, gy, own, nx, ny, nz, pieces)
     filtered = apply_filter(core.reshape(1), packed, other, dims)
-    blocks = lax.all_to_all(filtered, ("band", "gx", "gy"), 0, 0).reshape(bands * rows, nz)
-
-    parts, offsets = [blocks], [band]
-    for mask in range(2, pieces, 2):
-        parts.append(lax.ppermute(blocks, "band", [(i, i ^ mask) for i in range(pieces)]))
-        offsets.append(band ^ mask)
-    for index in range(len(parts)):
-        parts.append(lax.ppermute(parts[index], "band", swap))
-        offsets.append(offsets[index] ^ 1)
-    chips = pieces // 2
-    offsets = [((at % 2) * chips + at // 2) * rows for at in offsets]
+    blocks = lax.all_to_all(filtered, ("chip", "core", "gx", "gy"), 0, 0).reshape(bands * rows, nz)
 
     margin = partial_margin(blocks, bands, 1.0 / (cells * nz * grid))
-    margin = sum_over(margin, "band", [1], pieces)
-    masks = [chip * 2 * gy + y for chip in range(chips) for y in range(gy)][1:]
-    margin = sum_over(margin, ("band", "gy"), masks, pieces * gy)
-    margin = sum_over(margin, "gx", range(1, gx), gx)
-    inverse = inverse_factor(margin, bands)
-    place = jnp.stack([band * own_bands] + offsets).astype(jnp.int32)
-    rotated = rotate(place, inverse, parts, own_bands)
+    margin = margin + lax.ppermute(margin, "core", swap)
+    margins = jnp.broadcast_to(margin[None], (chips * grid,) + margin.shape)
+    margins = lax.all_to_all(margins, ("chip", "gx", "gy"), 0, 0)
+
+    parts, offsets = [blocks], [(core * chips + chip) * rows]
+    for mask in range(1, chips):
+        parts.append(lax.ppermute(blocks, "chip", [(i, i ^ mask) for i in range(chips)]))
+        offsets.append((core * chips + (chip ^ mask)) * rows)
+    for index in range(chips):
+        source = parts[index]
+        if index:
+            source, margins = lax.optimization_barrier((source, margins))
+        parts.append(lax.ppermute(source, "core", swap))
+        offsets.append((1 - core) * chips * rows + offsets[index] - core * chips * rows)
+    place = jnp.stack([(chip * 2 + core) * own_bands] + offsets).astype(jnp.int32)
+    rotated = rotate(place, margins, parts, own_bands, bands)
     return rotated.reshape(start_bands.shape)
 
 
@@ -368,30 +419,40 @@
     return count & (count - 1) == 0
 
 
-def on_device(start_bands, potential):
-    own_bands, nx, ny, nz = start_bands.shape
-    gx, gy, pieces = lax.axis_size("gx"), lax.axis_size("gy"), lax.axis_size("band")
-    cells = nx * ny
-    whole_fields = (
+def whole_fields(mesh, shape):
+    gx, gy, pieces = mesh.shape["gx"], mesh.shape["gy"], mesh.shape["band"]
+    bands, nx, ny, nz = shape[0], shape[1] // gx, shape[2] // gy, shape[3]
+    own_bands, cells = bands // pieces, nx * ny
+    return (
         own_bands % (gx * gy) == 0
-        and own_bands % TILE == 0
-        and all(power_of_two(count) for count in (gx, gy, pieces))
-        and pieces > 1
+        and own_bands % (2 * TILE) == 0
+        and pieces % 2 == 0
+        and power_of_two(pieces)
         and ny % TILE == 0
         and nz % 128 == 0
+        and bands // 2 * (bands // 2) // TILE % 128 == 0
         and cells % (2 * TILE) == 0
         and cells % (pieces * TILE // 2) == 0
         and (own_bands // (gx * gy)) * (cells // pieces) % TILE == 0
-        and gx * nx > 2 * REACH
+        and shape[1] > 2 * REACH
     )
-    if whole_fields:
-        return on_device_fields(start_bands, potential)
-    return on_device_halo(start_bands, potential)
 
 
 def solution(mesh):
-    in_specs = (P("band", "gx", "gy", None), P("gx", "gy", None))
-    out_specs = P("band", "gx", "gy", None)
-    return jax.shard_map(
-        on_device, mesh=mesh, in_specs=in_specs, out_specs=out_specs, check_vma=False
-    )
+    def step(start_bands, potential):
+        if whole_fields(mesh, start_bands.shape):
+            chips = mesh.shape["band"] // 2
+            rest = mesh.devices.shape[1:]
+            split = Mesh(mesh.devices.reshape((chips, 2) + rest), ("chip", "core") + mesh.axis_names[1:])
+            program, band = on_device_fields, ("chip", "core")
+        else:
+            split, program, band = mesh, on_device_halo, "band"
+        return jax.shard_map(
+            program,
+            mesh=split,
+            in_specs=(P(band, "gx", "gy", None), P("gx", "gy", None)),
+            out_specs=P(band, "gx", "gy", None),
+            check_vma=False,
+        )(start_bands, potential)
+
+    return step

time: 74.8 us -> 66.3 us (0.89)
  Pallas kernels: 15.8 us -> 7.91 us
  waiting for transfers between devices: 7.87 us -> 12.7 us
  starting transfers between devices: 8.6 us -> 4.86 us
  other arithmetic: 2.36 us -> 1.04 us
    all_to_all x0 -> x1, waiting for transfers between devices: none -> 8.63 us  [on_device_fields(): margins = lax.all_to_all(margins, ('chip', 'gx', 'gy'), 0, 0)]
    ppermute x11 -> x5, starting transfers between devices: 8.6 us -> 0.79 us  [the longest x1 0.55 us: on_device_fields(): lax.ppermute(blocks, 'chip', [(i, i ^ mask) for i in range(chips)])]
    pallas_call x2 -> x1, Pallas kernels: 10.1 us -> 4.09 us  [rotate(): pl.pallas_call(functools.partial(rotate_kernel, dims), out_shape=jax.Shap...]
    all_to_all x0 -> x1, starting transfers between devices: none -> 4.07 us  [on_device_fields(): margins = lax.all_to_all(margins, ('chip', 'gx', 'gy'), 0, 0)]
    ppermute x11 -> x5, waiting for transfers between devices: 7.87 us -> 4.07 us  [the longest x2 1.64 us: on_device_fields(): parts.append(lax.ppermute(source, 'core', swap))]
    pallas_call x1, Pallas kernels: 2.44 us -> 0.53 us  [partial_margin(): pl.pallas_call(functools.partial(margin_kernel, rows, bands, scale), out_...]
    add x3 -> x1, other arithmetic: 1.33 us -> 0.01 us  [on_device_fields(): margin = margin + lax.ppermute(margin, 'core', swap)]
    unnamed x8 -> x6, local copies, waits for them, and re-layouts: 1.5 us -> 0.74 us
  transfers between devices with their start and end apart: 11 -> 6, of which waited for: 6 -> 4; matrix products, arithmetic and copies ran while one was open for 2% -> 1% of each run, Pallas kernels for 13% -> 1%
where the time goes in v2:
time: 66.3 us; the launch traced here: 66 us
  blocking collectives  37.9 us (57%)
  waiting for transfers between devices  12.7 us (19%)
  Pallas kernels  7.91 us (12%)
  starting transfers between devices  4.86 us (7%)
  local copies, waits for them, and re-layouts  1.54 us (2%)
  other arithmetic  1.04 us (2%)
    all_to_all x1, blocking collectives, on_device_fields(): packed = lax.all_to_all(packed, ('gx', 'gy'), 0, 0)  20.9 us
    all_to_all x1, blocking collectives, on_device_fields(): lax.all_to_all(filtered, ('chip', 'core', 'gx', 'gy'), 0, 0)  17 us
    all_to_all x1, waiting for transfers between devices, on_device_fields(): margins = lax.all_to_all(margins, ('chip', 'gx', 'gy'), 0, 0)  8.63 us
    pallas_call x1, Pallas kernels, rotate(): pl.pallas_call(functools.partial(rotate_kernel, dims), out_shape=jax.Shap...  4.09 us
    all_to_all x1, starting transfers between devices, on_device_fields(): margins = lax.all_to_all(margins, ('chip', 'gx', 'gy'), 0, 0)  4.07 us
    pallas_call x1, Pallas kernels, apply_filter(): pl.pallas_call(functools.partial(filter_kernel, dims), out_shape=jax.Shap...  3.29 us
    ppermute x2, waiting for transfers between devices, on_device_fields(): parts.append(lax.ppermute(source, 'core', swap))  1.64 us
  transfers between devices with their start and end apart: 6, of which 4 were waited for; matrix products, arithmetic and copies ran while one was open for 1% of the time, Pallas kernels for 1%

profile of v2, /device:TPU:0, one launch (start us, length us, event | category | flops | bytes accessed | tf_op | source)
XLA Modules:
  0.0 66.0 jit_solution(742416977611527869)
XLA Ops:
  0.0 0.0 copy-start
  0.0 0.7 %copy-done = f32[6,8,128]{2,1,0:T(8,128)S(1)} copy-done((f32[6,8,128]{2,1,0:T(8,128)S(1)}, f32[6,8,128]{2,1,0:T(8,128)}, u32[]{:S(2)}) %copy-start) | copy-done | bytes 24600
  0.8 1.0 %pad_maximum_fusion = f32[8,120,128]{2,1,0:T(8,128)S(1)} fusion(f32[8,24,128]{2,1,0:T(8,128)S(1)} %broadcast_in_dim.4, f32[8,96,128]{2,1,0:T(8,128)} %bitcast.15), kind=kLoop, calls=%fused_computation | loop fusion | flops 122880 | bytes 983040 | tf_op jit(solution)/shard_map/concatenate | solution.py:391
  1.8 20.9 %all_to_all.15.own_ref = f32[8,120,128]{2,1,0:T(8,128)S(1)} all-to-all(f32[8,120,128]{2,1,0:T(8,128)S(1)} %pad_maximum_fusion), channel_id=1, replica_groups=mesh['chip'=2,'core'=2,'gx'=4,'gy'=2] {'gx','gy'}, dimensions={0} | all-to-all | bytes 983040 | tf_op jit(solution)/shard_map/all_to_all | solution.py:392
  22.7 0.0 copy-start.1
  22.7 0.0 copy-start.2
  22.7 0.1 collective-permute-start
  22.8 1.3 %collective-permute-done.other_ref = f32[8,24,128]{2,1,0:T(8,128)S(1)} collective-permute-done((f32[8,24,128]{2,1,0:T(8,128)S(1)}, f32[8,24,128]{2,1,0:T(8,128)S(1)}, u32[]{:S(2)}, u32[]{:S(2)}) %collective-permute-start) | collective-permute-done | bytes 98336 | tf_op jit(solution)/shard_map/ppermute | solution.py:393
  24.1 0.0 copy-done.1
  24.1 0.0 copy-done.2
  24.1 3.3 %filter.1 = f32[32,24,128]{2,1,0:T(8,128)S(1)} custom-call(s32[1]{0:T(128)} %bitcast.5.core_ref, f32[8,120,128]{2,1,0:T(8,128)S(1)} %all_to_all.15.own_ref, f32[8,24,128]{2,1,0:T(8,128)S(1)} %collective-permute-done.other_ref, bf16[256,256]{1,0:T(8,128)(2,1)S(1)} %copy-done.1, bf16[256,128]{1,0:T(8,128)(2,1)S(1)} %copy-done.2), custom_call_target="tpu_custom_call" | custom-call | tf_op jit(solution)/shard_map/filter/pallas_call | solution.py:220
  27.4 17.0 %all_to_all.16 = f32[32,24,128]{2,1,0:T(8,128)S(1)} all-to-all(f32[32,24,128]{2,1,0:T(8,128)S(1)} %filter.1), channel_id=1, replica_groups=mesh['chip'=2,'core'=2,'gx'=4,'gy'=2] {'chip','core','gx','gy'}, dimensions={0} | all-to-all | bytes 786432 | tf_op jit(solution)/shard_map/all_to_all | solution.py:396
  44.3 0.5 collective-permute-start.1
  44.9 0.5 margin.1
  45.4 0.1 collective-permute-start.2
  45.5 1.1 %collective-permute-done.2 = f32[24,128]{1,0:T(8,128)S(1)} collective-permute-done((f32[24,128]{1,0:T(8,128)S(1)}, f32[24,128]{1,0:T(8,128)S(1)}, u32[]{:S(2)}, u32[]{:S(2)}) %collective-permute-start.2) | collective-permute-done | bytes 12320 | tf_op jit(solution)/shard_map/ppermute | solution.py:399
  46.7 0.7 %broadcast_in_dim.5 = f32[16,24,128]{2,1,0:T(8,128)} broadcast(f32[24,128]{1,0:T(8,128)S(1)} %add.27), dimensions={1,2} | broadcast | bytes 208896 | tf_op jit(solution)/shard_map/broadcast_in_dim | solution.py:400
  47.4 4.1 %all-to-all-start.2 = ((f32[16,24,128]{2,1,0:T(8,128)}), f32[16,24,128]{2,1,0:T(8,128)S(1)}, u32[]{:S(2)}, u32[]{:S(2)}) async-start(f32[16,24,128]{2,1,0:T(8,128)} %broadcast_in_dim.5), calls=%async_computation.2 | async-start | bytes 393216 | tf_op jit(solution)/shard_map/all_to_all | solution.py:401
  51.4 0.1 collective-permute-start.3
  51.5 8.6 %all-to-all-done.2.margins_ref = f32[16,24,128]{2,1,0:T(8,128)S(1)} async-done(((f32[16,24,128]{2,1,0:T(8,128)}), f32[16,24,128]{2,1,0:T(8,128)S(1)}, u32[]{:S(2)}, u32[]{:S(2)}) %all-to-all-start.2) | async-done | bytes 196640 | tf_op jit(solution)/shard_map/all_to_all | solution.py:401
  60.1 0.0 collective-permute-done.1.refs_1_
  60.1 0.0 collective-permute-start.4
  60.1 0.1 stack.23.place_ref
  60.2 0.0 collective-permute-done.3.refs_2_
  60.2 1.6 %collective-permute-done.4.refs_3_ = f32[768,128]{1,0:T(8,128)S(1)} collective-permute-done((f32[768,128]{1,0:T(8,128)S(1)}, f32[768,128]{1,0:T(8,128)S(1)}, u32[]{:S(2)}, u32[]{:S(2)}) %collective-permute-start.4) | collective-permute-done | bytes 393248 | tf_op jit(solution)/shard_map/ppermute | solution.py:411
  61.9 4.1 %rotate.1 = f32[768,128]{1,0:T(8,128)} custom-call(s32[5]{0:T(128)S(1)} %stack.23.place_ref, f32[16,24,128]{2,1,0:T(8,128)S(1)} %all-to-all-done.2.margins_ref, f32[768,128]{1,0:T(8,128)S(1)} %bitcast.14, f32[768,128]{1,0:T(8,128)S(1)} %collective-permute-done.1.refs_1_, f32[768,128]{1,0:T(8,128)S(1)} %collective-permute-done.3.refs_2_, ...), custom_call_target="tpu_custom_call" | custom-call | tf_op jit(solution)/shard_map/rotate/pallas_call | solution.py:361
  (4 shorter events, 0.0 us)
Async XLA Ops:
  0.0 0.7 %copy-start = (f32[6,8,128]{2,1,0:T(8,128)S(1)}, f32[6,8,128]{2,1,0:T(8,128)}, u32[]{:S(2)}) copy-start(f32[6,8,128]{2,1,0:T(8,128)} %param.5) | copy-start | bytes 73732
  22.7 1.4 %copy-start.1 = (bf16[256,256]{1,0:T(8,128)(2,1)S(1)}, bf16[256,256]{1,0:T(8,128)(2,1)}, u32[]{:S(2)}) copy-start(bf16[256,256]{1,0:T(8,128)(2,1)} %constant.30.clone.w1_ref) | copy-start | bytes 393220
  22.7 1.4 %copy-start.2 = (bf16[256,128]{1,0:T(8,128)(2,1)S(1)}, bf16[256,128]{1,0:T(8,128)(2,1)}, u32[]{:S(2)}) copy-start(bf16[256,128]{1,0:T(8,128)(2,1)} %constant.31.clone.w2_ref) | copy-start | bytes 196612
  22.7 1.4 %collective-permute-start = (f32[8,24,128]{2,1,0:T(8,128)S(1)}, f32[8,24,128]{2,1,0:T(8,128)S(1)}, u32[]{:S(2)}, u32[]{:S(2)}) collective-permute-start(f32[8,24,128]{2,1,0:T(8,128)S(1)} %slice.4), channel_id=1, source_target_pairs={{0,8},{8,0},{1,9},{9,1},{2,10},{10,2},{3,11},{11,3},{4,12},{12,4},... | collective-permute-start | bytes 294920 | tf_op jit(solution)/shard_map/ppermute | solution.py:393
  44.3 15.8 %collective-permute-start.1 = (f32[768,128]{1,0:T(8,128)S(1)}, f32[768,128]{1,0:T(8,128)S(1)}, u32[]{:S(2)}, u32[]{:S(2)}) collective-permute-start(f32[768,128]{1,0:T(8,128)S(1)} %bitcast.11), channel_id=1, source_target_pairs={{0,16},{16,0},{1,17},{17,1},{2,18},{18,2},{3,19},{19,3},{4,20},{20... | collective-permute-start | bytes 1179656 | tf_op jit(solution)/shard_map/ppermute | solution.py:405
  45.4 1.2 %collective-permute-start.2 = (f32[24,128]{1,0:T(8,128)S(1)}, f32[24,128]{1,0:T(8,128)S(1)}, u32[]{:S(2)}, u32[]{:S(2)}) collective-permute-start(f32[24,128]{1,0:T(8,128)S(1)} %margin.1), channel_id=1, source_target_pairs={{0,8},{8,0},{1,9},{9,1},{2,10},{10,2},{3,11},{11,3},{4,12},{12,4},... | collective-permute-start | bytes 36872 | tf_op jit(solution)/shard_map/ppermute | solution.py:399
  47.4 12.8 %all-to-all-start.2 = ((f32[16,24,128]{2,1,0:T(8,128)}), f32[16,24,128]{2,1,0:T(8,128)S(1)}, u32[]{:S(2)}, u32[]{:S(2)}) async-start(f32[16,24,128]{2,1,0:T(8,128)} %broadcast_in_dim.5), calls=%async_computation.2 | async-start | bytes 393216 | tf_op jit(solution)/shard_map/all_to_all | solution.py:401
  51.4 8.8 %collective-permute-start.3 = (f32[768,128]{1,0:T(8,128)S(1)}, f32[768,128]{1,0:T(8,128)S(1)}, u32[]{:S(2)}, u32[]{:S(2)}) collective-permute-start(f32[768,128]{1,0:T(8,128)S(1)} %bitcast.13), channel_id=1, source_target_pairs={{0,8},{8,0},{1,9},{9,1},{2,10},{10,2},{3,11},{11,3},{4,12},{12,4},... | collective-permute-start | bytes 1179656 | tf_op jit(solution)/shard_map/ppermute | solution.py:411
  60.1 1.7 %collective-permute-start.4 = (f32[768,128]{1,0:T(8,128)S(1)}, f32[768,128]{1,0:T(8,128)S(1)}, u32[]{:S(2)}, u32[]{:S(2)}) collective-permute-start(f32[768,128]{1,0:T(8,128)S(1)} %collective-permute-done.1.refs_1_), channel_id=1, source_target_pairs={{0,8},{8,0},{1,9},{9,1},{2,10},{10,2},{3,11},{11,3},{4,12},{12,4},... | collective-permute-start | bytes 1179656 | tf_op jit(solution)/shard_map/ppermute | solution.py:411

commit v3 on v2

--- a/solution.py
+++ b/solution.py
@@ -2,8 +2,6 @@
 
 import jax
 import jax.numpy as jnp
-import ml_dtypes
-import numpy as np
 from jax import lax
 from jax.experimental import pallas as pl
 from jax.experimental.pallas import tpu as pltpu
@@ -127,78 +125,110 @@
 
 
 def z_weights(nz):
-    circulant = np.zeros((nz, nz), np.float32)
-    at = np.arange(nz)
+    row = lax.broadcasted_iota(jnp.int32, (nz, nz), 0)
+    col = lax.broadcasted_iota(jnp.int32, (nz, nz), 1)
+    apart = jnp.abs(row - col)
+    apart = jnp.minimum(apart, nz - apart)
+    circulant = jnp.zeros((nz, nz), jnp.float32)
     for offset in range(1, REACH + 1):
-        circulant[at, (at + offset) % nz] += np.float32(-0.5 * COEFFS[offset])
-        circulant[at, (at - offset) % nz] += np.float32(-0.5 * COEFFS[offset])
-    high = circulant.astype(ml_dtypes.bfloat16)
-    rest = circulant - high.astype(np.float32)
-    mid = rest.astype(ml_dtypes.bfloat16)
-    low = (rest - mid.astype(np.float32)).astype(ml_dtypes.bfloat16)
-    first = np.block([[high, mid], [high, mid]])
-    second = np.concatenate([high, low], 0)
-    return first, second
-
-
-def filter_kernel(dims, core_ref, own_ref, other_ref, w1_ref, w2_ref, out_ref, pot, buf_a, buf_b, zbuf):
-    gx, gy, own, nx, ny, nz, pieces = dims
-    width = gx * nx
-    height = gy * ny
-    cells = nx * ny
-    half = cells // 2
-    rows = cells // pieces
-    middle, first, others = filter_weights(DEGREE)
-    shift = -middle - 1.5 * COEFFS[0]
-    pad = TILE
-
-    def place(buf, k, x, tile, value):
-        buf[k, x, pl.ds(pad + tile * TILE, TILE), :] = value
-        if tile == 0:
-            buf[k, x, pl.ds(pad + height, TILE), :] = value
-        if tile == height // TILE - 1:
-            buf[k, x, pl.ds(0, TILE), :] = value
-
-    core = core_ref[0]
+        circulant = jnp.where(apart == offset, -0.5 * COEFFS[offset], circulant)
+    return split3(circulant)
+
+
+PAD = TILE
+
+
+def place(buf, k, x, tile, height, value):
+    buf[k, x, pl.ds(PAD + tile * TILE, TILE), :] = value
+    if tile == 0:
+        buf[k, x, pl.ds(PAD + height, TILE), :] = value
+    if tile == height // TILE - 1:
+        buf[k, x, pl.ds(0, TILE), :] = value
+
+
+def along_z(field, w1_ref, w2_ref):
+    nz = field.shape[1]
+    high, mid, low = split3(field)
+    part = jnp.dot(jnp.concatenate([high, mid], 1), w1_ref[...], preferred_element_type=jnp.float32)
+    rest = jnp.dot(jnp.concatenate([low, high], 1), w2_ref[...], preferred_element_type=jnp.float32)
+    return part[:, :nz] + part[:, nz:] + rest
+
+
+def add_xy(src, k, x, tile, total):
+    width = src.shape[1]
+    at = PAD + tile * TILE
+    for j in range(1, REACH + 1):
+        near = src[k, (x + j) % width, pl.ds(at, TILE), :] + src[k, (x - j) % width, pl.ds(at, TILE), :]
+        near = near + src[k, x, pl.ds(at + j, TILE), :] + src[k, x, pl.ds(at - j, TILE), :]
+        total = total + (-0.5 * COEFFS[j]) * near
+    return total
+
+
+def laplace_kernel(dims, in_ref, field_ref, lap_ref, w1_ref, w2_ref):
+    gx, gy, own, nx, ny, nz, pieces, skip = dims
+    width, height, cells = gx * nx, gy * ny, nx * ny
+    high, mid, low = z_weights(nz)
+    for at in (0, nz):
+        w1_ref[pl.ds(at, nz), pl.ds(0, nz)] = high
+        w1_ref[pl.ds(at, nz), pl.ds(nz, nz)] = mid
+    w2_ref[pl.ds(0, nz), :] = high
+    w2_ref[pl.ds(nz, nz), :] = low
     for g in range(gx * gy):
         at_x, at_y = (g // gy) * nx, (g % gy) * ny
         for k in range(own):
             for i in range(nx):
                 for t in range(ny // TILE):
-                    value = own_ref[g, pl.ds(k * cells + i * ny + t * TILE, TILE), :]
-                    place(buf_a, k, at_x + i, at_y // TILE + t, value)
+                    value = in_ref[g, pl.ds(k * cells + i * ny + t * TILE, TILE), :]
+                    place(field_ref, k, at_x + i, at_y // TILE + t, height, value)
+    field = field_ref[:, :, pl.ds(PAD, height), :].reshape(own * width * height, nz)
+    lap_ref[...] = along_z(field, w1_ref, w2_ref).reshape(own, width, height, nz)
+    for k in range(own):
+        for x in range(width):
+            for tile in range(height // TILE):
+                rows = pl.ds(tile * TILE, TILE)
+                lap_ref[k, x, rows, :] = add_xy(field_ref, k, x, tile, lap_ref[k, x, rows, :])
+
+
+def filter_kernel(dims, core_ref, field_ref, lap_ref, half_ref, other_ref, w1_ref, w2_ref, out_ref, pot, buf_a, buf_b, zbuf):
+    gx, gy, own, nx, ny, nz, pieces, skip = dims
+    width, height, cells = gx * nx, gy * ny, nx * ny
+    half = cells // 2
+    rows = cells // pieces
+    middle, first, others = filter_weights(DEGREE)
+    shift = -middle - 1.5 * COEFFS[0]
+
+    core = core_ref[0]
+    for g in range(gx * gy):
         mine = pl.ds(pl.multiple_of(core * half, TILE), half)
         theirs = pl.ds(pl.multiple_of((1 - core) * half, TILE), half)
-        pot[g, mine, :] = own_ref[g, own * cells :, :] + shift
+        pot[g, mine, :] = half_ref[g, pl.ds(skip, half), :] + shift
         pot[g, theirs, :] = other_ref[g] + shift
 
-    buffers = (buf_a, buf_b)
+    chain = (field_ref, buf_a, buf_b, buf_a)
     steps = [(first, None)] + others
     for step, (scale, back) in enumerate(steps):
-        src, dst = buffers[step % 2], buffers[(step + 1) % 2]
+        src, dst, old = chain[step], buf_b if step % 2 else buf_a, chain[step - 1]
         last = step == len(steps) - 1
-        field = src[:, :, pl.ds(pad, height), :].reshape(own * width * height, nz)
-        high, mid, low = split3(field)
-        part = jnp.dot(jnp.concatenate([high, mid], 1), w1_ref[...], preferred_element_type=jnp.float32)
-        rest = jnp.dot(jnp.concatenate([low, high], 1), w2_ref[...], preferred_element_type=jnp.float32)
-        zbuf[...] = (part[:, :nz] + part[:, nz:] + rest).reshape(own, width, height, nz)
+        if step:
+            field = src[:, :, pl.ds(PAD, height), :].reshape(own * width * height, nz)
+            zbuf[...] = along_z(field, w1_ref, w2_ref).reshape(own, width, height, nz)
         for k in range(own):
             for x in range(width):
                 for tile in range(height // TILE):
                     g = (x // nx) * gy + tile * TILE // ny
                     in_pencil = (x % nx) * ny + (tile * TILE) % ny
-                    at = pad + tile * TILE
-                    centre = src[k, x, pl.ds(at, TILE), :]
-                    total = zbuf[k, x, pl.ds(tile * TILE, TILE), :] + pot[g, pl.ds(in_pencil, TILE), :] * centre
-                    for j in range(1, REACH + 1):
-                        near = src[k, (x + j) % width, pl.ds(at, TILE), :] + src[k, (x - j) % width, pl.ds(at, TILE), :]
-                        near = near + src[k, x, pl.ds(at + j, TILE), :] + src[k, x, pl.ds(at - j, TILE), :]
-                        total = total + (-0.5 * COEFFS[j]) * near
+                    inner = pl.ds(PAD + tile * TILE, TILE)
+                    plain = pl.ds(tile * TILE, TILE)
+                    if step:
+                        total = add_xy(src, k, x, tile, zbuf[k, x, plain, :])
+                    else:
+                        total = lap_ref[k, x, plain, :]
+                    total = total + pot[g, pl.ds(in_pencil, TILE), :] * src[k, x, inner, :]
                     value = scale * total
-                    if back is not None:
-                        value = value - back * dst[k, x, pl.ds(at, TILE), :]
+                    if step:
+                        value = value - back * old[k, x, inner, :]
                     if not last:
-                        place(dst, k, x, tile, value)
+                        place(dst, k, x, tile, height, value)
                         continue
                     for r in range(0, TILE, TILE // 2):
                         piece, row = divmod(in_pencil + r, rows)
@@ -211,26 +241,44 @@
     return (piece % chips) * 2 + piece // chips
 
 
-def apply_filter(core, own, other, dims):
-    gx, gy, bands, nx, ny, nz, pieces = dims
+def first_laplace(packed, dims):
+    gx, gy, bands, nx, ny, nz, pieces, skip = dims
     width, height = gx * nx, gy * ny
-    w1, w2 = z_weights(nz)
-    padded = (bands, width, height + 2 * TILE, nz)
+    vmem = pl.BlockSpec(memory_space=pltpu.VMEM)
+    cells = bands * width * height * nz
+    return pl.pallas_call(
+        functools.partial(laplace_kernel, dims),
+        out_shape=(
+            jax.ShapeDtypeStruct((bands, width, height + 2 * PAD, nz), jnp.float32),
+            jax.ShapeDtypeStruct((bands, width, height, nz), jnp.float32),
+            jax.ShapeDtypeStruct((2 * nz, 2 * nz), jnp.bfloat16),
+            jax.ShapeDtypeStruct((2 * nz, nz), jnp.bfloat16),
+        ),
+        in_specs=[vmem],
+        out_specs=(vmem,) * 4,
+        compiler_params=pltpu.CompilerParams(vmem_limit_bytes=12 * 1024 * 1024),
+        cost_estimate=pl.CostEstimate(flops=44 * cells, bytes_accessed=16 * cells, transcendentals=0),
+        name="laplace",
+    )(packed)
+
+
+def apply_filter(core, field, laplace, packed, other, weights, dims):
+    gx, gy, bands, nx, ny, nz, pieces, skip = dims
     vmem = pl.BlockSpec(memory_space=pltpu.VMEM)
     return pl.pallas_call(
         functools.partial(filter_kernel, dims),
         out_shape=jax.ShapeDtypeStruct((pieces * gx * gy, bands * nx * ny // pieces, nz), jnp.float32),
-        in_specs=[pl.BlockSpec(memory_space=pltpu.SMEM)] + [vmem] * 4,
+        in_specs=[pl.BlockSpec(memory_space=pltpu.SMEM)] + [vmem] * 6,
         out_specs=vmem,
         scratch_shapes=[
             pltpu.VMEM((gx * gy, nx * ny, nz), jnp.float32),
-            pltpu.VMEM(padded, jnp.float32),
-            pltpu.VMEM(padded, jnp.float32),
-            pltpu.VMEM((bands, width, height, nz), jnp.float32),
+            pltpu.VMEM(field.shape, jnp.float32),
+            pltpu.VMEM(field.shape, jnp.float32),
+            pltpu.VMEM(laplace.shape, jnp.float32),
         ],
-        compiler_params=pltpu.CompilerParams(vmem_limit_bytes=16 * 1024 * 1024),
+        compiler_params=pltpu.CompilerParams(vmem_limit_bytes=12 * 1024 * 1024),
         name="filter",
-    )(core, own, other, w1, w2)
+    )(core, field, laplace, packed, other, *weights)
 
 
 def margin_kernel(rows, bands, scale, x_ref, out_ref):
@@ -277,40 +325,51 @@
     width = 2 * bands
     lines = lax.broadcasted_iota(jnp.int32, (TILE, width), 0)
     both = [both[t * TILE : (t + 1) * TILE] for t in range(tiles)]
+
+    def spread(t, at):
+        return jnp.broadcast_to(both[t][:, at : at + 1], (TILE, width))
+
+    def line_of(value, at):
+        return jnp.broadcast_to(value[at : at + 1, :], (TILE, width))
+
+    heads = [spread(0, c) for c in range(TILE)]
     for p in range(tiles):
         between(p)
-        spread = [
-            [
-                jnp.broadcast_to(both[t][:, p * TILE + c : p * TILE + c + 1], (TILE, width)) if t >= p else None
-                for t in range(tiles)
-            ]
-            for c in range(TILE)
-        ]
+        here = range(p * TILE, (p + 1) * TILE)
+        panel = [{t: spread(t, at) for t in range(p + 1, tiles)} for at in here]
+        later = [spread(p + 1, at + TILE) for at in here] if p + 1 < tiles else []
+        square = [[line_of(heads[c], d) if d >= c else None for d in range(TILE)] for c in range(TILE)]
         pivots = None
         for j in range(TILE):
-            pivot = jnp.broadcast_to(spread[j][p][j : j + 1, :], (TILE, width))
+            pivot = square[j][j]
             pivots = pivot if j == 0 else jnp.where(lines == j, pivot, pivots)
-            ratio = 1.0 / pivot
-            factor = [spread[j][t] * ratio if t >= p else None for t in range(tiles)]
-            factor[p] = jnp.where(lines > j, factor[p], 0.0)
+            ratio = pl.reciprocal(pivot, approx=True)
             for c in range(j + 1, TILE):
-                entry = jnp.broadcast_to(spread[j][p][c : c + 1, :], (TILE, width))
-                for t in range(p, tiles):
-                    spread[c][t] = spread[c][t] - factor[t] * entry
-            line = jnp.broadcast_to(both[p][j : j + 1, :], (TILE, width))
+                for d in range(c, TILE):
+                    square[c][d] = square[c][d] - (square[j][c] * square[j][d]) * ratio
+            factor = {t: panel[j][t] * ratio for t in range(p + 1, tiles)}
+            factor[p] = jnp.where(lines > j, heads[j] * ratio, 0.0)
+            for c in range(j + 1, TILE):
+                heads[c] = heads[c] - factor[p] * square[j][c]
+                for t in range(p + 1, tiles):
+                    panel[c][t] = panel[c][t] - factor[t] * square[j][c]
+            for c, column in enumerate(later):
+                later[c] = column - factor[p + 1] * line_of(panel[j][p + 1], c)
+            line = line_of(both[p], j)
             for t in range(p, tiles):
                 both[t] = both[t] - factor[t] * line
+        heads = later
         both[p] = both[p] * lax.rsqrt(pivots)
     return jnp.concatenate(both, 0)[:, bands:]
 
 
-def rotate_kernel(dims, place_ref, margins_ref, *refs):
+def rotate_kernel(dims, place_ref, *refs):
     rows, bands, own, pieces, tiles = dims
-    parts = refs[:pieces]
-    out_ref, inv_ref, split_ref = refs[pieces:]
-    folded = margins_ref[0]
-    for term in range(1, margins_ref.shape[0]):
-        folded = folded + margins_ref[term]
+    margins, parts = refs[: pieces // 2], refs[pieces // 2 : -3]
+    out_ref, inv_ref, split_ref = refs[-3:]
+    folded = margins[0][...]
+    for term in margins[1:]:
+        folded = folded + term[...]
     half = bands // 2
     quarters = []
     for at in range(3):
@@ -361,7 +420,7 @@
     return pl.pallas_call(
         functools.partial(rotate_kernel, dims),
         out_shape=jax.ShapeDtypeStruct((own * rows * pieces, nz), jnp.float32),
-        in_specs=[pl.BlockSpec(memory_space=pltpu.SMEM)] + [vmem] * (1 + pieces),
+        in_specs=[pl.BlockSpec(memory_space=pltpu.SMEM)] + [vmem] * (len(margins) + pieces),
         out_specs=vmem,
         scratch_shapes=[
             pltpu.VMEM((bands, bands), jnp.float32),
@@ -369,7 +428,7 @@
         ],
         compiler_params=pltpu.CompilerParams(vmem_limit_bytes=12 * 1024 * 1024),
         name="rotate",
-    )(place, margins, *parts)
+    )(place, *margins, *parts)
 
 
 def on_device_fields(start_bands, potential):
@@ -391,25 +450,30 @@
     packed = jnp.concatenate([fields, jnp.broadcast_to(own_half[None], (grid, half, nz))], 1)
     packed = lax.all_to_all(packed, ("gx", "gy"), 0, 0)
     other = lax.ppermute(packed[:, own * cells :, :], "core", swap)
-    dims = (gx, gy, own, nx, ny, nz, pieces)
-    filtered = apply_filter(core.reshape(1), packed, other, dims)
+    dims = (gx, gy, own, nx, ny, nz, pieces, own * cells)
+    field, laplace, *weights = first_laplace(packed, dims)
+    filtered = apply_filter(core.reshape(1), field, laplace, packed, other, weights, dims)
     blocks = lax.all_to_all(filtered, ("chip", "core", "gx", "gy"), 0, 0).reshape(bands * rows, nz)
 
+    def tied(value, first):
+        return lax.optimization_barrier((value, first))[0]
+
+    def copies(value, axis):
+        count = lax.axis_size(axis)
+        pairs = [[(i, i ^ mask) for i in range(count)] for mask in range(1, count)]
+        return [value] + [lax.ppermute(value, axis, pair) for pair in pairs]
+
     margin = partial_margin(blocks, bands, 1.0 / (cells * nz * grid))
-    margin = margin + lax.ppermute(margin, "core", swap)
-    margins = jnp.broadcast_to(margin[None], (chips * grid,) + margin.shape)
-    margins = lax.all_to_all(margins, ("chip", "gx", "gy"), 0, 0)
-
-    parts, offsets = [blocks], [(core * chips + chip) * rows]
-    for mask in range(1, chips):
-        parts.append(lax.ppermute(blocks, "chip", [(i, i ^ mask) for i in range(chips)]))
-        offsets.append((core * chips + (chip ^ mask)) * rows)
-    for index in range(chips):
-        source = parts[index]
-        if index:
-            source, margins = lax.optimization_barrier((source, margins))
-        parts.append(lax.ppermute(source, "core", swap))
-        offsets.append((1 - core) * chips * rows + offsets[index] - core * chips * rows)
+    parts = copies(tied(blocks, margin), "chip")
+    margin = sum(copies(margin, "core"))
+    crossed = [lax.ppermute(tied(blocks, margin), "core", swap)]
+    for axis in ("gx", "gy"):
+        margin = sum(copies(margin, axis))
+    margins = copies(margin, "chip")
+    crossed += [lax.ppermute(tied(part, margin), "core", swap) for part in parts[1:]]
+    parts += crossed
+    offsets = [(core * chips + (chip ^ mask)) * rows for mask in range(chips)]
+    offsets += [at + (1 - 2 * core) * chips * rows for at in offsets]
     place = jnp.stack([(chip * 2 + core) * own_bands] + offsets).astype(jnp.int32)
     rotated = rotate(place, margins, parts, own_bands, bands)
     return rotated.reshape(start_bands.shape)

time: 66.3 us -> 63.6 us (0.959)
  waiting for transfers between devices: 12.7 us -> 9.85 us
  starting transfers between devices: 4.86 us -> 6.57 us
  Pallas kernels: 7.91 us -> 7.1 us
  local copies, waits for them, and re-layouts: 1.54 us -> 0.84 us
    all_to_all x1 -> x0, waiting for transfers between devices: 8.63 us -> none  [on_device_fields(): margins = lax.all_to_all(margins, ('chip', 'gx', 'gy'), 0, 0)]
    ppermute x4 -> x9, waiting for transfers between devices: 2.78 us -> 9.26 us  [the longest x7 9.25 us: copies(): return [value] + [lax.ppermute(value, axis, pair) for pair in pairs]]
    ppermute x4 -> x9, starting transfers between devices: 0.72 us -> 6.49 us  [the longest x7 6.49 us: copies(): return [value] + [lax.ppermute(value, axis, pair) for pair in pairs]]
    all_to_all x1 -> x0, starting transfers between devices: 4.07 us -> none  [on_device_fields(): margins = lax.all_to_all(margins, ('chip', 'gx', 'gy'), 0, 0)]
    pallas_call x1, Pallas kernels: 3.29 us -> 2.31 us  [apply_filter(): pl.pallas_call(functools.partial(filter_kernel, dims), out_shape=jax.Shap...]
    broadcast_in_dim x1 -> x0, local copies, waits for them, and re-layouts: 0.69 us -> none  [on_device_fields(): margins = jnp.broadcast_to(margin[None], (chips * grid,) + margin.shape)]
    ppermute x1, waiting for transfers between devices: 1.29 us -> 0.59 us  [on_device_fields(): other = lax.ppermute(packed[:, own * cells:, :], 'core', swap)]
    pallas_call x0 -> x1, Pallas kernels: none -> 0.69 us  [first_laplace(): pl.pallas_call(functools.partial(laplace_kernel, dims), out_shape=(jax.Sh...]
  transfers between devices with their start and end apart: 6 -> 10, of which waited for: 4 -> 6; matrix products, arithmetic and copies ran while one was open for 1% -> 0% of each run, Pallas kernels for 1% -> 1%
where the time goes in v3:
time: 63.6 us; the launch traced here: 63.3 us
  blocking collectives  37.9 us (60%)
  waiting for transfers between devices  9.85 us (15%)
  Pallas kernels  7.1 us (11%)
  starting transfers between devices  6.57 us (10%)
  other arithmetic  1.05 us (2%)
  local copies, waits for them, and re-layouts  0.84 us (1%)
    all_to_all x1, blocking collectives, on_device_fields(): packed = lax.all_to_all(packed, ('gx', 'gy'), 0, 0)  20.9 us
    all_to_all x1, blocking collectives, on_device_fields(): lax.all_to_all(filtered, ('chip', 'core', 'gx', 'gy'), 0, 0)  17 us
    ppermute x7, waiting for transfers between devices, copies(): return [value] + [lax.ppermute(value, axis, pair) for pair in pairs]  9.25 us
    ppermute x7, starting transfers between devices, copies(): return [value] + [lax.ppermute(value, axis, pair) for pair in pairs]  6.49 us
    pallas_call x1, Pallas kernels, rotate(): pl.pallas_call(functools.partial(rotate_kernel, dims), out_shape=jax.Shap...  3.58 us
    pallas_call x1, Pallas kernels, apply_filter(): pl.pallas_call(functools.partial(filter_kernel, dims), out_shape=jax.Shap...  2.31 us
  transfers between devices with their start and end apart: 10, of which 6 were waited for; matrix products, arithmetic and copies ran while one was open for 0% of the time, Pallas kernels for 1%

profile of v3, /device:TPU:0, one launch (start us, length us, event | category | flops | bytes accessed | tf_op | source)
XLA Modules:
  0.0 63.3 jit_solution(10139712697227193980)
XLA Ops:
  0.0 0.0 copy-start
  0.0 0.7 %copy-done = f32[6,8,128]{2,1,0:T(8,128)S(1)} copy-done((f32[6,8,128]{2,1,0:T(8,128)S(1)}, f32[6,8,128]{2,1,0:T(8,128)}, u32[]{:S(2)}) %copy-start) | copy-done | bytes 24600
  0.8 1.0 %pad_maximum_fusion = f32[8,120,128]{2,1,0:T(8,128)S(1)} fusion(f32[8,24,128]{2,1,0:T(8,128)S(1)} %broadcast_in_dim.2, f32[8,96,128]{2,1,0:T(8,128)} %bitcast.15), kind=kLoop, calls=%fused_computation | loop fusion | flops 122880 | bytes 983040 | tf_op jit(solution)/shard_map/concatenate | solution.py:450
  1.8 20.9 %all_to_all.10.in_ref.half_ref = f32[8,120,128]{2,1,0:T(8,128)S(1)} all-to-all(f32[8,120,128]{2,1,0:T(8,128)S(1)} %pad_maximum_fusion), channel_id=1, replica_groups=mesh['chip'=2,'core'=2,'gx'=4,'gy'=2] {'gx','gy'}, dimensions={0} | all-to-all | bytes 983040 | tf_op jit(solution)/shard_map/all_to_all | solution.py:451
  22.7 0.1 collective-permute-start
  22.8 0.7 %laplace.1 = (f32[2,24,32,128]{3,2,1,0:T(8,128)S(1)}, f32[2,24,16,128]{3,2,1,0:T(8,128)S(1)}, bf16[256,256]{1,0:T(8,128)(2,1)S(1)}, bf16[256,128]{1,0:T(8,128)(2,1)S(1)}) custom-call(f32[8,120,128]{2,1,0:T(8,128)S(1)} %all_to_all.10.in_ref.half_ref), custom_call_target="tpu_custom_call" | custom-call | flops 4325376 | bytes 1572864 | tf_op jit(solution)/shard_map/laplace/pallas_call | solution.py:249
  23.5 0.6 collective-permute-done.other_ref
  24.1 2.3 %filter.1 = f32[32,24,128]{2,1,0:T(8,128)S(1)} custom-call(s32[1]{0:T(128)} %bitcast.5.core_ref, f32[2,24,32,128]{3,2,1,0:T(8,128)S(1)} %get-tuple-element.12.field_ref, f32[2,24,16,128]{3,2,1,0:T(8,128)S(1)} %get-tuple-element.13.lap_ref, f32[8,120,128]{2,1,0:T(8,128)S(1)} %all_to_all.10.in_ref.half_ref, f32[8,24,128]{2,1,0:T(8,128)S(1)} %collective-permute-done.other_ref, ...), custom_call_target="tpu_custom_call" | custom-call | tf_op jit(solution)/shard_map/filter/pallas_call | solution.py:268
  26.4 17.0 %all_to_all.11 = f32[32,24,128]{2,1,0:T(8,128)S(1)} all-to-all(f32[32,24,128]{2,1,0:T(8,128)S(1)} %filter.1), channel_id=1, replica_groups=mesh['chip'=2,'core'=2,'gx'=4,'gy'=2] {'chip','core','gx','gy'}, dimensions={0} | all-to-all | bytes 786432 | tf_op jit(solution)/shard_map/all_to_all | solution.py:456
  43.3 0.5 margin.1
  43.9 0.6 collective-permute-start.7
  44.5 0.0 collective-permute-start.1
  44.5 1.1 %collective-permute-done.1 = f32[24,128]{1,0:T(8,128)S(1)} collective-permute-done((f32[24,128]{1,0:T(8,128)S(1)}, f32[24,128]{1,0:T(8,128)S(1)}, u32[]{:S(2)}, u32[]{:S(2)}) %collective-permute-start.1) | collective-permute-done | bytes 12320 | tf_op jit(solution)/shard_map/ppermute | solution.py:464
  45.7 1.9 %collective-permute-start.4 = (f32[24,128]{1,0:T(8,128)S(1)}, f32[24,128]{1,0:T(8,128)S(1)}, u32[]{:S(2)}, u32[]{:S(2)}) collective-permute-start(f32[24,128]{1,0:T(8,128)S(1)} %add.39), channel_id=1, source_target_pairs={{0,6},{2,4},{4,2},{6,0},{1,7},{3,5},{5,3},{7,1},{8,14},{10,12},{12... | collective-permute-start | bytes 36872 | tf_op jit(solution)/shard_map/ppermute | solution.py:464
  47.6 0.3 collective-permute-start.3
  47.9 2.1 %collective-permute-start.2 = (f32[24,128]{1,0:T(8,128)S(1)}, f32[24,128]{1,0:T(8,128)S(1)}, u32[]{:S(2)}, u32[]{:S(2)}) collective-permute-start(f32[24,128]{1,0:T(8,128)S(1)} %add.39), channel_id=1, source_target_pairs={{0,2},{2,0},{4,6},{6,4},{1,3},{3,1},{5,7},{7,5},{8,10},{10,8},{12,... | collective-permute-start | bytes 36872 | tf_op jit(solution)/shard_map/ppermute | solution.py:464
  50.1 1.2 %collective-permute-done.4 = f32[24,128]{1,0:T(8,128)S(1)} collective-permute-done((f32[24,128]{1,0:T(8,128)S(1)}, f32[24,128]{1,0:T(8,128)S(1)}, u32[]{:S(2)}, u32[]{:S(2)}) %collective-permute-start.4) | collective-permute-done | bytes 12320 | tf_op jit(solution)/shard_map/ppermute | solution.py:464
  51.2 1.0 %collective-permute-done.3 = f32[24,128]{1,0:T(8,128)S(1)} collective-permute-done((f32[24,128]{1,0:T(8,128)S(1)}, f32[24,128]{1,0:T(8,128)S(1)}, u32[]{:S(2)}, u32[]{:S(2)}) %collective-permute-start.3) | collective-permute-done | bytes 12320 | tf_op jit(solution)/shard_map/ppermute | solution.py:464
  52.2 0.0 collective-permute-done.2
  52.2 0.4 collective-permute-start.5
  52.6 0.0 collective-permute-start.8
  52.6 3.3 %collective-permute-done.5 = f32[24,128]{1,0:T(8,128)S(1)} collective-permute-done((f32[24,128]{1,0:T(8,128)S(1)}, f32[24,128]{1,0:T(8,128)S(1)}, u32[]{:S(2)}, u32[]{:S(2)}) %collective-permute-start.5) | collective-permute-done | bytes 12320 | tf_op jit(solution)/shard_map/ppermute | solution.py:464
  56.0 0.0 collective-permute-done.7.refs_3_
  56.0 0.0 collective-permute-start.9
  56.0 1.0 %collective-permute-start.6 = (f32[24,128]{1,0:T(8,128)S(1)}, f32[24,128]{1,0:T(8,128)S(1)}, u32[]{:S(2)}, u32[]{:S(2)}) collective-permute-start(f32[24,128]{1,0:T(8,128)S(1)} %add.43.refs_0_), channel_id=1, source_target_pairs={{0,16},{16,0},{1,17},{17,1},{2,18},{18,2},{3,19},{19,3},{4,20},{20... | collective-permute-start | bytes 36872 | tf_op jit(solution)/shard_map/ppermute | solution.py:464
  57.0 0.1 stack.23.place_ref
  57.1 2.7 %collective-permute-done.6.refs_1_ = f32[24,128]{1,0:T(8,128)S(1)} collective-permute-done((f32[24,128]{1,0:T(8,128)S(1)}, f32[24,128]{1,0:T(8,128)S(1)}, u32[]{:S(2)}, u32[]{:S(2)}) %collective-permute-start.6) | collective-permute-done | bytes 12320 | tf_op jit(solution)/shard_map/ppermute | solution.py:464
  59.7 0.0 collective-permute-done.8.refs_4_
  59.7 0.0 collective-permute-done.9.refs_5_
  59.7 3.6 %rotate.1 = f32[768,128]{1,0:T(8,128)} custom-call(s32[5]{0:T(128)S(1)} %stack.23.place_ref, f32[24,128]{1,0:T(8,128)S(1)} %add.43.refs_0_, f32[24,128]{1,0:T(8,128)S(1)} %collective-permute-done.6.refs_1_, f32[768,128]{1,0:T(8,128)S(1)} %bitcast.14, f32[768,128]{1,0:T(8,128)S(1)} %collective-permute-done.7.refs_3_, ...), custom_call_target="tpu_custom_call" | custom-call | tf_op jit(solution)/shard_map/rotate/pallas_call | solution.py:420
  (6 shorter events, 0.0 us)
Async XLA Ops:
  0.0 0.7 %copy-start = (f32[6,8,128]{2,1,0:T(8,128)S(1)}, f32[6,8,128]{2,1,0:T(8,128)}, u32[]{:S(2)}) copy-start(f32[6,8,128]{2,1,0:T(8,128)} %param.3) | copy-start | bytes 73732
  22.7 1.4 %collective-permute-start = (f32[8,24,128]{2,1,0:T(8,128)S(1)}, f32[8,24,128]{2,1,0:T(8,128)S(1)}, u32[]{:S(2)}, u32[]{:S(2)}) collective-permute-start(f32[8,24,128]{2,1,0:T(8,128)S(1)} %slice.4), channel_id=1, source_target_pairs={{0,8},{8,0},{1,9},{9,1},{2,10},{10,2},{3,11},{11,3},{4,12},{12,4},... | collective-permute-start | bytes 294920 | tf_op jit(solution)/shard_map/ppermute | solution.py:452
  43.9 12.1 %collective-permute-start.7 = (f32[768,128]{1,0:T(8,128)S(1)}, f32[768,128]{1,0:T(8,128)S(1)}, u32[]{:S(2)}, u32[]{:S(2)}) collective-permute-start(f32[768,128]{1,0:T(8,128)S(1)} %bitcast.12), channel_id=1, source_target_pairs={{0,16},{16,0},{1,17},{17,1},{2,18},{18,2},{3,19},{19,3},{4,20},{20... | collective-permute-start | bytes 1179656 | tf_op jit(solution)/shard_map/ppermute | solution.py:464
  44.5 1.2 %collective-permute-start.1 = (f32[24,128]{1,0:T(8,128)S(1)}, f32[24,128]{1,0:T(8,128)S(1)}, u32[]{:S(2)}, u32[]{:S(2)}) collective-permute-start(f32[24,128]{1,0:T(8,128)S(1)} %margin.1), channel_id=1, source_target_pairs={{0,8},{8,0},{1,9},{9,1},{2,10},{10,2},{3,11},{11,3},{4,12},{12,4},... | collective-permute-start | bytes 36872 | tf_op jit(solution)/shard_map/ppermute | solution.py:464
  45.7 5.6 %collective-permute-start.4 = (f32[24,128]{1,0:T(8,128)S(1)}, f32[24,128]{1,0:T(8,128)S(1)}, u32[]{:S(2)}, u32[]{:S(2)}) collective-permute-start(f32[24,128]{1,0:T(8,128)S(1)} %add.39), channel_id=1, source_target_pairs={{0,6},{2,4},{4,2},{6,0},{1,7},{3,5},{5,3},{7,1},{8,14},{10,12},{12... | collective-permute-start | bytes 36872 | tf_op jit(solution)/shard_map/ppermute | solution.py:464
  47.6 4.6 %collective-permute-start.3 = (f32[24,128]{1,0:T(8,128)S(1)}, f32[24,128]{1,0:T(8,128)S(1)}, u32[]{:S(2)}, u32[]{:S(2)}) collective-permute-start(f32[24,128]{1,0:T(8,128)S(1)} %add.39), channel_id=1, source_target_pairs={{0,4},{2,6},{4,0},{6,2},{1,5},{3,7},{5,1},{7,3},{8,12},{10,14},{12... | collective-permute-start | bytes 36872 | tf_op jit(solution)/shard_map/ppermute | solution.py:464
  47.9 4.3 %collective-permute-start.2 = (f32[24,128]{1,0:T(8,128)S(1)}, f32[24,128]{1,0:T(8,128)S(1)}, u32[]{:S(2)}, u32[]{:S(2)}) collective-permute-start(f32[24,128]{1,0:T(8,128)S(1)} %add.39), channel_id=1, source_target_pairs={{0,2},{2,0},{4,6},{6,4},{1,3},{3,1},{5,7},{7,5},{8,10},{10,8},{12,... | collective-permute-start | bytes 36872 | tf_op jit(solution)/shard_map/ppermute | solution.py:464
  52.2 3.8 %collective-permute-start.5 = (f32[24,128]{1,0:T(8,128)S(1)}, f32[24,128]{1,0:T(8,128)S(1)}, u32[]{:S(2)}, u32[]{:S(2)}) collective-permute-start(f32[24,128]{1,0:T(8,128)S(1)} %add_add_fusion), channel_id=1, source_target_pairs={{0,1},{1,0},{2,3},{3,2},{4,5},{5,4},{6,7},{7,6},{8,9},{9,8},{10,11... | collective-permute-start | bytes 36872 | tf_op jit(solution)/shard_map/ppermute | solution.py:464
  52.6 7.1 %collective-permute-start.8 = (f32[768,128]{1,0:T(8,128)S(1)}, f32[768,128]{1,0:T(8,128)S(1)}, u32[]{:S(2)}, u32[]{:S(2)}) collective-permute-start(f32[768,128]{1,0:T(8,128)S(1)} %bitcast.13), channel_id=1, source_target_pairs={{0,8},{8,0},{1,9},{9,1},{2,10},{10,2},{3,11},{11,3},{4,12},{12,4},... | collective-permute-start | bytes 1179656 | tf_op jit(solution)/shard_map/ppermute | solution.py:469
  56.0 3.8 %collective-permute-start.9 = (f32[768,128]{1,0:T(8,128)S(1)}, f32[768,128]{1,0:T(8,128)S(1)}, u32[]{:S(2)}, u32[]{:S(2)}) collective-permute-start(f32[768,128]{1,0:T(8,128)S(1)} %collective-permute-done.7.refs_3_), channel_id=1, source_target_pairs={{0,8},{8,0},{1,9},{9,1},{2,10},{10,2},{3,11},{11,3},{4,12},{12,4},... | collective-permute-start | bytes 1179656 | tf_op jit(solution)/shard_map/ppermute | solution.py:473
  56.0 3.8 %collective-permute-start.6 = (f32[24,128]{1,0:T(8,128)S(1)}, f32[24,128]{1,0:T(8,128)S(1)}, u32[]{:S(2)}, u32[]{:S(2)}) collective-permute-start(f32[24,128]{1,0:T(8,128)S(1)} %add.43.refs_0_), channel_id=1, source_target_pairs={{0,16},{16,0},{1,17},{17,1},{2,18},{18,2},{3,19},{19,3},{4,20},{20... | collective-permute-start | bytes 36872 | tf_op jit(solution)/shard_map/ppermute | solution.py:464

commit v4 on v3

--- a/solution.py
+++ b/solution.py
@@ -1,4 +1,5 @@
 import functools
+import math
 
 import jax
 import jax.numpy as jnp
@@ -189,7 +190,7 @@
                 lap_ref[k, x, rows, :] = add_xy(field_ref, k, x, tile, lap_ref[k, x, rows, :])
 
 
-def filter_kernel(dims, core_ref, field_ref, lap_ref, half_ref, other_ref, w1_ref, w2_ref, out_ref, pot, buf_a, buf_b, zbuf):
+def filter_kernel(dims, field_ref, lap_ref, half_ref, other_ref, w1_ref, w2_ref, out_ref, pot, buf_a, buf_b, zbuf):
     gx, gy, own, nx, ny, nz, pieces, skip = dims
     width, height, cells = gx * nx, gy * ny, nx * ny
     half = cells // 2
@@ -197,7 +198,7 @@
     middle, first, others = filter_weights(DEGREE)
     shift = -middle - 1.5 * COEFFS[0]
 
-    core = core_ref[0]
+    core = lax.axis_index("core")
     for g in range(gx * gy):
         mine = pl.ds(pl.multiple_of(core * half, TILE), half)
         theirs = pl.ds(pl.multiple_of((1 - core) * half, TILE), half)
@@ -262,13 +263,13 @@
     )(packed)
 
 
-def apply_filter(core, field, laplace, packed, other, weights, dims):
+def apply_filter(field, laplace, packed, other, weights, dims):
     gx, gy, bands, nx, ny, nz, pieces, skip = dims
     vmem = pl.BlockSpec(memory_space=pltpu.VMEM)
     return pl.pallas_call(
         functools.partial(filter_kernel, dims),
         out_shape=jax.ShapeDtypeStruct((pieces * gx * gy, bands * nx * ny // pieces, nz), jnp.float32),
-        in_specs=[pl.BlockSpec(memory_space=pltpu.SMEM)] + [vmem] * 6,
+        in_specs=[vmem] * 6,
         out_specs=vmem,
         scratch_shapes=[
             pltpu.VMEM((gx * gy, nx * ny, nz), jnp.float32),
@@ -278,7 +279,7 @@
         ],
         compiler_params=pltpu.CompilerParams(vmem_limit_bytes=12 * 1024 * 1024),
         name="filter",
-    )(core, field, laplace, packed, other, *weights)
+    )(field, laplace, packed, other, *weights)
 
 
 def margin_kernel(rows, bands, scale, x_ref, out_ref):
@@ -297,18 +298,15 @@
 
     small = block(0, 2) + block(2, 0) + block(1, 1)
     total = (small + (block(0, 1) + block(1, 0)) + block(0, 0)) * scale
-    half = bands // 2
-    for at, (i, j) in enumerate(((0, 0), (1, 0), (1, 1))):
-        part = total[i * half : (i + 1) * half, j * half : (j + 1) * half]
-        folds = [part[t * TILE : (t + 1) * TILE] for t in range(half // TILE)]
-        out_ref[pl.ds(at * TILE, TILE), :] = jnp.concatenate(folds, 1)
+    out_ref[:, pl.ds(0, bands)] = total[: bands // 2]
+    out_ref[:, pl.ds(bands, bands)] = total[bands // 2 :]
 
 
 def partial_margin(blocks, bands, scale):
     rows = blocks.shape[0] // bands
     return pl.pallas_call(
         functools.partial(margin_kernel, rows, bands, scale),
-        out_shape=jax.ShapeDtypeStruct((3 * TILE, bands // 2 * (bands // 2) // TILE), jnp.float32),
+        out_shape=jax.ShapeDtypeStruct((bands // 2, 2 * bands), jnp.float32),
         in_specs=[pl.BlockSpec(memory_space=pltpu.VMEM)],
         out_specs=pl.BlockSpec(memory_space=pltpu.VMEM),
         compiler_params=pltpu.CompilerParams(vmem_limit_bytes=8 * 1024 * 1024),
@@ -316,25 +314,28 @@
     )(blocks)
 
 
-def eliminate(margin, between):
-    bands = margin.shape[0]
+def eliminate(folded):
+    bands = folded.shape[1] // 2
     tiles = bands // TILE
-    row_at = lax.broadcasted_iota(jnp.int32, (bands, bands), 0)
-    col_at = lax.broadcasted_iota(jnp.int32, (bands, bands), 1)
-    both = jnp.concatenate([margin, jnp.where(row_at == col_at, 1.0, 0.0)], 1)
     width = 2 * bands
     lines = lax.broadcasted_iota(jnp.int32, (TILE, width), 0)
-    both = [both[t * TILE : (t + 1) * TILE] for t in range(tiles)]
+    lanes = lax.broadcasted_iota(jnp.int32, (TILE, width), 1)
+    swapped = jnp.concatenate([folded[:, bands:], folded[:, :bands]], 1)
+    both = []
+    for t in range(tiles):
+        at = t * TILE % (bands // 2)
+        right = (swapped if t < tiles // 2 else folded)[at : at + TILE]
+        eye = jnp.where(lines + t * TILE == lanes % bands, 1.0, 0.0)
+        both.append([eye, jnp.where(lanes < bands, eye, right)])
 
     def spread(t, at):
-        return jnp.broadcast_to(both[t][:, at : at + 1], (TILE, width))
+        return jnp.broadcast_to(both[t][1][:, bands + at : bands + at + 1], (TILE, width))
 
     def line_of(value, at):
         return jnp.broadcast_to(value[at : at + 1, :], (TILE, width))
 
     heads = [spread(0, c) for c in range(TILE)]
     for p in range(tiles):
-        between(p)
         here = range(p * TILE, (p + 1) * TILE)
         panel = [{t: spread(t, at) for t in range(p + 1, tiles)} for at in here]
         later = [spread(p + 1, at + TILE) for at in here] if p + 1 < tiles else []
@@ -355,80 +356,90 @@
                     panel[c][t] = panel[c][t] - factor[t] * square[j][c]
             for c, column in enumerate(later):
                 later[c] = column - factor[p + 1] * line_of(panel[j][p + 1], c)
-            line = line_of(both[p], j)
+            pair = [line_of(value, j) for value in both[p]]
             for t in range(p, tiles):
-                both[t] = both[t] - factor[t] * line
+                both[t] = [value - factor[t] * line for value, line in zip(both[t], pair)]
         heads = later
-        both[p] = both[p] * lax.rsqrt(pivots)
-    return jnp.concatenate(both, 0)[:, bands:]
-
-
-def rotate_kernel(dims, place_ref, *refs):
-    rows, bands, own, pieces, tiles = dims
-    margins, parts = refs[: pieces // 2], refs[pieces // 2 : -3]
-    out_ref, inv_ref, split_ref = refs[-3:]
+        scale = lax.rsqrt(pivots)
+        both[p] = [value * scale for value in both[p]]
+    return [jnp.concatenate(value, 1) for value in both]
+
+
+def split_pair(split_ref, at, part, pair, bands):
+    rows = part.shape[0] // bands
+    nz = part.shape[1]
+    for i in range(2):
+        terms = split3(part[pl.ds(2 * pair + i, bands, stride=rows), :])
+        for j, term in enumerate(terms):
+            split_ref[at, pl.ds(j * bands, bands), pl.ds(i * nz, nz)] = term
+
+
+def inverse_kernel(dims, *refs):
+    bands, own = dims
+    margins, left_ref, inv_ref = refs[:-2], refs[-2], refs[-1]
     folded = margins[0][...]
     for term in margins[1:]:
         folded = folded + term[...]
-    half = bands // 2
-    quarters = []
-    for at in range(3):
-        part = folded[at * TILE : (at + 1) * TILE]
-        quarters.append(jnp.concatenate([part[:, t * half : (t + 1) * half] for t in range(half // TILE)], 0))
-    low, cross, high = quarters
-    margin = jnp.concatenate(
-        [jnp.concatenate([low, cross.T], 1), jnp.concatenate([cross, high], 1)], 0
-    )
-    jobs = [(part, r) for part in range(pieces) for r in range(rows)]
-    nz = parts[0].shape[1]
-
-    def split_some(step):
-        share = -(-len(jobs) // tiles)
-        for at in range(step * share, min(len(jobs), (step + 1) * share)):
-            part, r = jobs[at]
-            terms_of = split3(parts[part][pl.ds(r, bands, stride=rows), :])
-            for i, term in enumerate(terms_of):
-                split_ref[at // 2, pl.ds(i * bands, bands), pl.ds((at % 2) * nz, nz)] = term
-
-    inv_ref[...] = eliminate(margin, split_some)
-    first = pl.multiple_of(place_ref[0], TILE)
-    high, mid, low = split3(inv_ref[pl.ds(first, own), :])
-    zero = jnp.zeros_like(high)
-    left = jnp.concatenate(
-        [
-            jnp.concatenate([high, high, high], 1),
-            jnp.concatenate([mid, mid, zero], 1),
-            jnp.concatenate([low, zero, zero], 1),
-        ],
-        0,
-    )
-    for pair in range(len(jobs) // 2):
-        product = jnp.dot(left, split_ref[pair], preferred_element_type=jnp.float32)
-        value = product[:own] + (product[own : 2 * own] + product[2 * own :])
-        for i in range(2):
-            part, r = jobs[2 * pair + i]
-            start = place_ref[1 + part] + r
-            out_ref[pl.ds(start, own, stride=rows * pieces), :] = value[:, i * nz : (i + 1) * nz]
-
-
-def rotate(place, margins, parts, own, bands):
-    pieces = len(parts)
+    for t, value in enumerate(eliminate(folded)):
+        inv_ref[pl.ds(t * TILE, TILE), :] = value
+    first = pl.multiple_of((lax.axis_index("chip") * 2 + lax.axis_index("core")) * own, TILE)
+    rows = inv_ref[pl.ds(first, own), pl.ds(0, 3 * bands)]
+    lanes = lax.broadcasted_iota(jnp.int32, rows.shape, 1)
+    high = rows.astype(jnp.bfloat16)
+    rest = rows - high.astype(jnp.float32)
+    mid = rest.astype(jnp.bfloat16)
+    low = rest - mid.astype(jnp.float32)
+    left_ref[pl.ds(0, own), :] = high
+    left_ref[pl.ds(own, own), :] = jnp.where(lanes < 2 * bands, rest, 0.0).astype(jnp.bfloat16)
+    left_ref[pl.ds(2 * own, own), :] = jnp.where(lanes < bands, low, 0.0).astype(jnp.bfloat16)
+
+
+def inverse_rows(margins, own, bands):
+    vmem = pl.BlockSpec(memory_space=pltpu.VMEM)
+    return pl.pallas_call(
+        functools.partial(inverse_kernel, (bands, own)),
+        out_shape=jax.ShapeDtypeStruct((3 * own, 3 * bands), jnp.bfloat16),
+        in_specs=[vmem] * len(margins),
+        out_specs=vmem,
+        scratch_shapes=[pltpu.VMEM((bands, 4 * bands), jnp.float32)],
+        compiler_params=pltpu.CompilerParams(vmem_limit_bytes=4 * 1024 * 1024),
+        name="inverse",
+    )(*margins)
+
+
+def rotate_kernel(dims, left_ref, *refs):
+    bands, own = dims
+    parts, out_ref = refs[:-1], refs[-1]
     rows = parts[0].shape[0] // bands
     nz = parts[0].shape[1]
+    left = left_ref[...]
+    chips = len(parts) // 2
+    chip, core = lax.axis_index("chip"), lax.axis_index("core")
+    for index, part in enumerate(parts):
+        piece = (core ^ (index // chips)) * chips + (chip ^ (index % chips))
+        for r in range(0, rows, 2):
+            terms = [split3(part[pl.ds(r + i, bands, stride=rows), :]) for i in range(2)]
+            block = jnp.concatenate([jnp.concatenate(term, 1) for term in zip(*terms)], 0)
+            product = jnp.dot(left, block, preferred_element_type=jnp.float32)
+            value = product[:own] + (product[own : 2 * own] + product[2 * own :])
+            for i in range(2):
+                start = piece * rows + r + i
+                out_ref[pl.ds(start, own, stride=rows * len(parts)), :] = value[:, i * nz : (i + 1) * nz]
+
+
+def rotate(left, parts, bands):
+    rows = parts[0].shape[0] // bands
+    own = left.shape[0] // 3
+    nz = parts[0].shape[1]
     vmem = pl.BlockSpec(memory_space=pltpu.VMEM)
-    dims = (rows, bands, own, pieces, bands // TILE)
     return pl.pallas_call(
-        functools.partial(rotate_kernel, dims),
-        out_shape=jax.ShapeDtypeStruct((own * rows * pieces, nz), jnp.float32),
-        in_specs=[pl.BlockSpec(memory_space=pltpu.SMEM)] + [vmem] * (len(margins) + pieces),
+        functools.partial(rotate_kernel, (bands, own)),
+        out_shape=jax.ShapeDtypeStruct((own * rows * len(parts), nz), jnp.float32),
+        in_specs=[vmem] * (1 + len(parts)),
         out_specs=vmem,
-        scratch_shapes=[
-            pltpu.VMEM((bands, bands), jnp.float32),
-            pltpu.VMEM((rows * pieces // 2, 3 * bands, 2 * nz), jnp.bfloat16),
-        ],
-        compiler_params=pltpu.CompilerParams(vmem_limit_bytes=12 * 1024 * 1024),
+        compiler_params=pltpu.CompilerParams(vmem_limit_bytes=6 * 1024 * 1024),
         name="rotate",
-    )(place, *margins, *parts)
+    )(left, *parts)
 
 
 def on_device_fields(start_bands, potential):
@@ -440,7 +451,7 @@
     cells = nx * ny
     bands = own_bands * pieces
     rows = cells // pieces
-    chip, core = lax.axis_index("chip"), lax.axis_index("core")
+    core = lax.axis_index("core")
     swap = [(0, 1), (1, 0)]
 
     fields = start_bands.reshape(grid, own * cells, nz)
@@ -452,30 +463,27 @@
     other = lax.ppermute(packed[:, own * cells :, :], "core", swap)
     dims = (gx, gy, own, nx, ny, nz, pieces, own * cells)
     field, laplace, *weights = first_laplace(packed, dims)
-    filtered = apply_filter(core.reshape(1), field, laplace, packed, other, weights, dims)
+    filtered = apply_filter(field, laplace, packed, other, weights, dims)
     blocks = lax.all_to_all(filtered, ("chip", "core", "gx", "gy"), 0, 0).reshape(bands * rows, nz)
 
     def tied(value, first):
         return lax.optimization_barrier((value, first))[0]
 
-    def copies(value, axis):
-        count = lax.axis_size(axis)
+    def copies(value, *axes):
+        count = math.prod(lax.axis_size(axis) for axis in axes)
         pairs = [[(i, i ^ mask) for i in range(count)] for mask in range(1, count)]
-        return [value] + [lax.ppermute(value, axis, pair) for pair in pairs]
+        return [value] + [lax.ppermute(value, axes, pair) for pair in pairs]
 
     margin = partial_margin(blocks, bands, 1.0 / (cells * nz * grid))
+    margin = sum(copies(margin, "chip", "core"))
     parts = copies(tied(blocks, margin), "chip")
-    margin = sum(copies(margin, "core"))
     crossed = [lax.ppermute(tied(blocks, margin), "core", swap)]
-    for axis in ("gx", "gy"):
-        margin = sum(copies(margin, axis))
-    margins = copies(margin, "chip")
-    crossed += [lax.ppermute(tied(part, margin), "core", swap) for part in parts[1:]]
-    parts += crossed
-    offsets = [(core * chips + (chip ^ mask)) * rows for mask in range(chips)]
-    offsets += [at + (1 - 2 * core) * chips * rows for at in offsets]
-    place = jnp.stack([(chip * 2 + core) * own_bands] + offsets).astype(jnp.int32)
-    rotated = rotate(place, margins, parts, own_bands, bands)
+    margin = sum(copies(margin, "gx"))
+    margins = copies(margin, "gy")
+    far, margins = lax.optimization_barrier((parts[1:], margins))
+    parts += crossed + [lax.ppermute(part, "core", swap) for part in far]
+    left = inverse_rows(margins, own_bands, bands)
+    rotated = rotate(left, parts, bands)
     return rotated.reshape(start_bands.shape)
 
 
@@ -494,9 +502,10 @@
         and power_of_two(pieces)
         and ny % TILE == 0
         and nz % 128 == 0
-        and bands // 2 * (bands // 2) // TILE % 128 == 0
+        and bands % 64 == 0
         and cells % (2 * TILE) == 0
         and cells % (pieces * TILE // 2) == 0
+        and pieces > 2
         and (own_bands // (gx * gy)) * (cells // pieces) % TILE == 0
         and shape[1] > 2 * REACH
     )

time: 63.6 us -> 62.4 us (0.981)
  waiting for transfers between devices: 9.85 us -> 7.93 us
  starting transfers between devices: 6.57 us -> 8.29 us
  Pallas kernels: 7.1 us -> 6.24 us
    ppermute x8 -> x9, waiting for transfers between devices: 9.26 us -> 7.32 us  [the longest x8 7.07 us: copies(): return [value] + [lax.ppermute(value, axes, pair) for pair in pairs]]
    ppermute x8 -> x9, starting transfers between devices: 6.49 us -> 8.21 us  [the longest x8 8.21 us: copies(): return [value] + [lax.ppermute(value, axes, pair) for pair in pairs]]
    pallas_call x1 -> x2, Pallas kernels: 3.58 us -> 2.68 us  [the longest x1 1.46 us: inverse_rows(): pl.pallas_call(functools.partial(inverse_kernel, (bands, own)), out_shape...]
  transfers between devices with their start and end apart: 10 -> 11, of which waited for: 6 -> 8; matrix products, arithmetic and copies ran while one was open for 0% -> 0% of each run, Pallas kernels for 1% -> 3%
where the time goes in v4:
time: 62.4 us; the launch traced here: 62.2 us
  blocking collectives  37.9 us (61%)
  starting transfers between devices  8.29 us (13%)
  waiting for transfers between devices  7.93 us (13%)
  Pallas kernels  6.24 us (10%)
  other arithmetic  1.05 us (2%)
  local copies, waits for them, and re-layouts  0.76 us (1%)
    all_to_all x1, blocking collectives, on_device_fields(): packed = lax.all_to_all(packed, ('gx', 'gy'), 0, 0)  20.9 us
    all_to_all x1, blocking collectives, on_device_fields(): lax.all_to_all(filtered, ('chip', 'core', 'gx', 'gy'), 0, 0)  17 us
    ppermute x8, starting transfers between devices, copies(): return [value] + [lax.ppermute(value, axes, pair) for pair in pairs]  8.21 us
    ppermute x8, waiting for transfers between devices, copies(): return [value] + [lax.ppermute(value, axes, pair) for pair in pairs]  7.07 us
    pallas_call x1, Pallas kernels, apply_filter(): pl.pallas_call(functools.partial(filter_kernel, dims), out_shape=jax.Shap...  2.35 us
    pallas_call x1, Pallas kernels, inverse_rows(): pl.pallas_call(functools.partial(inverse_kernel, (bands, own)), out_shape...  1.46 us
  transfers between devices with their start and end apart: 11, of which 8 were waited for; matrix products, arithmetic and copies ran while one was open for 0% of the time, Pallas kernels for 3%

profile of v4, /device:TPU:0, one launch (start us, length us, event | category | flops | bytes accessed | tf_op | source)
XLA Modules:
  0.0 62.2 jit_solution(7566338504018667720)
XLA Ops:
  0.0 0.0 copy-start
  0.0 0.7 %copy-done = f32[6,8,128]{2,1,0:T(8,128)S(1)} copy-done((f32[6,8,128]{2,1,0:T(8,128)S(1)}, f32[6,8,128]{2,1,0:T(8,128)}, u32[]{:S(2)}) %copy-start) | copy-done | bytes 24600
  0.8 1.0 %pad_maximum_fusion = f32[8,120,128]{2,1,0:T(8,128)S(1)} fusion(f32[8,24,128]{2,1,0:T(8,128)S(1)} %broadcast_in_dim.2, f32[8,96,128]{2,1,0:T(8,128)} %bitcast.9), kind=kLoop, calls=%fused_computation | loop fusion | flops 122880 | bytes 983040 | tf_op jit(solution)/shard_map/concatenate | solution.py:461
  1.8 20.9 %all_to_all.10.in_ref.half_ref = f32[8,120,128]{2,1,0:T(8,128)S(1)} all-to-all(f32[8,120,128]{2,1,0:T(8,128)S(1)} %pad_maximum_fusion), channel_id=1, replica_groups=mesh['chip'=2,'core'=2,'gx'=4,'gy'=2] {'gx','gy'}, dimensions={0} | all-to-all | bytes 983040 | tf_op jit(solution)/shard_map/all_to_all | solution.py:462
  22.7 0.1 collective-permute-start
  22.8 0.7 %laplace.1 = (f32[2,24,32,128]{3,2,1,0:T(8,128)S(1)}, f32[2,24,16,128]{3,2,1,0:T(8,128)S(1)}, bf16[256,256]{1,0:T(8,128)(2,1)S(1)}, bf16[256,128]{1,0:T(8,128)(2,1)S(1)}) custom-call(f32[8,120,128]{2,1,0:T(8,128)S(1)} %all_to_all.10.in_ref.half_ref), custom_call_target="tpu_custom_call" | custom-call | flops 4325376 | bytes 1572864 | tf_op jit(solution)/shard_map/laplace/pallas_call | solution.py:250
  23.5 0.6 collective-permute-done.other_ref
  24.1 2.4 %filter.1 = f32[32,24,128]{2,1,0:T(8,128)S(1)} custom-call(f32[2,24,32,128]{3,2,1,0:T(8,128)S(1)} %get-tuple-element.13.field_ref, f32[2,24,16,128]{3,2,1,0:T(8,128)S(1)} %get-tuple-element.14.lap_ref, f32[8,120,128]{2,1,0:T(8,128)S(1)} %all_to_all.10.in_ref.half_ref, f32[8,24,128]{2,1,0:T(8,128)S(1)} %collective-permute-done.other_ref, ...), custom_call_target="tpu_custom_call" | custom-call | tf_op jit(solution)/shard_map/filter/pallas_call | solution.py:269
  26.4 17.0 %all_to_all.11 = f32[32,24,128]{2,1,0:T(8,128)S(1)} all-to-all(f32[32,24,128]{2,1,0:T(8,128)S(1)} %filter.1), channel_id=1, replica_groups=mesh['chip'=2,'core'=2,'gx'=4,'gy'=2] {'chip','core','gx','gy'}, dimensions={0} | all-to-all | bytes 786432 | tf_op jit(solution)/shard_map/all_to_all | solution.py:467
  43.4 0.5 margin.1
  43.9 0.5 collective-permute-start.3
  44.4 0.8 %collective-permute-start.2 = (f32[32,128]{1,0:T(8,128)S(1)}, f32[32,128]{1,0:T(8,128)S(1)}, u32[]{:S(2)}, u32[]{:S(2)}) collective-permute-start(f32[32,128]{1,0:T(8,128)S(1)} %margin.1), channel_id=1, source_target_pairs={{0,16},{8,24},{16,0},{24,8},{1,17},{9,25},{17,1},{25,9},{2,18},{10... | collective-permute-start | bytes 49160 | tf_op jit(solution)/shard_map/ppermute | solution.py:475
  45.2 0.6 collective-permute-start.1
  45.8 1.3 %collective-permute-done.3 = f32[32,128]{1,0:T(8,128)S(1)} collective-permute-done((f32[32,128]{1,0:T(8,128)S(1)}, f32[32,128]{1,0:T(8,128)S(1)}, u32[]{:S(2)}, u32[]{:S(2)}) %collective-permute-start.3) | collective-permute-done | bytes 16416 | tf_op jit(solution)/shard_map/ppermute | solution.py:475
  47.1 1.0 %collective-permute-done.2 = f32[32,128]{1,0:T(8,128)S(1)} collective-permute-done((f32[32,128]{1,0:T(8,128)S(1)}, f32[32,128]{1,0:T(8,128)S(1)}, u32[]{:S(2)}, u32[]{:S(2)}) %collective-permute-start.2) | collective-permute-done | bytes 16416 | tf_op jit(solution)/shard_map/ppermute | solution.py:475
  48.1 0.0 collective-permute-done.1
  48.1 0.9 %collective-permute-start.4 = (f32[768,128]{1,0:T(8,128)S(1)}, f32[768,128]{1,0:T(8,128)S(1)}, u32[]{:S(2)}, u32[]{:S(2)}) collective-permute-start(f32[768,128]{1,0:T(8,128)S(1)} %bitcast.6), channel_id=1, source_target_pairs={{0,16},{16,0},{1,17},{17,1},{2,18},{18,2},{3,19},{19,3},{4,20},{20... | collective-permute-start | bytes 1179656 | tf_op jit(solution)/shard_map/ppermute | solution.py:475
  49.1 1.4 %collective-permute-start.7 = (f32[32,128]{1,0:T(8,128)S(1)}, f32[32,128]{1,0:T(8,128)S(1)}, u32[]{:S(2)}, u32[]{:S(2)}) collective-permute-start(f32[32,128]{1,0:T(8,128)S(1)} %add_add_fusion.1), channel_id=1, source_target_pairs={{0,6},{2,4},{4,2},{6,0},{1,7},{3,5},{5,3},{7,1},{8,14},{10,12},{12... | collective-permute-start | bytes 49160 | tf_op jit(solution)/shard_map/ppermute | solution.py:475
  50.4 1.3 %collective-permute-start.6 = (f32[32,128]{1,0:T(8,128)S(1)}, f32[32,128]{1,0:T(8,128)S(1)}, u32[]{:S(2)}, u32[]{:S(2)}) collective-permute-start(f32[32,128]{1,0:T(8,128)S(1)} %add_add_fusion.1), channel_id=1, source_target_pairs={{0,4},{2,6},{4,0},{6,2},{1,5},{3,7},{5,1},{7,3},{8,12},{10,14},{12... | collective-permute-start | bytes 49160 | tf_op jit(solution)/shard_map/ppermute | solution.py:475
  51.7 1.7 %collective-permute-start.5 = (f32[32,128]{1,0:T(8,128)S(1)}, f32[32,128]{1,0:T(8,128)S(1)}, u32[]{:S(2)}, u32[]{:S(2)}) collective-permute-start(f32[32,128]{1,0:T(8,128)S(1)} %add_add_fusion.1), channel_id=1, source_target_pairs={{0,2},{2,0},{4,6},{6,4},{1,3},{3,1},{5,7},{7,5},{8,10},{10,8},{12,... | collective-permute-start | bytes 49160 | tf_op jit(solution)/shard_map/ppermute | solution.py:475
  53.5 1.1 %collective-permute-done.7 = f32[32,128]{1,0:T(8,128)S(1)} collective-permute-done((f32[32,128]{1,0:T(8,128)S(1)}, f32[32,128]{1,0:T(8,128)S(1)}, u32[]{:S(2)}, u32[]{:S(2)}) %collective-permute-start.7) | collective-permute-done | bytes 16416 | tf_op jit(solution)/shard_map/ppermute | solution.py:475
  54.6 0.5 collective-permute-done.6
  55.1 0.4 collective-permute-done.5
  55.5 1.0 %collective-permute-start.8 = (f32[32,128]{1,0:T(8,128)S(1)}, f32[32,128]{1,0:T(8,128)S(1)}, u32[]{:S(2)}, u32[]{:S(2)}) collective-permute-start(f32[32,128]{1,0:T(8,128)S(1)} %add_add_fusion.refs_0_), channel_id=1, source_target_pairs={{0,1},{1,0},{2,3},{3,2},{4,5},{5,4},{6,7},{7,6},{8,9},{9,8},{10,11... | collective-permute-start | bytes 49160 | tf_op jit(solution)/shard_map/ppermute | solution.py:475
  56.5 0.0 collective-permute-start.9
  56.5 2.7 %collective-permute-done.8.refs_1_ = f32[32,128]{1,0:T(8,128)S(1)} collective-permute-done((f32[32,128]{1,0:T(8,128)S(1)}, f32[32,128]{1,0:T(8,128)S(1)}, u32[]{:S(2)}, u32[]{:S(2)}) %collective-permute-start.8) | collective-permute-done | bytes 16416 | tf_op jit(solution)/shard_map/ppermute | solution.py:475
  59.2 0.0 collective-permute-done.4.refs_1_
  59.2 0.0 collective-permute-start.10
  59.2 1.5 %inverse.1.left_ref = bf16[48,192]{1,0:T(8,128)(2,1)S(1)} custom-call(f32[32,128]{1,0:T(8,128)S(1)} %add_add_fusion.refs_0_, f32[32,128]{1,0:T(8,128)S(1)} %collective-permute-done.8.refs_1_), custom_call_target="tpu_custom_call" | custom-call | tf_op jit(solution)/shard_map/inverse/pallas_call | solution.py:399
  60.7 0.0 collective-permute-done.9.refs_2_
  60.7 0.3 collective-permute-done.10.refs_3_
  60.9 1.2 %rotate.1 = f32[768,128]{1,0:T(8,128)} custom-call(bf16[48,192]{1,0:T(8,128)(2,1)S(1)} %inverse.1.left_ref, f32[768,128]{1,0:T(8,128)S(1)} %bitcast.8, f32[768,128]{1,0:T(8,128)S(1)} %collective-permute-done.4.refs_1_, f32[768,128]{1,0:T(8,128)S(1)} %collective-permute-done.9.refs_2_, f32[768,128]{1,0:T(8,128)S(1)} %collective-permute-done.10.refs_3_), custom_call_target="tpu_custom_call" | custom-call | tf_op jit(solution)/shard_map/rotate/pallas_call | solution.py:435
  (5 shorter events, 0.0 us)
Async XLA Ops:
  0.0 0.7 %copy-start = (f32[6,8,128]{2,1,0:T(8,128)S(1)}, f32[6,8,128]{2,1,0:T(8,128)}, u32[]{:S(2)}) copy-start(f32[6,8,128]{2,1,0:T(8,128)} %param.3) | copy-start | bytes 73732
  22.7 1.4 %collective-permute-start = (f32[8,24,128]{2,1,0:T(8,128)S(1)}, f32[8,24,128]{2,1,0:T(8,128)S(1)}, u32[]{:S(2)}, u32[]{:S(2)}) collective-permute-start(f32[8,24,128]{2,1,0:T(8,128)S(1)} %slice.4), channel_id=1, source_target_pairs={{0,8},{8,0},{1,9},{9,1},{2,10},{10,2},{3,11},{11,3},{4,12},{12,4},... | collective-permute-start | bytes 294920 | tf_op jit(solution)/shard_map/ppermute | solution.py:463
  43.9 3.2 %collective-permute-start.3 = (f32[32,128]{1,0:T(8,128)S(1)}, f32[32,128]{1,0:T(8,128)S(1)}, u32[]{:S(2)}, u32[]{:S(2)}) collective-permute-start(f32[32,128]{1,0:T(8,128)S(1)} %margin.1), channel_id=1, source_target_pairs={{0,24},{8,16},{16,8},{24,0},{1,25},{9,17},{17,9},{25,1},{2,26},{10... | collective-permute-start | bytes 49160 | tf_op jit(solution)/shard_map/ppermute | solution.py:475
  44.4 3.7 %collective-permute-start.2 = (f32[32,128]{1,0:T(8,128)S(1)}, f32[32,128]{1,0:T(8,128)S(1)}, u32[]{:S(2)}, u32[]{:S(2)}) collective-permute-start(f32[32,128]{1,0:T(8,128)S(1)} %margin.1), channel_id=1, source_target_pairs={{0,16},{8,24},{16,0},{24,8},{1,17},{9,25},{17,1},{25,9},{2,18},{10... | collective-permute-start | bytes 49160 | tf_op jit(solution)/shard_map/ppermute | solution.py:475
  45.2 2.9 %collective-permute-start.1 = (f32[32,128]{1,0:T(8,128)S(1)}, f32[32,128]{1,0:T(8,128)S(1)}, u32[]{:S(2)}, u32[]{:S(2)}) collective-permute-start(f32[32,128]{1,0:T(8,128)S(1)} %margin.1), channel_id=1, source_target_pairs={{0,8},{8,0},{16,24},{24,16},{1,9},{9,1},{17,25},{25,17},{2,10},{10... | collective-permute-start | bytes 49160 | tf_op jit(solution)/shard_map/ppermute | solution.py:475
  48.1 11.1 %collective-permute-start.4 = (f32[768,128]{1,0:T(8,128)S(1)}, f32[768,128]{1,0:T(8,128)S(1)}, u32[]{:S(2)}, u32[]{:S(2)}) collective-permute-start(f32[768,128]{1,0:T(8,128)S(1)} %bitcast.6), channel_id=1, source_target_pairs={{0,16},{16,0},{1,17},{17,1},{2,18},{18,2},{3,19},{19,3},{4,20},{20... | collective-permute-start | bytes 1179656 | tf_op jit(solution)/shard_map/ppermute | solution.py:475
  49.1 5.5 %collective-permute-start.7 = (f32[32,128]{1,0:T(8,128)S(1)}, f32[32,128]{1,0:T(8,128)S(1)}, u32[]{:S(2)}, u32[]{:S(2)}) collective-permute-start(f32[32,128]{1,0:T(8,128)S(1)} %add_add_fusion.1), channel_id=1, source_target_pairs={{0,6},{2,4},{4,2},{6,0},{1,7},{3,5},{5,3},{7,1},{8,14},{10,12},{12... | collective-permute-start | bytes 49160 | tf_op jit(solution)/shard_map/ppermute | solution.py:475
  50.4 4.6 %collective-permute-start.6 = (f32[32,128]{1,0:T(8,128)S(1)}, f32[32,128]{1,0:T(8,128)S(1)}, u32[]{:S(2)}, u32[]{:S(2)}) collective-permute-start(f32[32,128]{1,0:T(8,128)S(1)} %add_add_fusion.1), channel_id=1, source_target_pairs={{0,4},{2,6},{4,0},{6,2},{1,5},{3,7},{5,1},{7,3},{8,12},{10,14},{12... | collective-permute-start | bytes 49160 | tf_op jit(solution)/shard_map/ppermute | solution.py:475
  51.7 3.7 %collective-permute-start.5 = (f32[32,128]{1,0:T(8,128)S(1)}, f32[32,128]{1,0:T(8,128)S(1)}, u32[]{:S(2)}, u32[]{:S(2)}) collective-permute-start(f32[32,128]{1,0:T(8,128)S(1)} %add_add_fusion.1), channel_id=1, source_target_pairs={{0,2},{2,0},{4,6},{6,4},{1,3},{3,1},{5,7},{7,5},{8,10},{10,8},{12,... | collective-permute-start | bytes 49160 | tf_op jit(solution)/shard_map/ppermute | solution.py:475
  55.5 3.7 %collective-permute-start.8 = (f32[32,128]{1,0:T(8,128)S(1)}, f32[32,128]{1,0:T(8,128)S(1)}, u32[]{:S(2)}, u32[]{:S(2)}) collective-permute-start(f32[32,128]{1,0:T(8,128)S(1)} %add_add_fusion.refs_0_), channel_id=1, source_target_pairs={{0,1},{1,0},{2,3},{3,2},{4,5},{5,4},{6,7},{7,6},{8,9},{9,8},{10,11... | collective-permute-start | bytes 49160 | tf_op jit(solution)/shard_map/ppermute | solution.py:475
  56.5 4.2 %collective-permute-start.9 = (f32[768,128]{1,0:T(8,128)S(1)}, f32[768,128]{1,0:T(8,128)S(1)}, u32[]{:S(2)}, u32[]{:S(2)}) collective-permute-start(f32[768,128]{1,0:T(8,128)S(1)} %bitcast.7), channel_id=1, source_target_pairs={{0,8},{8,0},{1,9},{9,1},{2,10},{10,2},{3,11},{11,3},{4,12},{12,4},... | collective-permute-start | bytes 1179656 | tf_op jit(solution)/shard_map/ppermute | solution.py:480
  59.2 1.7 %collective-permute-start.10 = (f32[768,128]{1,0:T(8,128)S(1)}, f32[768,128]{1,0:T(8,128)S(1)}, u32[]{:S(2)}, u32[]{:S(2)}) collective-permute-start(f32[768,128]{1,0:T(8,128)S(1)} %collective-permute-done.4.refs_1_), channel_id=1, source_target_pairs={{0,8},{8,0},{1,9},{9,1},{2,10},{10,2},{3,11},{11,3},{4,12},{12,4},... | collective-permute-start | bytes 1179656 | tf_op jit(solution)/shard_map/ppermute | solution.py:484

commit v5 on v4

--- a/solution.py
+++ b/solution.py
@@ -213,6 +213,7 @@
         if step:
             field = src[:, :, pl.ds(PAD, height), :].reshape(own * width * height, nz)
             zbuf[...] = along_z(field, w1_ref, w2_ref).reshape(own, width, height, nz)
+        squares = [jnp.zeros((TILE, nz), jnp.float32) for _ in range(own)]
         for k in range(own):
             for x in range(width):
                 for tile in range(height // TILE):
@@ -231,10 +232,18 @@
                     if not last:
                         place(dst, k, x, tile, height, value)
                         continue
+                    squares[k] = squares[k] + value * value
                     for r in range(0, TILE, TILE // 2):
                         piece, row = divmod(in_pencil + r, rows)
                         to = piece_owner(piece, pieces) * gx * gy + g
                         out_ref[to, pl.ds(k * rows + row, TILE // 2), :] = value[r : r + TILE // 2]
+    line = lax.broadcasted_iota(jnp.int32, out_ref.shape[1:], 0)
+    factor = jnp.zeros(out_ref.shape[1:], jnp.float32)
+    for k in range(own):
+        mean = jnp.sum(squares[k], keepdims=True) * (1.0 / (width * height * nz))
+        factor = jnp.where(line // rows == k, lax.rsqrt(mean), factor)
+    for to in range(out_ref.shape[0]):
+        out_ref[to] = out_ref[to] * factor
 
 
 def piece_owner(piece, pieces):
@@ -282,7 +291,7 @@
     )(field, laplace, packed, other, *weights)
 
 
-def margin_kernel(rows, bands, scale, x_ref, out_ref):
+def margin_kernel(rows, bands, scale, grid, x_ref, out_ref):
     highs, mids, lows = [], [], []
     for r in range(rows):
         high, mid, low = split3(x_ref[pl.ds(r, bands, stride=rows), :])
@@ -298,15 +307,22 @@
 
     small = block(0, 2) + block(2, 0) + block(1, 1)
     total = (small + (block(0, 1) + block(1, 0)) + block(0, 0)) * scale
-    out_ref[:, pl.ds(0, bands)] = total[: bands // 2]
-    out_ref[:, pl.ds(bands, bands)] = total[bands // 2 :]
-
-
-def partial_margin(blocks, bands, scale):
+    half = bands // 2
+    row = lax.broadcasted_iota(jnp.int32, (half, half), 0)
+    col = lax.broadcasted_iota(jnp.int32, (half, half), 1)
+    strict = jnp.where(row > col, total[:half, :half], total[half:, half:])
+    for core, part in enumerate((total[half:, :half], strict)):
+        folded = jnp.concatenate([part[at : at + TILE] for at in range(0, half, TILE)], 1)
+        for to in range(out_ref.shape[0]):
+            if to // grid % 2 == core:
+                out_ref[to] = folded
+
+
+def partial_margin(blocks, bands, scale, pieces, grid):
     rows = blocks.shape[0] // bands
     return pl.pallas_call(
-        functools.partial(margin_kernel, rows, bands, scale),
-        out_shape=jax.ShapeDtypeStruct((bands // 2, 2 * bands), jnp.float32),
+        functools.partial(margin_kernel, rows, bands, scale, grid),
+        out_shape=jax.ShapeDtypeStruct((pieces * grid, TILE, (bands // 2) ** 2 // TILE), jnp.float32),
         in_specs=[pl.BlockSpec(memory_space=pltpu.VMEM)],
         out_specs=pl.BlockSpec(memory_space=pltpu.VMEM),
         compiler_params=pltpu.CompilerParams(vmem_limit_bytes=8 * 1024 * 1024),
@@ -314,17 +330,34 @@
     )(blocks)
 
 
-def eliminate(folded):
-    bands = folded.shape[1] // 2
+def sum_kernel(in_ref, out_ref):
+    total = in_ref[0]
+    for term in range(1, in_ref.shape[0]):
+        total = total + in_ref[term]
+    out_ref[...] = total
+
+
+def sum_first(value):
+    return pl.pallas_call(
+        sum_kernel,
+        out_shape=jax.ShapeDtypeStruct(value.shape[1:], value.dtype),
+        in_specs=[pl.BlockSpec(memory_space=pltpu.VMEM)],
+        out_specs=pl.BlockSpec(memory_space=pltpu.VMEM),
+        compiler_params=pltpu.CompilerParams(vmem_limit_bytes=4 * 1024 * 1024),
+        name="sum",
+    )(value)
+
+
+def eliminate(margin):
+    bands = margin.shape[0]
     tiles = bands // TILE
+    margin = jnp.concatenate([margin, margin], 1)
     width = 2 * bands
     lines = lax.broadcasted_iota(jnp.int32, (TILE, width), 0)
     lanes = lax.broadcasted_iota(jnp.int32, (TILE, width), 1)
-    swapped = jnp.concatenate([folded[:, bands:], folded[:, :bands]], 1)
     both = []
     for t in range(tiles):
-        at = t * TILE % (bands // 2)
-        right = (swapped if t < tiles // 2 else folded)[at : at + TILE]
+        right = margin[t * TILE : (t + 1) * TILE]
         eye = jnp.where(lines + t * TILE == lanes % bands, 1.0, 0.0)
         both.append([eye, jnp.where(lanes < bands, eye, right)])
 
@@ -376,11 +409,23 @@
 
 def inverse_kernel(dims, *refs):
     bands, own = dims
-    margins, left_ref, inv_ref = refs[:-2], refs[-2], refs[-1]
-    folded = margins[0][...]
-    for term in margins[1:]:
-        folded = folded + term[...]
-    for t, value in enumerate(eliminate(folded)):
+    own_ref, other_ref, left_ref, inv_ref = refs
+    half = bands // 2
+    here, there = own_ref[...], other_ref[...]
+    first = lax.axis_index("core") == 0
+    cross, strict = [
+        jnp.concatenate([value[:, at : at + half] for at in range(0, half * half // TILE, half)], 0)
+        for value in (jnp.where(first, here, there), jnp.where(first, there, here))
+    ]
+    row = lax.broadcasted_iota(jnp.int32, (half, half), 0)
+    col = lax.broadcasted_iota(jnp.int32, (half, half), 1)
+    turned = strict.T
+    low = jnp.where(row == col, 1.0, jnp.where(row > col, strict, turned))
+    high = jnp.where(row == col, 1.0, jnp.where(row < col, strict, turned))
+    margin = jnp.concatenate(
+        [jnp.concatenate([low, cross.T], 1), jnp.concatenate([cross, high], 1)], 0
+    )
+    for t, value in enumerate(eliminate(margin)):
         inv_ref[pl.ds(t * TILE, TILE), :] = value
     first = pl.multiple_of((lax.axis_index("chip") * 2 + lax.axis_index("core")) * own, TILE)
     rows = inv_ref[pl.ds(first, own), pl.ds(0, 3 * bands)]
@@ -474,12 +519,12 @@
         pairs = [[(i, i ^ mask) for i in range(count)] for mask in range(1, count)]
         return [value] + [lax.ppermute(value, axes, pair) for pair in pairs]
 
-    margin = partial_margin(blocks, bands, 1.0 / (cells * nz * grid))
-    margin = sum(copies(margin, "chip", "core"))
-    parts = copies(tied(blocks, margin), "chip")
-    crossed = [lax.ppermute(tied(blocks, margin), "core", swap)]
-    margin = sum(copies(margin, "gx"))
-    margins = copies(margin, "gy")
+    spread = partial_margin(blocks, bands, 1.0 / (cells * nz * grid), pieces, grid)
+    parts = copies(blocks, "chip")
+    crossed = [lax.ppermute(blocks, "core", swap)]
+    crossed, spread = lax.optimization_barrier((crossed, spread))
+    margins = lax.all_to_all(spread, ("chip", "core", "gx", "gy"), 0, 0)
+    margins = copies(sum_first(margins), "core")
     far, margins = lax.optimization_barrier((parts[1:], margins))
     parts += crossed + [lax.ppermute(part, "core", swap) for part in far]
     left = inverse_rows(margins, own_bands, bands)

time: 62.4 us -> 61.4 us (0.984)
  blocking collectives: 37.9 us -> 49.3 us
  starting transfers between devices: 8.29 us -> 1.27 us
  waiting for transfers between devices: 7.93 us -> 1.92 us
    all_to_all x0 -> x1, blocking collectives: none -> 11.4 us  [on_device_fields(): margins = lax.all_to_all(spread, ('chip', 'core', 'gx', 'gy'), 0, 0)]
    ppermute x8 -> x2, starting transfers between devices: 8.21 us -> 1.03 us  [copies(): return [value] + [lax.ppermute(value, axes, pair) for pair in pairs]]
    ppermute x8 -> x2, waiting for transfers between devices: 7.07 us -> 1.05 us  [copies(): return [value] + [lax.ppermute(value, axes, pair) for pair in pairs]]
  transfers between devices with their start and end apart: 11 -> 5, of which waited for: 8 -> 3; matrix products, arithmetic and copies ran while one was open for 0% -> 0% of each run, Pallas kernels for 3% -> 5%
where the time goes in v5:
time: 61.4 us; the launch traced here: 61.1 us
  blocking collectives  49.3 us (80%)
  Pallas kernels  6.79 us (11%)
  waiting for transfers between devices  1.92 us (3%)
  starting transfers between devices  1.27 us (2%)
  other arithmetic  1.03 us (2%)
  local copies, waits for them, and re-layouts  0.76 us (1%)
    all_to_all x1, blocking collectives, on_device_fields(): packed = lax.all_to_all(packed, ('gx', 'gy'), 0, 0)  20.9 us
    all_to_all x1, blocking collectives, on_device_fields(): lax.all_to_all(filtered, ('chip', 'core', 'gx', 'gy'), 0, 0)  17 us
    all_to_all x1, blocking collectives, on_device_fields(): margins = lax.all_to_all(spread, ('chip', 'core', 'gx', 'gy'), 0, 0)  11.4 us
    pallas_call x1, Pallas kernels, apply_filter(): pl.pallas_call(functools.partial(filter_kernel, dims), out_shape=jax.Shap...  2.58 us
    pallas_call x1, Pallas kernels, inverse_rows(): pl.pallas_call(functools.partial(inverse_kernel, (bands, own)), out_shape...  1.68 us
  transfers between devices with their start and end apart: 5, of which 3 were waited for; matrix products, arithmetic and copies ran while one was open for 0% of the time, Pallas kernels for 5%

profile of v5, /device:TPU:0, one launch (start us, length us, event | category | flops | bytes accessed | tf_op | source)
XLA Modules:
  0.0 61.1 jit_solution(10394842573453290808)
XLA Ops:
  0.0 0.0 copy-start
  0.0 0.7 %copy-done = f32[6,8,128]{2,1,0:T(8,128)S(1)} copy-done((f32[6,8,128]{2,1,0:T(8,128)S(1)}, f32[6,8,128]{2,1,0:T(8,128)}, u32[]{:S(2)}) %copy-start) | copy-done | bytes 24600
  0.8 1.0 %pad_maximum_fusion = f32[8,120,128]{2,1,0:T(8,128)S(1)} fusion(f32[8,24,128]{2,1,0:T(8,128)S(1)} %broadcast_in_dim.2, f32[8,96,128]{2,1,0:T(8,128)} %bitcast.9), kind=kLoop, calls=%fused_computation | loop fusion | flops 122880 | bytes 983040 | tf_op jit(solution)/shard_map/concatenate | solution.py:506
  1.8 20.9 %all_to_all.15.in_ref.half_ref = f32[8,120,128]{2,1,0:T(8,128)S(1)} all-to-all(f32[8,120,128]{2,1,0:T(8,128)S(1)} %pad_maximum_fusion), channel_id=1, replica_groups=mesh['chip'=2,'core'=2,'gx'=4,'gy'=2] {'gx','gy'}, dimensions={0} | all-to-all | bytes 983040 | tf_op jit(solution)/shard_map/all_to_all | solution.py:507
  22.7 0.1 collective-permute-start
  22.8 0.7 %laplace.1 = (f32[2,24,32,128]{3,2,1,0:T(8,128)S(1)}, f32[2,24,16,128]{3,2,1,0:T(8,128)S(1)}, bf16[256,256]{1,0:T(8,128)(2,1)S(1)}, bf16[256,128]{1,0:T(8,128)(2,1)S(1)}) custom-call(f32[8,120,128]{2,1,0:T(8,128)S(1)} %all_to_all.15.in_ref.half_ref), custom_call_target="tpu_custom_call" | custom-call | flops 4325376 | bytes 1572864 | tf_op jit(solution)/shard_map/laplace/pallas_call | solution.py:259
  23.5 0.6 collective-permute-done.other_ref
  24.1 2.6 %filter.1 = f32[32,24,128]{2,1,0:T(8,128)S(1)} custom-call(f32[2,24,32,128]{3,2,1,0:T(8,128)S(1)} %get-tuple-element.14.field_ref, f32[2,24,16,128]{3,2,1,0:T(8,128)S(1)} %get-tuple-element.15.lap_ref, f32[8,120,128]{2,1,0:T(8,128)S(1)} %all_to_all.15.in_ref.half_ref, f32[8,24,128]{2,1,0:T(8,128)S(1)} %collective-permute-done.other_ref, ...), custom_call_target="tpu_custom_call" | custom-call | tf_op jit(solution)/shard_map/filter/pallas_call | solution.py:278
  26.7 17.0 %all_to_all.16 = f32[32,24,128]{2,1,0:T(8,128)S(1)} all-to-all(f32[32,24,128]{2,1,0:T(8,128)S(1)} %filter.1), channel_id=1, replica_groups=mesh['chip'=2,'core'=2,'gx'=4,'gy'=2] {'chip','core','gx','gy'}, dimensions={0} | all-to-all | bytes 786432 | tf_op jit(solution)/shard_map/all_to_all | solution.py:512
  43.6 0.0 collective-permute-start.2
  43.6 0.9 %collective-permute-start.1 = (f32[768,128]{1,0:T(8,128)S(1)}, f32[768,128]{1,0:T(8,128)S(1)}, u32[]{:S(2)}, u32[]{:S(2)}) collective-permute-start(f32[768,128]{1,0:T(8,128)S(1)} %bitcast.6), channel_id=1, source_target_pairs={{0,16},{16,0},{1,17},{17,1},{2,18},{18,2},{3,19},{19,3},{4,20},{20... | collective-permute-start | bytes 1179656 | tf_op jit(solution)/shard_map/ppermute | solution.py:520
  44.5 0.6 margin.1
  45.1 0.3 collective-permute-done.2.refs_2_
  45.3 11.4 %all_to_all.17.in_ref = f32[32,8,128]{2,1,0:T(8,128)S(1)} all-to-all(f32[32,8,128]{2,1,0:T(8,128)S(1)} %margin.1), channel_id=1, replica_groups=mesh['chip'=2,'core'=2,'gx'=4,'gy'=2] {'chip','core','gx','gy'}, dimensions={0} | all-to-all | bytes 262144 | tf_op jit(solution)/shard_map/all_to_all | solution.py:526
  56.8 0.2 collective-permute-start.3
  57.0 0.0 collective-permute-done.1.refs_1_
  57.0 1.0 %collective-permute-done.3.refs_1_ = f32[8,128]{1,0:T(8,128)S(1)} collective-permute-done((f32[8,128]{1,0:T(8,128)S(1)}, f32[8,128]{1,0:T(8,128)S(1)}, u32[]{:S(2)}, u32[]{:S(2)}) %collective-permute-start.3) | collective-permute-done | bytes 4128 | tf_op jit(solution)/shard_map/ppermute | solution.py:520
  58.0 0.2 collective-permute-start.4
  58.2 1.7 %inverse.1.left_ref = bf16[48,192]{1,0:T(8,128)(2,1)S(1)} custom-call(f32[8,128]{1,0:T(8,128)S(1)} %sum.1.refs_0_, f32[8,128]{1,0:T(8,128)S(1)} %collective-permute-done.3.refs_1_), custom_call_target="tpu_custom_call" | custom-call | tf_op jit(solution)/shard_map/inverse/pallas_call | solution.py:444
  59.9 0.0 collective-permute-done.4.refs_3_
  59.9 1.2 %rotate.1 = f32[768,128]{1,0:T(8,128)} custom-call(bf16[48,192]{1,0:T(8,128)(2,1)S(1)} %inverse.1.left_ref, f32[768,128]{1,0:T(8,128)S(1)} %bitcast.8, f32[768,128]{1,0:T(8,128)S(1)} %collective-permute-done.1.refs_1_, f32[768,128]{1,0:T(8,128)S(1)} %collective-permute-done.2.refs_2_, f32[768,128]{1,0:T(8,128)S(1)} %collective-permute-done.4.refs_3_), custom_call_target="tpu_custom_call" | custom-call | tf_op jit(solution)/shard_map/rotate/pallas_call | solution.py:480
  (4 shorter events, 0.1 us)
Async XLA Ops:
  0.0 0.7 %copy-start = (f32[6,8,128]{2,1,0:T(8,128)S(1)}, f32[6,8,128]{2,1,0:T(8,128)}, u32[]{:S(2)}) copy-start(f32[6,8,128]{2,1,0:T(8,128)} %param.3) | copy-start | bytes 73732
  22.7 1.4 %collective-permute-start = (f32[8,24,128]{2,1,0:T(8,128)S(1)}, f32[8,24,128]{2,1,0:T(8,128)S(1)}, u32[]{:S(2)}, u32[]{:S(2)}) collective-permute-start(f32[8,24,128]{2,1,0:T(8,128)S(1)} %slice.4), channel_id=1, source_target_pairs={{0,8},{8,0},{1,9},{9,1},{2,10},{10,2},{3,11},{11,3},{4,12},{12,4},... | collective-permute-start | bytes 294920 | tf_op jit(solution)/shard_map/ppermute | solution.py:508
  43.6 1.7 %collective-permute-start.2 = (f32[768,128]{1,0:T(8,128)S(1)}, f32[768,128]{1,0:T(8,128)S(1)}, u32[]{:S(2)}, u32[]{:S(2)}) collective-permute-start(f32[768,128]{1,0:T(8,128)S(1)} %bitcast.5), channel_id=1, source_target_pairs={{0,8},{8,0},{1,9},{9,1},{2,10},{10,2},{3,11},{11,3},{4,12},{12,4},... | collective-permute-start | bytes 1179656 | tf_op jit(solution)/shard_map/ppermute | solution.py:524
  43.6 13.4 %collective-permute-start.1 = (f32[768,128]{1,0:T(8,128)S(1)}, f32[768,128]{1,0:T(8,128)S(1)}, u32[]{:S(2)}, u32[]{:S(2)}) collective-permute-start(f32[768,128]{1,0:T(8,128)S(1)} %bitcast.6), channel_id=1, source_target_pairs={{0,16},{16,0},{1,17},{17,1},{2,18},{18,2},{3,19},{19,3},{4,20},{20... | collective-permute-start | bytes 1179656 | tf_op jit(solution)/shard_map/ppermute | solution.py:520
  56.8 1.2 %collective-permute-start.3 = (f32[8,128]{1,0:T(8,128)S(1)}, f32[8,128]{1,0:T(8,128)S(1)}, u32[]{:S(2)}, u32[]{:S(2)}) collective-permute-start(f32[8,128]{1,0:T(8,128)S(1)} %sum.1.refs_0_), channel_id=1, source_target_pairs={{0,8},{8,0},{1,9},{9,1},{2,10},{10,2},{3,11},{11,3},{4,12},{12,4},... | collective-permute-start | bytes 12296 | tf_op jit(solution)/shard_map/ppermute | solution.py:520
  58.0 1.8 %collective-permute-start.4 = (f32[768,128]{1,0:T(8,128)S(1)}, f32[768,128]{1,0:T(8,128)S(1)}, u32[]{:S(2)}, u32[]{:S(2)}) collective-permute-start(f32[768,128]{1,0:T(8,128)S(1)} %collective-permute-done.1.refs_1_), channel_id=1, source_target_pairs={{0,8},{8,0},{1,9},{9,1},{2,10},{10,2},{3,11},{11,3},{4,12},{12,4},... | collective-permute-start | bytes 1179656 | tf_op jit(solution)/shard_map/ppermute | solution.py:529

commit v6 on v5

--- a/solution.py
+++ b/solution.py
@@ -136,15 +136,10 @@
     return split3(circulant)
 
 
-PAD = TILE
-
-
 def place(buf, k, x, tile, height, value):
-    buf[k, x, pl.ds(PAD + tile * TILE, TILE), :] = value
+    buf[k, x, pl.ds(tile * TILE, TILE), :] = value
     if tile == 0:
-        buf[k, x, pl.ds(PAD + height, TILE), :] = value
-    if tile == height // TILE - 1:
-        buf[k, x, pl.ds(0, TILE), :] = value
+        buf[k, x, pl.ds(height, TILE), :] = value
 
 
 def along_z(field, w1_ref, w2_ref):
@@ -155,14 +150,40 @@
     return part[:, :nz] + part[:, nz:] + rest
 
 
-def add_xy(src, k, x, tile, total):
+def along_xy(src, k, height, wanted):
     width = src.shape[1]
-    at = PAD + tile * TILE
-    for j in range(1, REACH + 1):
-        near = src[k, (x + j) % width, pl.ds(at, TILE), :] + src[k, (x - j) % width, pl.ds(at, TILE), :]
-        near = near + src[k, x, pl.ds(at + j, TILE), :] + src[k, x, pl.ds(at - j, TILE), :]
-        total = total + (-0.5 * COEFFS[j]) * near
-    return total
+    tiles = range(height // TILE)
+    window = {}
+
+    def plane(x, t):
+        if (x, t) not in window:
+            window[x, t] = src[k, x % width, pl.ds(t * TILE, TILE), :]
+        return window[x, t]
+
+    for x in range(width):
+        rows, pairs = {}, {}
+
+        def shifted(at):
+            if at not in rows:
+                rows[at] = src[k, x, pl.ds(at, TILE), :]
+            return rows[at]
+
+        def pair(*ends):
+            ends = tuple(sorted(at % height for at in ends))
+            if ends not in pairs:
+                pairs[ends] = shifted(ends[0]) + shifted(ends[1])
+            return pairs[ends]
+
+        totals = []
+        for t in tiles if wanted else ():
+            total = None
+            for j in range(1, REACH + 1):
+                near = plane(x + j, t) + plane(x - j, t)
+                near = near + pair(t * TILE + j, t * TILE - j)
+                near = (-0.5 * COEFFS[j]) * near
+                total = near if total is None else total + near
+            totals.append(total)
+        yield x, [plane(x, t) for t in tiles], totals
 
 
 def laplace_kernel(dims, in_ref, field_ref, lap_ref, w1_ref, w2_ref):
@@ -181,13 +202,13 @@
                 for t in range(ny // TILE):
                     value = in_ref[g, pl.ds(k * cells + i * ny + t * TILE, TILE), :]
                     place(field_ref, k, at_x + i, at_y // TILE + t, height, value)
-    field = field_ref[:, :, pl.ds(PAD, height), :].reshape(own * width * height, nz)
+    field = field_ref[:, :, pl.ds(0, height), :].reshape(own * width * height, nz)
     lap_ref[...] = along_z(field, w1_ref, w2_ref).reshape(own, width, height, nz)
     for k in range(own):
-        for x in range(width):
-            for tile in range(height // TILE):
+        for x, _, totals in along_xy(field_ref, k, height, True):
+            for tile, total in enumerate(totals):
                 rows = pl.ds(tile * TILE, TILE)
-                lap_ref[k, x, rows, :] = add_xy(field_ref, k, x, tile, lap_ref[k, x, rows, :])
+                lap_ref[k, x, rows, :] = lap_ref[k, x, rows, :] + total
 
 
 def filter_kernel(dims, field_ref, lap_ref, half_ref, other_ref, w1_ref, w2_ref, out_ref, pot, buf_a, buf_b, zbuf):
@@ -211,24 +232,23 @@
         src, dst, old = chain[step], buf_b if step % 2 else buf_a, chain[step - 1]
         last = step == len(steps) - 1
         if step:
-            field = src[:, :, pl.ds(PAD, height), :].reshape(own * width * height, nz)
+            field = src[:, :, pl.ds(0, height), :].reshape(own * width * height, nz)
             zbuf[...] = along_z(field, w1_ref, w2_ref).reshape(own, width, height, nz)
         squares = [jnp.zeros((TILE, nz), jnp.float32) for _ in range(own)]
         for k in range(own):
-            for x in range(width):
+            for x, centres, totals in along_xy(src, k, height, bool(step)):
                 for tile in range(height // TILE):
                     g = (x // nx) * gy + tile * TILE // ny
                     in_pencil = (x % nx) * ny + (tile * TILE) % ny
-                    inner = pl.ds(PAD + tile * TILE, TILE)
                     plain = pl.ds(tile * TILE, TILE)
                     if step:
-                        total = add_xy(src, k, x, tile, zbuf[k, x, plain, :])
+                        total = zbuf[k, x, plain, :] + totals[tile]
                     else:
                         total = lap_ref[k, x, plain, :]
-                    total = total + pot[g, pl.ds(in_pencil, TILE), :] * src[k, x, inner, :]
+                    total = total + pot[g, pl.ds(in_pencil, TILE), :] * centres[tile]
                     value = scale * total
                     if step:
-                        value = value - back * old[k, x, inner, :]
+                        value = value - back * old[k, x, plain, :]
                     if not last:
                         place(dst, k, x, tile, height, value)
                         continue
@@ -259,7 +279,7 @@
     return pl.pallas_call(
         functools.partial(laplace_kernel, dims),
         out_shape=(
-            jax.ShapeDtypeStruct((bands, width, height + 2 * PAD, nz), jnp.float32),
+            jax.ShapeDtypeStruct((bands, width, height + TILE, nz), jnp.float32),
             jax.ShapeDtypeStruct((bands, width, height, nz), jnp.float32),
             jax.ShapeDtypeStruct((2 * nz, 2 * nz), jnp.bfloat16),
             jax.ShapeDtypeStruct((2 * nz, nz), jnp.bfloat16),

time: 61.4 us -> 60.7 us (0.989)
  Pallas kernels: 6.79 us -> 6.01 us
    pallas_call x1, Pallas kernels: 2.58 us -> 1.89 us  [apply_filter(): pl.pallas_call(functools.partial(filter_kernel, dims), out_shape=jax.Shap...]
where the time goes in v6:
time: 60.7 us; the launch traced here: 60.4 us
  blocking collectives  49.3 us (81%)
  Pallas kernels  6.01 us (10%)
  waiting for transfers between devices  2.01 us (3%)
  starting transfers between devices  1.27 us (2%)
  other arithmetic  1.03 us (2%)
  local copies, waits for them, and re-layouts  0.76 us (1%)
    all_to_all x1, blocking collectives, on_device_fields(): packed = lax.all_to_all(packed, ('gx', 'gy'), 0, 0)  20.9 us
    all_to_all x1, blocking collectives, on_device_fields(): lax.all_to_all(filtered, ('chip', 'core', 'gx', 'gy'), 0, 0)  17 us
    all_to_all x1, blocking collectives, on_device_fields(): margins = lax.all_to_all(spread, ('chip', 'core', 'gx', 'gy'), 0, 0)  11.4 us
    pallas_call x1, Pallas kernels, apply_filter(): pl.pallas_call(functools.partial(filter_kernel, dims), out_shape=jax.Shap...  1.89 us
    pallas_call x1, Pallas kernels, inverse_rows(): pl.pallas_call(functools.partial(inverse_kernel, (bands, own)), out_shape...  1.68 us
    pallas_call x1, Pallas kernels, rotate(): pl.pallas_call(functools.partial(rotate_kernel, (bands, own)), out_shape=...  1.23 us
  transfers between devices with their start and end apart: 5, of which 3 were waited for; matrix products, arithmetic and copies ran while one was open for 0% of the time, Pallas kernels for 5%

profile of v6, /device:TPU:0, one launch (start us, length us, event | category | flops | bytes accessed | tf_op | source)
XLA Modules:
  0.0 60.4 jit_solution(10807753897482313655)
XLA Ops:
  0.0 0.0 copy-start
  0.0 0.7 %copy-done = f32[6,8,128]{2,1,0:T(8,128)S(1)} copy-done((f32[6,8,128]{2,1,0:T(8,128)S(1)}, f32[6,8,128]{2,1,0:T(8,128)}, u32[]{:S(2)}) %copy-start) | copy-done | bytes 24600
  0.8 1.0 %pad_maximum_fusion = f32[8,120,128]{2,1,0:T(8,128)S(1)} fusion(f32[8,24,128]{2,1,0:T(8,128)S(1)} %broadcast_in_dim.2, f32[8,96,128]{2,1,0:T(8,128)} %bitcast.9), kind=kLoop, calls=%fused_computation | loop fusion | flops 122880 | bytes 983040 | tf_op jit(solution)/shard_map/concatenate | solution.py:526
  1.8 20.9 %all_to_all.15.in_ref.half_ref = f32[8,120,128]{2,1,0:T(8,128)S(1)} all-to-all(f32[8,120,128]{2,1,0:T(8,128)S(1)} %pad_maximum_fusion), channel_id=1, replica_groups=mesh['chip'=2,'core'=2,'gx'=4,'gy'=2] {'gx','gy'}, dimensions={0} | all-to-all | bytes 983040 | tf_op jit(solution)/shard_map/all_to_all | solution.py:527
  22.7 0.1 collective-permute-start
  22.8 0.6 laplace.1
  23.4 0.7 %collective-permute-done.other_ref = f32[8,24,128]{2,1,0:T(8,128)S(1)} collective-permute-done((f32[8,24,128]{2,1,0:T(8,128)S(1)}, f32[8,24,128]{2,1,0:T(8,128)S(1)}, u32[]{:S(2)}, u32[]{:S(2)}) %collective-permute-start) | collective-permute-done | bytes 98336 | tf_op jit(solution)/shard_map/ppermute | solution.py:528
  24.1 1.9 %filter.1 = f32[32,24,128]{2,1,0:T(8,128)S(1)} custom-call(f32[2,24,24,128]{3,2,1,0:T(8,128)S(1)} %get-tuple-element.14.field_ref, f32[2,24,16,128]{3,2,1,0:T(8,128)S(1)} %get-tuple-element.15.lap_ref, f32[8,120,128]{2,1,0:T(8,128)S(1)} %all_to_all.15.in_ref.half_ref, f32[8,24,128]{2,1,0:T(8,128)S(1)} %collective-permute-done.other_ref, ...), custom_call_target="tpu_custom_call" | custom-call | tf_op jit(solution)/shard_map/filter/pallas_call | solution.py:298
  26.0 17.0 %all_to_all.16 = f32[32,24,128]{2,1,0:T(8,128)S(1)} all-to-all(f32[32,24,128]{2,1,0:T(8,128)S(1)} %filter.1), channel_id=1, replica_groups=mesh['chip'=2,'core'=2,'gx'=4,'gy'=2] {'chip','core','gx','gy'}, dimensions={0} | all-to-all | bytes 786432 | tf_op jit(solution)/shard_map/all_to_all | solution.py:532
  42.9 0.0 collective-permute-start.2
  42.9 0.9 %collective-permute-start.1 = (f32[768,128]{1,0:T(8,128)S(1)}, f32[768,128]{1,0:T(8,128)S(1)}, u32[]{:S(2)}, u32[]{:S(2)}) collective-permute-start(f32[768,128]{1,0:T(8,128)S(1)} %bitcast.6), channel_id=1, source_target_pairs={{0,16},{16,0},{1,17},{17,1},{2,18},{18,2},{3,19},{19,3},{4,20},{20... | collective-permute-start | bytes 1179656 | tf_op jit(solution)/shard_map/ppermute | solution.py:540
  43.8 0.6 margin.1
  44.4 0.3 collective-permute-done.2.refs_2_
  44.7 11.4 %all_to_all.17.in_ref = f32[32,8,128]{2,1,0:T(8,128)S(1)} all-to-all(f32[32,8,128]{2,1,0:T(8,128)S(1)} %margin.1), channel_id=1, replica_groups=mesh['chip'=2,'core'=2,'gx'=4,'gy'=2] {'chip','core','gx','gy'}, dimensions={0} | all-to-all | bytes 262144 | tf_op jit(solution)/shard_map/all_to_all | solution.py:546
  56.1 0.2 collective-permute-start.3
  56.3 0.0 collective-permute-done.1.refs_1_
  56.3 1.0 %collective-permute-done.3.refs_1_ = f32[8,128]{1,0:T(8,128)S(1)} collective-permute-done((f32[8,128]{1,0:T(8,128)S(1)}, f32[8,128]{1,0:T(8,128)S(1)}, u32[]{:S(2)}, u32[]{:S(2)}) %collective-permute-start.3) | collective-permute-done | bytes 4128 | tf_op jit(solution)/shard_map/ppermute | solution.py:540
  57.4 0.2 collective-permute-start.4
  57.5 1.7 %inverse.1.left_ref = bf16[48,192]{1,0:T(8,128)(2,1)S(1)} custom-call(f32[8,128]{1,0:T(8,128)S(1)} %sum.1.refs_0_, f32[8,128]{1,0:T(8,128)S(1)} %collective-permute-done.3.refs_1_), custom_call_target="tpu_custom_call" | custom-call | tf_op jit(solution)/shard_map/inverse/pallas_call | solution.py:464
  59.2 0.0 collective-permute-done.4.refs_3_
  59.2 1.2 %rotate.1 = f32[768,128]{1,0:T(8,128)} custom-call(bf16[48,192]{1,0:T(8,128)(2,1)S(1)} %inverse.1.left_ref, f32[768,128]{1,0:T(8,128)S(1)} %bitcast.8, f32[768,128]{1,0:T(8,128)S(1)} %collective-permute-done.1.refs_1_, f32[768,128]{1,0:T(8,128)S(1)} %collective-permute-done.2.refs_2_, f32[768,128]{1,0:T(8,128)S(1)} %collective-permute-done.4.refs_3_), custom_call_target="tpu_custom_call" | custom-call | tf_op jit(solution)/shard_map/rotate/pallas_call | solution.py:500
  (4 shorter events, 0.1 us)
Async XLA Ops:
  0.0 0.7 %copy-start = (f32[6,8,128]{2,1,0:T(8,128)S(1)}, f32[6,8,128]{2,1,0:T(8,128)}, u32[]{:S(2)}) copy-start(f32[6,8,128]{2,1,0:T(8,128)} %param.3) | copy-start | bytes 73732
  22.7 1.4 %collective-permute-start = (f32[8,24,128]{2,1,0:T(8,128)S(1)}, f32[8,24,128]{2,1,0:T(8,128)S(1)}, u32[]{:S(2)}, u32[]{:S(2)}) collective-permute-start(f32[8,24,128]{2,1,0:T(8,128)S(1)} %slice.4), channel_id=1, source_target_pairs={{0,8},{8,0},{1,9},{9,1},{2,10},{10,2},{3,11},{11,3},{4,12},{12,4},... | collective-permute-start | bytes 294920 | tf_op jit(solution)/shard_map/ppermute | solution.py:528
  42.9 1.7 %collective-permute-start.2 = (f32[768,128]{1,0:T(8,128)S(1)}, f32[768,128]{1,0:T(8,128)S(1)}, u32[]{:S(2)}, u32[]{:S(2)}) collective-permute-start(f32[768,128]{1,0:T(8,128)S(1)} %bitcast.5), channel_id=1, source_target_pairs={{0,8},{8,0},{1,9},{9,1},{2,10},{10,2},{3,11},{11,3},{4,12},{12,4},... | collective-permute-start | bytes 1179656 | tf_op jit(solution)/shard_map/ppermute | solution.py:544
  42.9 13.4 %collective-permute-start.1 = (f32[768,128]{1,0:T(8,128)S(1)}, f32[768,128]{1,0:T(8,128)S(1)}, u32[]{:S(2)}, u32[]{:S(2)}) collective-permute-start(f32[768,128]{1,0:T(8,128)S(1)} %bitcast.6), channel_id=1, source_target_pairs={{0,16},{16,0},{1,17},{17,1},{2,18},{18,2},{3,19},{19,3},{4,20},{20... | collective-permute-start | bytes 1179656 | tf_op jit(solution)/shard_map/ppermute | solution.py:540
  56.1 1.2 %collective-permute-start.3 = (f32[8,128]{1,0:T(8,128)S(1)}, f32[8,128]{1,0:T(8,128)S(1)}, u32[]{:S(2)}, u32[]{:S(2)}) collective-permute-start(f32[8,128]{1,0:T(8,128)S(1)} %sum.1.refs_0_), channel_id=1, source_target_pairs={{0,8},{8,0},{1,9},{9,1},{2,10},{10,2},{3,11},{11,3},{4,12},{12,4},... | collective-permute-start | bytes 12296 | tf_op jit(solution)/shard_map/ppermute | solution.py:540
  57.4 1.8 %collective-permute-start.4 = (f32[768,128]{1,0:T(8,128)S(1)}, f32[768,128]{1,0:T(8,128)S(1)}, u32[]{:S(2)}, u32[]{:S(2)}) collective-permute-start(f32[768,128]{1,0:T(8,128)S(1)} %collective-permute-done.1.refs_1_), channel_id=1, source_target_pairs={{0,8},{8,0},{1,9},{9,1},{2,10},{10,2},{3,11},{11,3},{4,12},{12,4},... | collective-permute-start | bytes 1179656 | tf_op jit(solution)/shard_map/ppermute | solution.py:549

commit v7 on v6

--- a/solution.py
+++ b/solution.py
@@ -257,13 +257,17 @@
                         piece, row = divmod(in_pencil + r, rows)
                         to = piece_owner(piece, pieces) * gx * gy + g
                         out_ref[to, pl.ds(k * rows + row, TILE // 2), :] = value[r : r + TILE // 2]
-    line = lax.broadcasted_iota(jnp.int32, out_ref.shape[1:], 0)
-    factor = jnp.zeros(out_ref.shape[1:], jnp.float32)
+    scales = []
     for k in range(own):
         mean = jnp.sum(squares[k], keepdims=True) * (1.0 / (width * height * nz))
-        factor = jnp.where(line // rows == k, lax.rsqrt(mean), factor)
-    for to in range(out_ref.shape[0]):
-        out_ref[to] = out_ref[to] * factor
+        scales.append(jnp.broadcast_to(lax.rsqrt(mean), (TILE, nz)))
+    line = lax.broadcasted_iota(jnp.int32, (TILE, nz), 0)
+    for at in range(0, own * rows, TILE):
+        factor = scales[at // rows]
+        for k in range(at // rows + 1, (at + TILE - 1) // rows + 1):
+            factor = jnp.where(line + at < k * rows, factor, scales[k])
+        for to in range(out_ref.shape[0]):
+            out_ref[to, pl.ds(at, TILE), :] = out_ref[to, pl.ds(at, TILE), :] * factor
 
 
 def piece_owner(piece, pieces):
@@ -523,7 +527,8 @@
     flat_potential = potential.reshape(cells, nz)
     half = cells // 2
     own_half = lax.dynamic_slice_in_dim(flat_potential, core * half, half, 0)
-    packed = jnp.concatenate([fields, jnp.broadcast_to(own_half[None], (grid, half, nz))], 1)
+    packed = lax.optimization_barrier(jnp.pad(fields, ((0, 0), (0, half), (0, 0))))
+    packed = packed.at[:, own * cells :, :].set(own_half[None])
     packed = lax.all_to_all(packed, ("gx", "gy"), 0, 0)
     other = lax.ppermute(packed[:, own * cells :, :], "core", swap)
     dims = (gx, gy, own, nx, ny, nz, pieces, own * cells)

time: 60.7 us -> 59.9 us (0.987)
  other arithmetic: 1.03 us -> 0 us
    pad x0 -> x1, local copies, waits for them, and re-layouts: none -> 1.03 us  [on_device_fields(): jnp.pad(fields, ((0, 0), (0, half), (0, 0)))]
    concatenate x1 -> x0, other arithmetic: 1.03 us -> none  [on_device_fields(): jnp.concatenate([fields, jnp.broadcast_to(own_half[None], (grid, half, nz...]
    unnamed x2, local copies, waits for them, and re-layouts: 0.74 us -> 0.01 us
where the time goes in v7:
time: 59.9 us; the launch traced here: 59.7 us
  blocking collectives  49.3 us (82%)
  Pallas kernels  6 us (10%)
  waiting for transfers between devices  2.01 us (3%)
  starting transfers between devices  1.27 us (2%)
  local copies, waits for them, and re-layouts  1.07 us (2%)
    all_to_all x1, blocking collectives, on_device_fields(): packed = lax.all_to_all(packed, ('gx', 'gy'), 0, 0)  20.9 us
    all_to_all x1, blocking collectives, on_device_fields(): lax.all_to_all(filtered, ('chip', 'core', 'gx', 'gy'), 0, 0)  17 us
    all_to_all x1, blocking collectives, on_device_fields(): margins = lax.all_to_all(spread, ('chip', 'core', 'gx', 'gy'), 0, 0)  11.4 us
    pallas_call x1, Pallas kernels, apply_filter(): pl.pallas_call(functools.partial(filter_kernel, dims), out_shape=jax.Shap...  1.88 us
    pallas_call x1, Pallas kernels, inverse_rows(): pl.pallas_call(functools.partial(inverse_kernel, (bands, own)), out_shape...  1.68 us
    pallas_call x1, Pallas kernels, rotate(): pl.pallas_call(functools.partial(rotate_kernel, (bands, own)), out_shape=...  1.23 us
  transfers between devices with their start and end apart: 5, of which 3 were waited for; matrix products, arithmetic and copies ran while one was open for 0% of the time, Pallas kernels for 5%

profile of v7, /device:TPU:0, one launch (start us, length us, event | category | flops | bytes accessed | tf_op | source)
XLA Modules:
  0.0 59.7 jit_solution(13618191611432148128)
XLA Ops:
  0.0 0.0 copy-start
  0.0 1.0 %pad.6 = f32[8,120,128]{2,1,0:T(8,128)S(1)} pad(f32[8,96,128]{2,1,0:T(8,128)} %bitcast.9, f32[]{:T(128)} %constant.35.clone.1), padding=0_0x0_24x0_0 | pad | bytes 884740 | tf_op jit(solution)/shard_map/jit(_pad)/pad | solution.py:530
  1.0 0.0 copy-done
  1.1 20.9 %all_to_all.15.in_ref.half_ref = f32[8,120,128]{2,1,0:T(8,128)S(1)} all-to-all(f32[8,120,128]{2,1,0:T(8,128)S(1)} %broadcast_dynamic-update-slice_fusion), channel_id=1, replica_groups=mesh['chip'=2,'core'=2,'gx'=4,'gy'=2] {'gx','gy'}, dimensions={0} | all-to-all | bytes 983040 | tf_op jit(solution)/shard_map/all_to_all | solution.py:532
  22.0 0.1 collective-permute-start
  22.1 0.6 laplace.1
  22.7 0.7 %collective-permute-done.other_ref = f32[8,24,128]{2,1,0:T(8,128)S(1)} collective-permute-done((f32[8,24,128]{2,1,0:T(8,128)S(1)}, f32[8,24,128]{2,1,0:T(8,128)S(1)}, u32[]{:S(2)}, u32[]{:S(2)}) %collective-permute-start) | collective-permute-done | bytes 98336 | tf_op jit(solution)/shard_map/ppermute | solution.py:533
  23.4 1.9 %filter.1 = f32[32,24,128]{2,1,0:T(8,128)S(1)} custom-call(f32[2,24,24,128]{3,2,1,0:T(8,128)S(1)} %get-tuple-element.26.field_ref, f32[2,24,16,128]{3,2,1,0:T(8,128)S(1)} %get-tuple-element.27.lap_ref, f32[8,120,128]{2,1,0:T(8,128)S(1)} %all_to_all.15.in_ref.half_ref, f32[8,24,128]{2,1,0:T(8,128)S(1)} %collective-permute-done.other_ref, ...), custom_call_target="tpu_custom_call" | custom-call | tf_op jit(solution)/shard_map/filter/pallas_call | solution.py:302
  25.3 17.0 %all_to_all.16 = f32[32,24,128]{2,1,0:T(8,128)S(1)} all-to-all(f32[32,24,128]{2,1,0:T(8,128)S(1)} %filter.1), channel_id=1, replica_groups=mesh['chip'=2,'core'=2,'gx'=4,'gy'=2] {'chip','core','gx','gy'}, dimensions={0} | all-to-all | bytes 786432 | tf_op jit(solution)/shard_map/all_to_all | solution.py:537
  42.2 0.0 collective-permute-start.2
  42.2 0.9 %collective-permute-start.1 = (f32[768,128]{1,0:T(8,128)S(1)}, f32[768,128]{1,0:T(8,128)S(1)}, u32[]{:S(2)}, u32[]{:S(2)}) collective-permute-start(f32[768,128]{1,0:T(8,128)S(1)} %bitcast.6), channel_id=1, source_target_pairs={{0,16},{16,0},{1,17},{17,1},{2,18},{18,2},{3,19},{19,3},{4,20},{20... | collective-permute-start | bytes 1179656 | tf_op jit(solution)/shard_map/ppermute | solution.py:545
  43.1 0.6 %margin.1 = f32[32,8,128]{2,1,0:T(8,128)S(1)} custom-call(f32[768,128]{1,0:T(8,128)S(1)} %bitcast.7), custom_call_target="tpu_custom_call" | custom-call | tf_op jit(solution)/shard_map/margin/pallas_call | solution.py:347
  43.7 0.3 collective-permute-done.2.refs_2_
  43.9 11.4 %all_to_all.17.in_ref = f32[32,8,128]{2,1,0:T(8,128)S(1)} all-to-all(f32[32,8,128]{2,1,0:T(8,128)S(1)} %margin.1), channel_id=1, replica_groups=mesh['chip'=2,'core'=2,'gx'=4,'gy'=2] {'chip','core','gx','gy'}, dimensions={0} | all-to-all | bytes 262144 | tf_op jit(solution)/shard_map/all_to_all | solution.py:551
  55.4 0.2 collective-permute-start.3
  55.6 0.0 collective-permute-done.1.refs_1_
  55.6 1.0 %collective-permute-done.3.refs_1_ = f32[8,128]{1,0:T(8,128)S(1)} collective-permute-done((f32[8,128]{1,0:T(8,128)S(1)}, f32[8,128]{1,0:T(8,128)S(1)}, u32[]{:S(2)}, u32[]{:S(2)}) %collective-permute-start.3) | collective-permute-done | bytes 4128 | tf_op jit(solution)/shard_map/ppermute | solution.py:545
  56.6 0.2 collective-permute-start.4
  56.8 1.7 %inverse.1.left_ref = bf16[48,192]{1,0:T(8,128)(2,1)S(1)} custom-call(f32[8,128]{1,0:T(8,128)S(1)} %sum.1.refs_0_, f32[8,128]{1,0:T(8,128)S(1)} %collective-permute-done.3.refs_1_), custom_call_target="tpu_custom_call" | custom-call | tf_op jit(solution)/shard_map/inverse/pallas_call | solution.py:468
  58.5 0.0 collective-permute-done.4.refs_3_
  58.5 1.2 %rotate.1 = f32[768,128]{1,0:T(8,128)} custom-call(bf16[48,192]{1,0:T(8,128)(2,1)S(1)} %inverse.1.left_ref, f32[768,128]{1,0:T(8,128)S(1)} %bitcast.8, f32[768,128]{1,0:T(8,128)S(1)} %collective-permute-done.1.refs_1_, f32[768,128]{1,0:T(8,128)S(1)} %collective-permute-done.2.refs_2_, f32[768,128]{1,0:T(8,128)S(1)} %collective-permute-done.4.refs_3_), custom_call_target="tpu_custom_call" | custom-call | tf_op jit(solution)/shard_map/rotate/pallas_call | solution.py:504
  (4 shorter events, 0.1 us)
Async XLA Ops:
  0.0 1.0 %copy-start = (f32[6,8,128]{2,1,0:T(8,128)S(1)}, f32[6,8,128]{2,1,0:T(8,128)}, u32[]{:S(2)}) copy-start(f32[6,8,128]{2,1,0:T(8,128)} %param.5) | copy-start | bytes 73732
  22.0 1.4 %collective-permute-start = (f32[8,24,128]{2,1,0:T(8,128)S(1)}, f32[8,24,128]{2,1,0:T(8,128)S(1)}, u32[]{:S(2)}, u32[]{:S(2)}) collective-permute-start(f32[8,24,128]{2,1,0:T(8,128)S(1)} %slice.26), channel_id=1, source_target_pairs={{0,8},{8,0},{1,9},{9,1},{2,10},{10,2},{3,11},{11,3},{4,12},{12,4},... | collective-permute-start | bytes 294920 | tf_op jit(solution)/shard_map/ppermute | solution.py:533
  42.2 1.7 %collective-permute-start.2 = (f32[768,128]{1,0:T(8,128)S(1)}, f32[768,128]{1,0:T(8,128)S(1)}, u32[]{:S(2)}, u32[]{:S(2)}) collective-permute-start(f32[768,128]{1,0:T(8,128)S(1)} %bitcast.5), channel_id=1, source_target_pairs={{0,8},{8,0},{1,9},{9,1},{2,10},{10,2},{3,11},{11,3},{4,12},{12,4},... | collective-permute-start | bytes 1179656 | tf_op jit(solution)/shard_map/ppermute | solution.py:549
  42.2 13.4 %collective-permute-start.1 = (f32[768,128]{1,0:T(8,128)S(1)}, f32[768,128]{1,0:T(8,128)S(1)}, u32[]{:S(2)}, u32[]{:S(2)}) collective-permute-start(f32[768,128]{1,0:T(8,128)S(1)} %bitcast.6), channel_id=1, source_target_pairs={{0,16},{16,0},{1,17},{17,1},{2,18},{18,2},{3,19},{19,3},{4,20},{20... | collective-permute-start | bytes 1179656 | tf_op jit(solution)/shard_map/ppermute | solution.py:545
  55.4 1.2 %collective-permute-start.3 = (f32[8,128]{1,0:T(8,128)S(1)}, f32[8,128]{1,0:T(8,128)S(1)}, u32[]{:S(2)}, u32[]{:S(2)}) collective-permute-start(f32[8,128]{1,0:T(8,128)S(1)} %sum.1.refs_0_), channel_id=1, source_target_pairs={{0,8},{8,0},{1,9},{9,1},{2,10},{10,2},{3,11},{11,3},{4,12},{12,4},... | collective-permute-start | bytes 12296 | tf_op jit(solution)/shard_map/ppermute | solution.py:545
  56.6 1.8 %collective-permute-start.4 = (f32[768,128]{1,0:T(8,128)S(1)}, f32[768,128]{1,0:T(8,128)S(1)}, u32[]{:S(2)}, u32[]{:S(2)}) collective-permute-start(f32[768,128]{1,0:T(8,128)S(1)} %collective-permute-done.1.refs_1_), channel_id=1, source_target_pairs={{0,8},{8,0},{1,9},{9,1},{2,10},{10,2},{3,11},{11,3},{4,12},{12,4},... | collective-permute-start | bytes 1179656 | tf_op jit(solution)/shard_map/ppermute | solution.py:554

commit v8 on v7

--- a/solution.py
+++ b/solution.py
@@ -196,7 +196,7 @@
     w2_ref[pl.ds(0, nz), :] = high
     w2_ref[pl.ds(nz, nz), :] = low
     for g in range(gx * gy):
-        at_x, at_y = (g // gy) * nx, (g % gy) * ny
+        at_x, at_y = (g % gx) * nx, (g // gx) * ny
         for k in range(own):
             for i in range(nx):
                 for t in range(ny // TILE):
@@ -238,7 +238,7 @@
         for k in range(own):
             for x, centres, totals in along_xy(src, k, height, bool(step)):
                 for tile in range(height // TILE):
-                    g = (x // nx) * gy + tile * TILE // ny
+                    g = (tile * TILE // ny) * gx + x // nx
                     in_pencil = (x % nx) * ny + (tile * TILE) % ny
                     plain = pl.ds(tile * TILE, TILE)
                     if step:
@@ -529,12 +529,12 @@
     own_half = lax.dynamic_slice_in_dim(flat_potential, core * half, half, 0)
     packed = lax.optimization_barrier(jnp.pad(fields, ((0, 0), (0, half), (0, 0))))
     packed = packed.at[:, own * cells :, :].set(own_half[None])
-    packed = lax.all_to_all(packed, ("gx", "gy"), 0, 0)
+    packed = lax.all_to_all(packed, ("gy", "gx"), 0, 0)
     other = lax.ppermute(packed[:, own * cells :, :], "core", swap)
     dims = (gx, gy, own, nx, ny, nz, pieces, own * cells)
     field, laplace, *weights = first_laplace(packed, dims)
     filtered = apply_filter(field, laplace, packed, other, weights, dims)
-    blocks = lax.all_to_all(filtered, ("chip", "core", "gx", "gy"), 0, 0).reshape(bands * rows, nz)
+    blocks = lax.all_to_all(filtered, ("chip", "core", "gy", "gx"), 0, 0).reshape(bands * rows, nz)
 
     def tied(value, first):
         return lax.optimization_barrier((value, first))[0]

time: 59.9 us -> 58.8 us (0.982)
  blocking collectives: 49.3 us -> 48 us
    all_to_all x2, blocking collectives: 37.9 us -> 36.7 us  [the longest x1 21.8 us: on_device_fields(): packed = lax.all_to_all(packed, ('gy', 'gx'), 0, 0)]
  transfers between devices with their start and end apart: 5 -> 5, of which waited for: 3 -> 2; matrix products, arithmetic and copies ran while one was open for 0% -> 0% of each run, Pallas kernels for 5% -> 5%
where the time goes in v8:
time: 58.8 us; the launch traced here: 58.6 us
  blocking collectives  48 us (82%)
  Pallas kernels  5.98 us (10%)
  waiting for transfers between devices  1.75 us (3%)
  starting transfers between devices  1.69 us (3%)
  local copies, waits for them, and re-layouts  1.07 us (2%)
    all_to_all x1, blocking collectives, on_device_fields(): packed = lax.all_to_all(packed, ('gy', 'gx'), 0, 0)  21.8 us
    all_to_all x1, blocking collectives, on_device_fields(): lax.all_to_all(filtered, ('chip', 'core', 'gy', 'gx'), 0, 0)  14.9 us
    all_to_all x1, blocking collectives, on_device_fields(): margins = lax.all_to_all(spread, ('chip', 'core', 'gx', 'gy'), 0, 0)  11.4 us
    pallas_call x1, Pallas kernels, apply_filter(): pl.pallas_call(functools.partial(filter_kernel, dims), out_shape=jax.Shap...  1.87 us
    pallas_call x1, Pallas kernels, inverse_rows(): pl.pallas_call(functools.partial(inverse_kernel, (bands, own)), out_shape...  1.68 us
    pallas_call x1, Pallas kernels, rotate(): pl.pallas_call(functools.partial(rotate_kernel, (bands, own)), out_shape=...  1.22 us
    ppermute x2, starting transfers between devices, copies(): return [value] + [lax.ppermute(value, axes, pair) for pair in pairs]  1.18 us
  transfers between devices with their start and end apart: 5, of which 2 were waited for; matrix products, arithmetic and copies ran while one was open for 0% of the time, Pallas kernels for 5%

profile of v8, /device:TPU:0, one launch (start us, length us, event | category | flops | bytes accessed | tf_op | source)
XLA Modules:
  0.0 58.6 jit_solution(4203646017831440445)
XLA Ops:
  0.0 0.0 copy-start
  0.0 1.0 %pad.6 = f32[8,120,128]{2,1,0:T(8,128)S(1)} pad(f32[8,96,128]{2,1,0:T(8,128)} %bitcast.9, f32[]{:T(128)} %constant.35.clone.1), padding=0_0x0_24x0_0 | pad | bytes 884740 | tf_op jit(solution)/shard_map/jit(_pad)/pad | solution.py:530
  1.0 0.0 copy-done
  1.1 21.8 %all_to_all.15.in_ref.half_ref = f32[8,120,128]{2,1,0:T(8,128)S(1)} all-to-all(f32[8,120,128]{2,1,0:T(8,128)S(1)} %broadcast_dynamic-update-slice_fusion), channel_id=1, replica_groups=mesh['chip'=2,'core'=2,'gx'=4,'gy'=2] {'gy','gx'}, dimensions={0} | all-to-all | bytes 983040 | tf_op jit(solution)/shard_map/all_to_all | solution.py:532
  22.9 0.1 collective-permute-start
  22.9 0.6 laplace.1
  23.5 0.7 %collective-permute-done.other_ref = f32[8,24,128]{2,1,0:T(8,128)S(1)} collective-permute-done((f32[8,24,128]{2,1,0:T(8,128)S(1)}, f32[8,24,128]{2,1,0:T(8,128)S(1)}, u32[]{:S(2)}, u32[]{:S(2)}) %collective-permute-start) | collective-permute-done | bytes 98336 | tf_op jit(solution)/shard_map/ppermute | solution.py:533
  24.2 1.9 %filter.1 = f32[32,24,128]{2,1,0:T(8,128)S(1)} custom-call(f32[2,24,24,128]{3,2,1,0:T(8,128)S(1)} %get-tuple-element.26.field_ref, f32[2,24,16,128]{3,2,1,0:T(8,128)S(1)} %get-tuple-element.27.lap_ref, f32[8,120,128]{2,1,0:T(8,128)S(1)} %all_to_all.15.in_ref.half_ref, f32[8,24,128]{2,1,0:T(8,128)S(1)} %collective-permute-done.other_ref, ...), custom_call_target="tpu_custom_call" | custom-call | tf_op jit(solution)/shard_map/filter/pallas_call | solution.py:302
  26.1 14.9 %all_to_all.16 = f32[32,24,128]{2,1,0:T(8,128)S(1)} all-to-all(f32[32,24,128]{2,1,0:T(8,128)S(1)} %filter.1), channel_id=1, replica_groups=mesh['chip'=2,'core'=2,'gx'=4,'gy'=2] {'chip','core','gy','gx'}, dimensions={0} | all-to-all | bytes 786432 | tf_op jit(solution)/shard_map/all_to_all | solution.py:537
  41.0 0.3 collective-permute-start.2
  41.3 1.0 %collective-permute-start.1 = (f32[768,128]{1,0:T(8,128)S(1)}, f32[768,128]{1,0:T(8,128)S(1)}, u32[]{:S(2)}, u32[]{:S(2)}) collective-permute-start(f32[768,128]{1,0:T(8,128)S(1)} %bitcast.6), channel_id=1, source_target_pairs={{0,16},{16,0},{1,17},{17,1},{2,18},{18,2},{3,19},{19,3},{4,20},{20... | collective-permute-start | bytes 1179656 | tf_op jit(solution)/shard_map/ppermute | solution.py:545
  42.3 0.6 %margin.1 = f32[32,8,128]{2,1,0:T(8,128)S(1)} custom-call(f32[768,128]{1,0:T(8,128)S(1)} %bitcast.7), custom_call_target="tpu_custom_call" | custom-call | tf_op jit(solution)/shard_map/margin/pallas_call | solution.py:347
  42.9 0.0 collective-permute-done.2.refs_2_
  42.9 11.4 %all_to_all.17.in_ref = f32[32,8,128]{2,1,0:T(8,128)S(1)} all-to-all(f32[32,8,128]{2,1,0:T(8,128)S(1)} %margin.1), channel_id=1, replica_groups=mesh['chip'=2,'core'=2,'gx'=4,'gy'=2] {'chip','core','gx','gy'}, dimensions={0} | all-to-all | bytes 262144 | tf_op jit(solution)/shard_map/all_to_all | solution.py:551
  54.3 0.2 collective-permute-start.3
  54.5 0.0 collective-permute-done.1.refs_1_
  54.5 1.0 %collective-permute-done.3.refs_1_ = f32[8,128]{1,0:T(8,128)S(1)} collective-permute-done((f32[8,128]{1,0:T(8,128)S(1)}, f32[8,128]{1,0:T(8,128)S(1)}, u32[]{:S(2)}, u32[]{:S(2)}) %collective-permute-start.3) | collective-permute-done | bytes 4128 | tf_op jit(solution)/shard_map/ppermute | solution.py:545
  55.5 0.2 collective-permute-start.4
  55.7 1.7 %inverse.1.left_ref = bf16[48,192]{1,0:T(8,128)(2,1)S(1)} custom-call(f32[8,128]{1,0:T(8,128)S(1)} %sum.1.refs_0_, f32[8,128]{1,0:T(8,128)S(1)} %collective-permute-done.3.refs_1_), custom_call_target="tpu_custom_call" | custom-call | tf_op jit(solution)/shard_map/inverse/pallas_call | solution.py:468
  57.4 0.0 collective-permute-done.4.refs_3_
  57.4 1.2 %rotate.1 = f32[768,128]{1,0:T(8,128)} custom-call(bf16[48,192]{1,0:T(8,128)(2,1)S(1)} %inverse.1.left_ref, f32[768,128]{1,0:T(8,128)S(1)} %bitcast.8, f32[768,128]{1,0:T(8,128)S(1)} %collective-permute-done.1.refs_1_, f32[768,128]{1,0:T(8,128)S(1)} %collective-permute-done.2.refs_2_, f32[768,128]{1,0:T(8,128)S(1)} %collective-permute-done.4.refs_3_), custom_call_target="tpu_custom_call" | custom-call | tf_op jit(solution)/shard_map/rotate/pallas_call | solution.py:504
  (4 shorter events, 0.1 us)
Async XLA Ops:
  0.0 1.0 %copy-start = (f32[6,8,128]{2,1,0:T(8,128)S(1)}, f32[6,8,128]{2,1,0:T(8,128)}, u32[]{:S(2)}) copy-start(f32[6,8,128]{2,1,0:T(8,128)} %param.5) | copy-start | bytes 73732
  22.9 1.4 %collective-permute-start = (f32[8,24,128]{2,1,0:T(8,128)S(1)}, f32[8,24,128]{2,1,0:T(8,128)S(1)}, u32[]{:S(2)}, u32[]{:S(2)}) collective-permute-start(f32[8,24,128]{2,1,0:T(8,128)S(1)} %slice.26), channel_id=1, source_target_pairs={{0,8},{8,0},{1,9},{9,1},{2,10},{10,2},{3,11},{11,3},{4,12},{12,4},... | collective-permute-start | bytes 294920 | tf_op jit(solution)/shard_map/ppermute | solution.py:533
  41.0 1.9 %collective-permute-start.2 = (f32[768,128]{1,0:T(8,128)S(1)}, f32[768,128]{1,0:T(8,128)S(1)}, u32[]{:S(2)}, u32[]{:S(2)}) collective-permute-start(f32[768,128]{1,0:T(8,128)S(1)} %bitcast.5), channel_id=1, source_target_pairs={{0,8},{8,0},{1,9},{9,1},{2,10},{10,2},{3,11},{11,3},{4,12},{12,4},... | collective-permute-start | bytes 1179656 | tf_op jit(solution)/shard_map/ppermute | solution.py:549
  41.3 13.2 %collective-permute-start.1 = (f32[768,128]{1,0:T(8,128)S(1)}, f32[768,128]{1,0:T(8,128)S(1)}, u32[]{:S(2)}, u32[]{:S(2)}) collective-permute-start(f32[768,128]{1,0:T(8,128)S(1)} %bitcast.6), channel_id=1, source_target_pairs={{0,16},{16,0},{1,17},{17,1},{2,18},{18,2},{3,19},{19,3},{4,20},{20... | collective-permute-start | bytes 1179656 | tf_op jit(solution)/shard_map/ppermute | solution.py:545
  54.3 1.2 %collective-permute-start.3 = (f32[8,128]{1,0:T(8,128)S(1)}, f32[8,128]{1,0:T(8,128)S(1)}, u32[]{:S(2)}, u32[]{:S(2)}) collective-permute-start(f32[8,128]{1,0:T(8,128)S(1)} %sum.1.refs_0_), channel_id=1, source_target_pairs={{0,8},{8,0},{1,9},{9,1},{2,10},{10,2},{3,11},{11,3},{4,12},{12,4},... | collective-permute-start | bytes 12296 | tf_op jit(solution)/shard_map/ppermute | solution.py:545
  55.5 1.8 %collective-permute-start.4 = (f32[768,128]{1,0:T(8,128)S(1)}, f32[768,128]{1,0:T(8,128)S(1)}, u32[]{:S(2)}, u32[]{:S(2)}) collective-permute-start(f32[768,128]{1,0:T(8,128)S(1)} %collective-permute-done.1.refs_1_), channel_id=1, source_target_pairs={{0,8},{8,0},{1,9},{9,1},{2,10},{10,2},{3,11},{11,3},{4,12},{12,4},... | collective-permute-start | bytes 1179656 | tf_op jit(solution)/shard_map/ppermute | solution.py:554

commit v9 on v8

--- a/solution.py
+++ b/solution.py
@@ -546,10 +546,9 @@
 
     spread = partial_margin(blocks, bands, 1.0 / (cells * nz * grid), pieces, grid)
     parts = copies(blocks, "chip")
-    crossed = [lax.ppermute(blocks, "core", swap)]
-    crossed, spread = lax.optimization_barrier((crossed, spread))
     margins = lax.all_to_all(spread, ("chip", "core", "gx", "gy"), 0, 0)
     margins = copies(sum_first(margins), "core")
+    crossed = [lax.ppermute(tied(blocks, margins[0]), "core", swap)]
     far, margins = lax.optimization_barrier((parts[1:], margins))
     parts += crossed + [lax.ppermute(part, "core", swap) for part in far]
     left = inverse_rows(margins, own_bands, bands)

time: 58.8 us -> 58.4 us (level)
  no operation moved by 1% of the time
where the time goes in v9:
time: 58.4 us; the launch traced here: 58.2 us
  blocking collectives  47.7 us (82%)
  Pallas kernels  5.98 us (10%)
  starting transfers between devices  2.08 us (4%)
  waiting for transfers between devices  1.36 us (2%)
  local copies, waits for them, and re-layouts  1.07 us (2%)
    all_to_all x1, blocking collectives, on_device_fields(): packed = lax.all_to_all(packed, ('gy', 'gx'), 0, 0)  21.8 us
    all_to_all x1, blocking collectives, on_device_fields(): lax.all_to_all(filtered, ('chip', 'core', 'gy', 'gx'), 0, 0)  14.9 us
    all_to_all x1, blocking collectives, on_device_fields(): margins = lax.all_to_all(spread, ('chip', 'core', 'gx', 'gy'), 0, 0)  11 us
    pallas_call x1, Pallas kernels, apply_filter(): pl.pallas_call(functools.partial(filter_kernel, dims), out_shape=jax.Shap...  1.87 us
    pallas_call x1, Pallas kernels, inverse_rows(): pl.pallas_call(functools.partial(inverse_kernel, (bands, own)), out_shape...  1.68 us
    ppermute x2, starting transfers between devices, copies(): return [value] + [lax.ppermute(value, axes, pair) for pair in pairs]  1.45 us
    pallas_call x1, Pallas kernels, rotate(): pl.pallas_call(functools.partial(rotate_kernel, (bands, own)), out_shape=...  1.23 us
  transfers between devices with their start and end apart: 5, of which 2 were waited for; matrix products, arithmetic and copies ran while one was open for 0% of the time, Pallas kernels for 5%

profile of v9, /device:TPU:0, one launch (start us, length us, event | category | flops | bytes accessed | tf_op | source)
XLA Modules:
  0.0 58.2 jit_solution(3582903449991599021)
XLA Ops:
  0.0 0.0 copy-start
  0.0 1.0 %pad.6 = f32[8,120,128]{2,1,0:T(8,128)S(1)} pad(f32[8,96,128]{2,1,0:T(8,128)} %bitcast.9, f32[]{:T(128)} %constant.35.clone.1), padding=0_0x0_24x0_0 | pad | bytes 884740 | tf_op jit(solution)/shard_map/jit(_pad)/pad | solution.py:530
  1.0 0.0 copy-done
  1.1 21.8 %all_to_all.15.in_ref.half_ref = f32[8,120,128]{2,1,0:T(8,128)S(1)} all-to-all(f32[8,120,128]{2,1,0:T(8,128)S(1)} %broadcast_dynamic-update-slice_fusion), channel_id=1, replica_groups=mesh['chip'=2,'core'=2,'gx'=4,'gy'=2] {'gy','gx'}, dimensions={0} | all-to-all | bytes 983040 | tf_op jit(solution)/shard_map/all_to_all | solution.py:532
  22.9 0.1 collective-permute-start
  22.9 0.6 laplace.1
  23.5 0.7 %collective-permute-done.other_ref = f32[8,24,128]{2,1,0:T(8,128)S(1)} collective-permute-done((f32[8,24,128]{2,1,0:T(8,128)S(1)}, f32[8,24,128]{2,1,0:T(8,128)S(1)}, u32[]{:S(2)}, u32[]{:S(2)}) %collective-permute-start) | collective-permute-done | bytes 98336 | tf_op jit(solution)/shard_map/ppermute | solution.py:533
  24.2 1.9 %filter.1 = f32[32,24,128]{2,1,0:T(8,128)S(1)} custom-call(f32[2,24,24,128]{3,2,1,0:T(8,128)S(1)} %get-tuple-element.25.field_ref, f32[2,24,16,128]{3,2,1,0:T(8,128)S(1)} %get-tuple-element.26.lap_ref, f32[8,120,128]{2,1,0:T(8,128)S(1)} %all_to_all.15.in_ref.half_ref, f32[8,24,128]{2,1,0:T(8,128)S(1)} %collective-permute-done.other_ref, ...), custom_call_target="tpu_custom_call" | custom-call | tf_op jit(solution)/shard_map/filter/pallas_call | solution.py:302
  26.1 14.9 %all_to_all.16 = f32[32,24,128]{2,1,0:T(8,128)S(1)} all-to-all(f32[32,24,128]{2,1,0:T(8,128)S(1)} %filter.1), channel_id=1, replica_groups=mesh['chip'=2,'core'=2,'gx'=4,'gy'=2] {'chip','core','gy','gx'}, dimensions={0} | all-to-all | bytes 786432 | tf_op jit(solution)/shard_map/all_to_all | solution.py:537
  41.0 1.3 %collective-permute-start.1 = (f32[768,128]{1,0:T(8,128)S(1)}, f32[768,128]{1,0:T(8,128)S(1)}, u32[]{:S(2)}, u32[]{:S(2)}) collective-permute-start(f32[768,128]{1,0:T(8,128)S(1)} %bitcast.5), channel_id=1, source_target_pairs={{0,16},{16,0},{1,17},{17,1},{2,18},{18,2},{3,19},{19,3},{4,20},{20... | collective-permute-start | bytes 1179656 | tf_op jit(solution)/shard_map/ppermute | solution.py:545
  42.3 0.6 %margin.1 = f32[32,8,128]{2,1,0:T(8,128)S(1)} custom-call(f32[768,128]{1,0:T(8,128)S(1)} %bitcast.6), custom_call_target="tpu_custom_call" | custom-call | tf_op jit(solution)/shard_map/margin/pallas_call | solution.py:347
  42.9 11.0 %all_to_all.17.in_ref = f32[32,8,128]{2,1,0:T(8,128)S(1)} all-to-all(f32[32,8,128]{2,1,0:T(8,128)S(1)} %margin.1), channel_id=1, replica_groups=mesh['chip'=2,'core'=2,'gx'=4,'gy'=2] {'chip','core','gx','gy'}, dimensions={0} | all-to-all | bytes 262144 | tf_op jit(solution)/shard_map/all_to_all | solution.py:549
  53.9 0.2 collective-permute-start.2
  54.1 0.4 collective-permute-start.3
  54.5 0.7 %collective-permute-done.2.refs_1_ = f32[8,128]{1,0:T(8,128)S(1)} collective-permute-done((f32[8,128]{1,0:T(8,128)S(1)}, f32[8,128]{1,0:T(8,128)S(1)}, u32[]{:S(2)}, u32[]{:S(2)}) %collective-permute-start.2) | collective-permute-done | bytes 4128 | tf_op jit(solution)/shard_map/ppermute | solution.py:545
  55.1 0.0 collective-permute-done.1.refs_1_
  55.1 0.2 collective-permute-start.4
  55.3 1.7 %inverse.1.left_ref = bf16[48,192]{1,0:T(8,128)(2,1)S(1)} custom-call(f32[8,128]{1,0:T(8,128)S(1)} %sum.1.refs_0_, f32[8,128]{1,0:T(8,128)S(1)} %collective-permute-done.2.refs_1_), custom_call_target="tpu_custom_call" | custom-call | tf_op jit(solution)/shard_map/inverse/pallas_call | solution.py:468
  57.0 0.0 collective-permute-done.3.refs_2_
  57.0 0.0 collective-permute-done.4.refs_3_
  57.0 1.2 %rotate.1 = f32[768,128]{1,0:T(8,128)} custom-call(bf16[48,192]{1,0:T(8,128)(2,1)S(1)} %inverse.1.left_ref, f32[768,128]{1,0:T(8,128)S(1)} %bitcast.8, f32[768,128]{1,0:T(8,128)S(1)} %collective-permute-done.1.refs_1_, f32[768,128]{1,0:T(8,128)S(1)} %collective-permute-done.3.refs_2_, f32[768,128]{1,0:T(8,128)S(1)} %collective-permute-done.4.refs_3_), custom_call_target="tpu_custom_call" | custom-call | tf_op jit(solution)/shard_map/rotate/pallas_call | solution.py:504
  (4 shorter events, 0.1 us)
Async XLA Ops:
  0.0 1.0 %copy-start = (f32[6,8,128]{2,1,0:T(8,128)S(1)}, f32[6,8,128]{2,1,0:T(8,128)}, u32[]{:S(2)}) copy-start(f32[6,8,128]{2,1,0:T(8,128)} %param.5) | copy-start | bytes 73732
  22.9 1.4 %collective-permute-start = (f32[8,24,128]{2,1,0:T(8,128)S(1)}, f32[8,24,128]{2,1,0:T(8,128)S(1)}, u32[]{:S(2)}, u32[]{:S(2)}) collective-permute-start(f32[8,24,128]{2,1,0:T(8,128)S(1)} %slice.26), channel_id=1, source_target_pairs={{0,8},{8,0},{1,9},{9,1},{2,10},{10,2},{3,11},{11,3},{4,12},{12,4},... | collective-permute-start | bytes 294920 | tf_op jit(solution)/shard_map/ppermute | solution.py:533
  41.0 14.1 %collective-permute-start.1 = (f32[768,128]{1,0:T(8,128)S(1)}, f32[768,128]{1,0:T(8,128)S(1)}, u32[]{:S(2)}, u32[]{:S(2)}) collective-permute-start(f32[768,128]{1,0:T(8,128)S(1)} %bitcast.5), channel_id=1, source_target_pairs={{0,16},{16,0},{1,17},{17,1},{2,18},{18,2},{3,19},{19,3},{4,20},{20... | collective-permute-start | bytes 1179656 | tf_op jit(solution)/shard_map/ppermute | solution.py:545
  53.9 1.2 %collective-permute-start.2 = (f32[8,128]{1,0:T(8,128)S(1)}, f32[8,128]{1,0:T(8,128)S(1)}, u32[]{:S(2)}, u32[]{:S(2)}) collective-permute-start(f32[8,128]{1,0:T(8,128)S(1)} %sum.1.refs_0_), channel_id=1, source_target_pairs={{0,8},{8,0},{1,9},{9,1},{2,10},{10,2},{3,11},{11,3},{4,12},{12,4},... | collective-permute-start | bytes 12296 | tf_op jit(solution)/shard_map/ppermute | solution.py:545
  54.1 2.9 %collective-permute-start.3 = (f32[768,128]{1,0:T(8,128)S(1)}, f32[768,128]{1,0:T(8,128)S(1)}, u32[]{:S(2)}, u32[]{:S(2)}) collective-permute-start(f32[768,128]{1,0:T(8,128)S(1)} %bitcast.7), channel_id=1, source_target_pairs={{0,8},{8,0},{1,9},{9,1},{2,10},{10,2},{3,11},{11,3},{4,12},{12,4},... | collective-permute-start | bytes 1179656 | tf_op jit(solution)/shard_map/ppermute | solution.py:551
  55.1 1.9 %collective-permute-start.4 = (f32[768,128]{1,0:T(8,128)S(1)}, f32[768,128]{1,0:T(8,128)S(1)}, u32[]{:S(2)}, u32[]{:S(2)}) collective-permute-start(f32[768,128]{1,0:T(8,128)S(1)} %collective-permute-done.1.refs_1_), channel_id=1, source_target_pairs={{0,8},{8,0},{1,9},{9,1},{2,10},{10,2},{3,11},{11,3},{4,12},{12,4},... | collective-permute-start | bytes 1179656 | tf_op jit(solution)/shard_map/ppermute | solution.py:553

commit v10 on v9

--- a/solution.py
+++ b/solution.py
@@ -403,8 +403,9 @@
             pivots = pivot if j == 0 else jnp.where(lines == j, pivot, pivots)
             ratio = pl.reciprocal(pivot, approx=True)
             for c in range(j + 1, TILE):
+                scaled = square[j][c] * ratio
                 for d in range(c, TILE):
-                    square[c][d] = square[c][d] - (square[j][c] * square[j][d]) * ratio
+                    square[c][d] = square[c][d] - scaled * square[j][d]
             factor = {t: panel[j][t] * ratio for t in range(p + 1, tiles)}
             factor[p] = jnp.where(lines > j, heads[j] * ratio, 0.0)
             for c in range(j + 1, TILE):

time: 58.4 us -> 58.3 us (level)
  no operation moved by 1% of the time
where the time goes in v10:
time: 58.3 us; the launch traced here: 58.1 us
  blocking collectives  47.7 us (82%)
  Pallas kernels  5.9 us (10%)
  starting transfers between devices  2.08 us (4%)
  waiting for transfers between devices  1.36 us (2%)
  local copies, waits for them, and re-layouts  1.07 us (2%)
    all_to_all x1, blocking collectives, on_device_fields(): packed = lax.all_to_all(packed, ('gy', 'gx'), 0, 0)  21.8 us
    all_to_all x1, blocking collectives, on_device_fields(): lax.all_to_all(filtered, ('chip', 'core', 'gy', 'gx'), 0, 0)  14.9 us
    all_to_all x1, blocking collectives, on_device_fields(): margins = lax.all_to_all(spread, ('chip', 'core', 'gx', 'gy'), 0, 0)  11 us
    pallas_call x1, Pallas kernels, apply_filter(): pl.pallas_call(functools.partial(filter_kernel, dims), out_shape=jax.Shap...  1.87 us
    pallas_call x1, Pallas kernels, inverse_rows(): pl.pallas_call(functools.partial(inverse_kernel, (bands, own)), out_shape...  1.59 us
    ppermute x2, starting transfers between devices, copies(): return [value] + [lax.ppermute(value, axes, pair) for pair in pairs]  1.45 us
    pallas_call x1, Pallas kernels, rotate(): pl.pallas_call(functools.partial(rotate_kernel, (bands, own)), out_shape=...  1.22 us
  transfers between devices with their start and end apart: 5, of which 2 were waited for; matrix products, arithmetic and copies ran while one was open for 0% of the time, Pallas kernels for 5%

profile of v10, /device:TPU:0, one launch (start us, length us, event | category | flops | bytes accessed | tf_op | source)
XLA Modules:
  0.0 58.1 jit_solution(3046222832359773266)
XLA Ops:
  0.0 0.0 copy-start
  0.0 1.0 %pad.6 = f32[8,120,128]{2,1,0:T(8,128)S(1)} pad(f32[8,96,128]{2,1,0:T(8,128)} %bitcast.9, f32[]{:T(128)} %constant.35.clone.1), padding=0_0x0_24x0_0 | pad | bytes 884740 | tf_op jit(solution)/shard_map/jit(_pad)/pad | solution.py:531
  1.0 0.0 copy-done
  1.1 21.8 %all_to_all.15.in_ref.half_ref = f32[8,120,128]{2,1,0:T(8,128)S(1)} all-to-all(f32[8,120,128]{2,1,0:T(8,128)S(1)} %broadcast_dynamic-update-slice_fusion), channel_id=1, replica_groups=mesh['chip'=2,'core'=2,'gx'=4,'gy'=2] {'gy','gx'}, dimensions={0} | all-to-all | bytes 983040 | tf_op jit(solution)/shard_map/all_to_all | solution.py:533
  22.9 0.1 collective-permute-start
  22.9 0.6 %laplace.1 = (f32[2,24,24,128]{3,2,1,0:T(8,128)S(1)}, f32[2,24,16,128]{3,2,1,0:T(8,128)S(1)}, bf16[256,256]{1,0:T(8,128)(2,1)S(1)}, bf16[256,128]{1,0:T(8,128)(2,1)S(1)}) custom-call(f32[8,120,128]{2,1,0:T(8,128)S(1)} %all_to_all.15.in_ref.half_ref), custom_call_target="tpu_custom_call" | custom-call | flops 4325376 | bytes 1572864 | tf_op jit(solution)/shard_map/laplace/pallas_call | solution.py:283
  23.5 0.7 %collective-permute-done.other_ref = f32[8,24,128]{2,1,0:T(8,128)S(1)} collective-permute-done((f32[8,24,128]{2,1,0:T(8,128)S(1)}, f32[8,24,128]{2,1,0:T(8,128)S(1)}, u32[]{:S(2)}, u32[]{:S(2)}) %collective-permute-start) | collective-permute-done | bytes 98336 | tf_op jit(solution)/shard_map/ppermute | solution.py:534
  24.2 1.9 %filter.1 = f32[32,24,128]{2,1,0:T(8,128)S(1)} custom-call(f32[2,24,24,128]{3,2,1,0:T(8,128)S(1)} %get-tuple-element.25.field_ref, f32[2,24,16,128]{3,2,1,0:T(8,128)S(1)} %get-tuple-element.26.lap_ref, f32[8,120,128]{2,1,0:T(8,128)S(1)} %all_to_all.15.in_ref.half_ref, f32[8,24,128]{2,1,0:T(8,128)S(1)} %collective-permute-done.other_ref, ...), custom_call_target="tpu_custom_call" | custom-call | tf_op jit(solution)/shard_map/filter/pallas_call | solution.py:302
  26.1 14.9 %all_to_all.16 = f32[32,24,128]{2,1,0:T(8,128)S(1)} all-to-all(f32[32,24,128]{2,1,0:T(8,128)S(1)} %filter.1), channel_id=1, replica_groups=mesh['chip'=2,'core'=2,'gx'=4,'gy'=2] {'chip','core','gy','gx'}, dimensions={0} | all-to-all | bytes 786432 | tf_op jit(solution)/shard_map/all_to_all | solution.py:538
  41.0 1.3 %collective-permute-start.1 = (f32[768,128]{1,0:T(8,128)S(1)}, f32[768,128]{1,0:T(8,128)S(1)}, u32[]{:S(2)}, u32[]{:S(2)}) collective-permute-start(f32[768,128]{1,0:T(8,128)S(1)} %bitcast.5), channel_id=1, source_target_pairs={{0,16},{16,0},{1,17},{17,1},{2,18},{18,2},{3,19},{19,3},{4,20},{20... | collective-permute-start | bytes 1179656 | tf_op jit(solution)/shard_map/ppermute | solution.py:546
  42.3 0.6 %margin.1 = f32[32,8,128]{2,1,0:T(8,128)S(1)} custom-call(f32[768,128]{1,0:T(8,128)S(1)} %bitcast.6), custom_call_target="tpu_custom_call" | custom-call | tf_op jit(solution)/shard_map/margin/pallas_call | solution.py:347
  42.9 11.0 %all_to_all.17.in_ref = f32[32,8,128]{2,1,0:T(8,128)S(1)} all-to-all(f32[32,8,128]{2,1,0:T(8,128)S(1)} %margin.1), channel_id=1, replica_groups=mesh['chip'=2,'core'=2,'gx'=4,'gy'=2] {'chip','core','gx','gy'}, dimensions={0} | all-to-all | bytes 262144 | tf_op jit(solution)/shard_map/all_to_all | solution.py:550
  53.9 0.2 collective-permute-start.2
  54.1 0.4 collective-permute-start.3
  54.5 0.7 %collective-permute-done.2.refs_1_ = f32[8,128]{1,0:T(8,128)S(1)} collective-permute-done((f32[8,128]{1,0:T(8,128)S(1)}, f32[8,128]{1,0:T(8,128)S(1)}, u32[]{:S(2)}, u32[]{:S(2)}) %collective-permute-start.2) | collective-permute-done | bytes 4128 | tf_op jit(solution)/shard_map/ppermute | solution.py:546
  55.1 0.0 collective-permute-done.1.refs_1_
  55.1 0.2 collective-permute-start.4
  55.3 1.6 %inverse.1.left_ref = bf16[48,192]{1,0:T(8,128)(2,1)S(1)} custom-call(f32[8,128]{1,0:T(8,128)S(1)} %sum.1.refs_0_, f32[8,128]{1,0:T(8,128)S(1)} %collective-permute-done.2.refs_1_), custom_call_target="tpu_custom_call" | custom-call | tf_op jit(solution)/shard_map/inverse/pallas_call | solution.py:469
  56.9 0.0 collective-permute-done.3.refs_2_
  56.9 0.0 collective-permute-done.4.refs_3_
  56.9 1.2 %rotate.1 = f32[768,128]{1,0:T(8,128)} custom-call(bf16[48,192]{1,0:T(8,128)(2,1)S(1)} %inverse.1.left_ref, f32[768,128]{1,0:T(8,128)S(1)} %bitcast.8, f32[768,128]{1,0:T(8,128)S(1)} %collective-permute-done.1.refs_1_, f32[768,128]{1,0:T(8,128)S(1)} %collective-permute-done.3.refs_2_, f32[768,128]{1,0:T(8,128)S(1)} %collective-permute-done.4.refs_3_), custom_call_target="tpu_custom_call" | custom-call | tf_op jit(solution)/shard_map/rotate/pallas_call | solution.py:505
  (4 shorter events, 0.1 us)
Async XLA Ops:
  0.0 1.0 %copy-start = (f32[6,8,128]{2,1,0:T(8,128)S(1)}, f32[6,8,128]{2,1,0:T(8,128)}, u32[]{:S(2)}) copy-start(f32[6,8,128]{2,1,0:T(8,128)} %param.5) | copy-start | bytes 73732
  22.9 1.4 %collective-permute-start = (f32[8,24,128]{2,1,0:T(8,128)S(1)}, f32[8,24,128]{2,1,0:T(8,128)S(1)}, u32[]{:S(2)}, u32[]{:S(2)}) collective-permute-start(f32[8,24,128]{2,1,0:T(8,128)S(1)} %slice.26), channel_id=1, source_target_pairs={{0,8},{8,0},{1,9},{9,1},{2,10},{10,2},{3,11},{11,3},{4,12},{12,4},... | collective-permute-start | bytes 294920 | tf_op jit(solution)/shard_map/ppermute | solution.py:534
  41.0 14.1 %collective-permute-start.1 = (f32[768,128]{1,0:T(8,128)S(1)}, f32[768,128]{1,0:T(8,128)S(1)}, u32[]{:S(2)}, u32[]{:S(2)}) collective-permute-start(f32[768,128]{1,0:T(8,128)S(1)} %bitcast.5), channel_id=1, source_target_pairs={{0,16},{16,0},{1,17},{17,1},{2,18},{18,2},{3,19},{19,3},{4,20},{20... | collective-permute-start | bytes 1179656 | tf_op jit(solution)/shard_map/ppermute | solution.py:546
  53.9 1.2 %collective-permute-start.2 = (f32[8,128]{1,0:T(8,128)S(1)}, f32[8,128]{1,0:T(8,128)S(1)}, u32[]{:S(2)}, u32[]{:S(2)}) collective-permute-start(f32[8,128]{1,0:T(8,128)S(1)} %sum.1.refs_0_), channel_id=1, source_target_pairs={{0,8},{8,0},{1,9},{9,1},{2,10},{10,2},{3,11},{11,3},{4,12},{12,4},... | collective-permute-start | bytes 12296 | tf_op jit(solution)/shard_map/ppermute | solution.py:546
  54.1 2.8 %collective-permute-start.3 = (f32[768,128]{1,0:T(8,128)S(1)}, f32[768,128]{1,0:T(8,128)S(1)}, u32[]{:S(2)}, u32[]{:S(2)}) collective-permute-start(f32[768,128]{1,0:T(8,128)S(1)} %bitcast.7), channel_id=1, source_target_pairs={{0,8},{8,0},{1,9},{9,1},{2,10},{10,2},{3,11},{11,3},{4,12},{12,4},... | collective-permute-start | bytes 1179656 | tf_op jit(solution)/shard_map/ppermute | solution.py:552
  55.1 1.8 %collective-permute-start.4 = (f32[768,128]{1,0:T(8,128)S(1)}, f32[768,128]{1,0:T(8,128)S(1)}, u32[]{:S(2)}, u32[]{:S(2)}) collective-permute-start(f32[768,128]{1,0:T(8,128)S(1)} %collective-permute-done.1.refs_1_), channel_id=1, source_target_pairs={{0,8},{8,0},{1,9},{9,1},{2,10},{10,2},{3,11},{11,3},{4,12},{12,4},... | collective-permute-start | bytes 1179656 | tf_op jit(solution)/shard_map/ppermute | solution.py:554
